TPU v7x, 32 devices: a whole 2x2x4 slice. The times are simulated.
32 devices in a mesh: seq: 4 (over y, x), head: 8 (over z, core).
Axes of the slice: x: 2, y: 2, z: 4, core: 2. Of those that a mesh axis runs over, the one named last changes fastest.
Arguments:
- layer_input: bfloat16 [16, 1024, 1024], P('seq', 'head'), may hold values from -6 to 6
- values_first: bfloat16 [16, 1024, 1024], P('seq', None, 'head'), may hold values from -6 to 6
- w_qkv: float32 [3, 1024, 1024], P(None, 'seq', 'head'), may hold values from -0.1875 to 0.1875
- w_gate_up: float32 [2, 1024, 2816], P(None, 'seq', 'head'), may hold values from -0.1875 to 0.1875
- w_out: float32 [1024, 1024], P('head', 'seq'), may hold values from -1.5 to 1.5
- w_down: float32 [2816, 1024], P('head', 'seq'), may hold values from -0.109375 to 0.109375
- norm_gains: float32 [2, 1024], replicated, may hold values from 0.5 to 1.5
- out_grad: bfloat16 [16, 1024, 1024], P('seq', 'head'), may hold values from -6 to 6
- segments: int32 [16, 1024], P('seq'), may hold values from 0 to 3, never falling along the last dimension, each value on 1 to 512 neighbouring positions
- counts: int32 [4], P('seq'), may hold values from 1 to 4, as said below
- stats_wide: float32 [7, 16, 1024, 1024], P(None, 'head', 'seq'), as said below
- roots_wide: float32 [7, 16, 1024, 1024], P(None, 'head', 'seq'), as said below
- stats_head: float32 [4, 16, 64, 64], P(None, 'head'), as said below
- roots_head: float32 [4, 16, 64, 64], P(None, 'head'), as said below
- stats_unit: float32 [3, 16, 176, 176], P(None, 'head'), as said below
- roots_unit: float32 [3, 16, 176, 176], P(None, 'head'), as said below
Outputs:
- block_out: float32 [16, 1024, 1024], P('seq', 'head')
- input_grad: float32 [16, 1024, 1024], P('seq', 'head')
- first_grad: float32 [16, 1024, 1024], P('seq', None, 'head')
- grad_qkv: float32 [3, 1024, 1024], P(None, 'seq', 'head')
- grad_gate_up: float32 [2, 1024, 2816], P(None, 'seq', 'head')
- grad_out: float32 [1024, 1024], P('head', 'seq')
- grad_down: float32 [2816, 1024], P('head', 'seq')
- grad_gains: float32 [2, 1024], replicated
- new_qkv: float32 [3, 1024, 1024], P(None, 'seq', 'head')
- new_gate_up: float32 [2, 1024, 2816], P(None, 'seq', 'head')
- new_out: float32 [1024, 1024], P('head', 'seq')
- new_down: float32 [2816, 1024], P('head', 'seq')
- new_gains: float32 [2, 1024], replicated
- new_stats_wide: float32 [6, 16, 1024, 1024], P(None, 'head', 'seq')
- new_out_right: float32 [16, 1024, 1024], P('head', 'seq')
- new_stats_head: float32 [4, 16, 64, 64], P(None, 'head')
- new_stats_unit: float32 [3, 16, 176, 176], P(None, 'head')
Inputs may be any that keep to these rules, and one draw needn't show every extreme that they name: Slots 0 to counts - 1 of a group are live; at least one group has all 4 live. `segments`: along each sequence the numbers never fall; each of 0 to 3 covers 1 to 512 positions. `stats_wide`: symmetric in its last two dimensions. `roots_wide`: symmetric in its last two dimensions. `stats_head`: symmetric in its last two dimensions. `roots_head`: symmetric in its last two dimensions. `stats_unit`: symmetric in its last two dimensions. `roots_unit`: symmetric in its last two dimensions.
All inputs are finite; a program needn't handle non-finite values.
Results may differ from a plain program's by a relative error of at most 0.018.
Values may be sent and summed in bfloat16 or wider, within the bound.
A program may use at most 192 MiB of HBM per device.

v0:
```python
import jax
import jax.numpy as jnp
from jax import lax
from jax.sharding import PartitionSpec as P

EPSILON = 1e-06
STAT_DECAY = 0.5
STEP_RATE = 0.02
OUT_RATE = 0.1
GAIN_RATE = 0.25
HIGHEST = lax.Precision.HIGHEST


def dot_nt(matrix_a, matrix_b):
    return lax.dot_general(
        matrix_a, matrix_b, (((1,), (1,)), ((), ())), preferred_element_type=jnp.float32
    )


def dot_tn(matrix_a, matrix_b):
    return lax.dot_general(
        matrix_a, matrix_b, (((0,), (0,)), ((), ())), preferred_element_type=jnp.float32
    )


def rotary_tables(segment_ids, head_dim):
    length = segment_ids.shape[0]
    position = jnp.arange(length, dtype=jnp.int32)
    opens = jnp.concatenate([jnp.ones((1,), dtype=bool), segment_ids[1:] != segment_ids[:-1]])
    first_pos = lax.cummax(jnp.where(opens, position, 0), axis=0)
    offset = (position - first_pos).astype(jnp.float32)
    half_width = head_dim // 2
    frequency = jnp.exp(-jnp.log(10000.0) * jnp.arange(half_width, dtype=jnp.float32) / half_width)
    angle = offset[:, None] * frequency[None, :]
    return (jnp.cos(angle), jnp.sin(angle))


def rotate(values, cosine, sine_part):
    half_width = values.shape[-1] // 2
    front = values[..., :half_width]
    behind = values[..., half_width:]
    cos_wide = cosine[:, None, :]
    sin_wide = sine_part[:, None, :]
    return jnp.concatenate(
        [front * cos_wide - behind * sin_wide, behind * cos_wide + front * sin_wide], axis=-1
    )


def unrotate(values, cosine, sine_part):
    half_width = values.shape[-1] // 2
    front = values[..., :half_width]
    behind = values[..., half_width:]
    cos_wide = cosine[:, None, :]
    sin_wide = sine_part[:, None, :]
    return jnp.concatenate(
        [front * cos_wide + behind * sin_wide, behind * cos_wide - front * sin_wide], axis=-1
    )


def norm_back(d_normed, normed, inverse):
    return inverse * (d_normed - normed * jnp.mean(d_normed * normed, axis=-1, keepdims=True))


def block_layout(q_rot, segment_ids):
    length, heads_here, head_dim = q_rot.shape
    block_rows = min(512, length)
    block_count = length // block_rows
    q_blocks = q_rot.reshape(block_count, block_rows, heads_here, head_dim)
    seg_blocks = segment_ids.reshape(block_count, block_rows)
    begins = jnp.arange(block_count, dtype=jnp.int32) * block_rows
    return (q_blocks, seg_blocks, begins, block_rows, block_count)


def visible_mask(segment_ids, seg_block, block_begin, block_rows):
    key_pos = jnp.arange(segment_ids.shape[0], dtype=jnp.int32)
    query_pos = block_begin + jnp.arange(block_rows, dtype=jnp.int32)
    return (key_pos[None, :] <= query_pos[:, None]) & (segment_ids[None, :] == seg_block[:, None])


def attend(q_rot, k_rot, v_mix, segment_ids):
    length, heads_here, head_dim = q_rot.shape
    q_blocks, seg_blocks, begins, block_rows, block_count = block_layout(q_rot, segment_ids)

    def one_block(operands):
        q_block, seg_block, block_begin = operands
        scores = jnp.einsum("qhd,khd->hqk", q_block, k_rot, preferred_element_type=jnp.float32)
        visible = visible_mask(segment_ids, seg_block, block_begin, block_rows)
        scores = jnp.where(visible[None], scores, -1e30)
        row_max = jnp.max(scores, axis=-1, keepdims=True)
        exp_scores = jnp.exp(scores - row_max)
        row_total = jnp.sum(exp_scores, axis=-1, keepdims=True)
        chances = (exp_scores / row_total).astype(jnp.bfloat16)
        attended = jnp.einsum(
            "hqk,khd->qhd", chances, v_mix, preferred_element_type=jnp.float32
        ).astype(jnp.bfloat16)
        return (attended, (row_max + jnp.log(row_total))[..., 0])

    attended, log_total = lax.map(one_block, (q_blocks, seg_blocks, begins))
    return (attended.reshape(length, heads_here, head_dim), log_total)


def attend_back(q_rot, k_rot, v_mix, segment_ids, log_total, d_attended):
    length, heads_here, head_dim = q_rot.shape
    q_blocks, seg_blocks, begins, block_rows, block_count = block_layout(q_rot, segment_ids)
    d_blocks = d_attended.reshape(block_count, block_rows, heads_here, head_dim)

    def one_block(running, operands):
        key_sum, value_sum = running
        q_block, seg_block, block_begin, total_block, d_block = operands
        scores = jnp.einsum("qhd,khd->hqk", q_block, k_rot, preferred_element_type=jnp.float32)
        visible = visible_mask(segment_ids, seg_block, block_begin, block_rows)
        chances = jnp.where(visible[None], jnp.exp(scores - total_block[..., None]), 0.0)
        d_chances = jnp.einsum("qhd,khd->hqk", d_block, v_mix, preferred_element_type=jnp.float32)
        inner = jnp.sum(chances * d_chances, axis=-1, keepdims=True)
        d_scores = (chances * (d_chances - inner)).astype(jnp.bfloat16)
        d_q_block = jnp.einsum("hqk,khd->qhd", d_scores, k_rot, preferred_element_type=jnp.float32)
        key_sum = key_sum + jnp.einsum(
            "hqk,qhd->khd", d_scores, q_block, preferred_element_type=jnp.float32
        )
        value_sum = value_sum + jnp.einsum(
            "hqk,qhd->khd",
            chances.astype(jnp.bfloat16),
            d_block,
            preferred_element_type=jnp.float32,
        )
        return ((key_sum, value_sum), d_q_block)

    zeros_kv = jnp.zeros((length, heads_here, head_dim), jnp.float32)
    (d_key, d_value), d_query = lax.scan(
        one_block, (zeros_kv, zeros_kv), (q_blocks, seg_blocks, begins, log_total, d_blocks)
    )
    return (d_query.reshape(length, heads_here, head_dim), d_key, d_value)


def left_update(
    weight_rows,
    grad_full,
    row_begin,
    row_part,
    big_stat,
    big_root,
    small_stat,
    small_root,
    block_width,
):
    members, model_width, columns = grad_full.shape
    blocks = columns // block_width
    grad_blocks = grad_full.reshape(members, model_width, blocks, block_width)
    grad_rows = lax.dynamic_slice_in_dim(grad_blocks, row_begin, row_part, 1)
    big_new = STAT_DECAY * big_stat + (1.0 - STAT_DECAY) * jnp.einsum(
        "nrbk,nsbk->nbrs", grad_rows, grad_blocks, precision=HIGHEST
    )
    small_new = STAT_DECAY * small_stat + (1.0 - STAT_DECAY) * jnp.einsum(
        "nrbk,nrbl->nbkl", grad_blocks, grad_blocks, precision=HIGHEST
    )
    step_dir = jnp.einsum("nbrs,nsbk->nrbk", big_root, grad_blocks, precision=HIGHEST)
    step_dir = jnp.einsum("nrbk,nbkl->nrbl", step_dir, small_root, precision=HIGHEST)
    step_dir = step_dir * lax.rsqrt(jnp.mean(step_dir * step_dir, axis=-1, keepdims=True) + EPSILON)
    new_rows = weight_rows - STEP_RATE * step_dir.reshape(members, row_part, columns)
    return (
        new_rows,
        big_new,
        small_new,
        lax.dynamic_slice_in_dim(grad_full, row_begin, row_part, 1),
    )


def right_update(
    weight_cols,
    grad_full,
    col_begin,
    col_part,
    big_stat,
    big_root,
    small_stat,
    small_root,
    block_width,
    rate,
):
    rows_all, model_width = grad_full.shape
    blocks = rows_all // block_width
    grad_blocks = grad_full.reshape(blocks, block_width, model_width)
    grad_cols = lax.dynamic_slice_in_dim(grad_blocks, col_begin, col_part, 2)
    big_new = STAT_DECAY * big_stat + (1.0 - STAT_DECAY) * jnp.einsum(
        "bkr,bks->brs", grad_cols, grad_blocks, precision=HIGHEST
    )
    small_new = STAT_DECAY * small_stat + (1.0 - STAT_DECAY) * jnp.einsum(
        "bkr,blr->bkl", grad_blocks, grad_blocks, precision=HIGHEST
    )
    step_dir = jnp.einsum("bkl,bls->bks", small_root, grad_blocks, precision=HIGHEST)
    step_dir = jnp.einsum("bks,brs->bkr", step_dir, big_root, precision=HIGHEST)
    step_dir = step_dir * lax.rsqrt(jnp.mean(step_dir * step_dir, axis=1, keepdims=True) + EPSILON)
    new_cols = weight_cols - rate * step_dir.reshape(rows_all, col_part)
    return (
        new_cols,
        big_new,
        small_new,
        lax.dynamic_slice_in_dim(grad_full, col_begin, col_part, 1),
    )


def shards(
    layer_input,
    values_first,
    w_qkv,
    w_gate_up,
    w_out,
    w_down,
    norm_gains,
    out_grad,
    segments,
    counts,
    stats_wide,
    roots_wide,
    stats_head,
    roots_head,
    stats_unit,
    roots_unit,
):
    micro_count, tok_rows, model_width = layer_input.shape
    length = segments.shape[1]
    row_part = w_qkv.shape[1]
    head_cols = w_qkv.shape[2]
    ffn_cols = w_gate_up.shape[2]
    head_dim = stats_head.shape[2]
    unit_block = stats_unit.shape[2]
    heads_here = head_cols // head_dim
    row_begin = lax.axis_index("seq") * row_part

    def fetch_weights():
        gathered = (
            lax.all_gather(w_qkv.astype(jnp.bfloat16), "seq", axis=1, tiled=True),
            lax.all_gather(w_gate_up.astype(jnp.bfloat16), "seq", axis=1, tiled=True),
            lax.all_gather(w_out.astype(jnp.bfloat16), "seq", axis=1, tiled=True),
            lax.all_gather(w_down.astype(jnp.bfloat16), "seq", axis=1, tiled=True),
        )
        gathered = tuple(gathered)
        whole = (gathered[2], gathered[0], gathered[1], gathered[3])
        return gathered + whole

    def micro_step(weights_now, x_micro, first_micro, grad_micro, segment_ids, is_live):
        (
            qkv_all,
            gate_up_all,
            out_cols,
            down_all,
            out_whole,
            qkv_whole,
            gate_up_whole,
            down_whole,
        ) = weights_now
        x_float = x_micro.astype(jnp.float32)
        inverse_one = lax.rsqrt(jnp.mean(x_float * x_float, axis=-1, keepdims=True) + EPSILON)
        normed_one = x_float * inverse_one
        normed_all = lax.all_gather(
            (normed_one * norm_gains[0]).astype(jnp.bfloat16), "head", axis=0, tiled=True
        )
        project = jnp.einsum("ld,idc->ilc", normed_all, qkv_all, preferred_element_type=jnp.float32)
        cosine, sine_part = rotary_tables(segment_ids, head_dim)
        split_heads = project.reshape(3, length, heads_here, head_dim)
        q_rot = (rotate(split_heads[0], cosine, sine_part) * 0.125).astype(jnp.bfloat16)
        k_rot = rotate(split_heads[1], cosine, sine_part).astype(jnp.bfloat16)
        first_float = first_micro.astype(jnp.float32).reshape(length, heads_here, head_dim)
        v_mix = (0.5 * split_heads[2] + 0.5 * first_float).astype(jnp.bfloat16)
        attended, log_total = attend(q_rot, k_rot, v_mix, segment_ids)
        attended_flat = attended.reshape(length, head_cols)
        attn_out = lax.psum_scatter(
            jnp.dot(attended_flat, out_cols, preferred_element_type=jnp.float32),
            "head",
            scatter_dimension=0,
            tiled=True,
        )
        middle = x_float + attn_out
        inverse_two = lax.rsqrt(jnp.mean(middle * middle, axis=-1, keepdims=True) + EPSILON)
        normed_two = middle * inverse_two
        normed_two_all = lax.all_gather(
            (normed_two * norm_gains[1]).astype(jnp.bfloat16), "head", axis=0, tiled=True
        )
        gate_up = jnp.einsum(
            "ld,idf->ilf", normed_two_all, gate_up_all, preferred_element_type=jnp.float32
        )
        sigmoid_gate = jax.nn.sigmoid(gate_up[0])
        activated = gate_up[0] * sigmoid_gate
        hidden = (activated * gate_up[1]).astype(jnp.bfloat16)
        ffn_out = lax.psum_scatter(
            jnp.dot(hidden, down_all, preferred_element_type=jnp.float32).astype(jnp.bfloat16),
            "head",
            scatter_dimension=0,
            tiled=True,
        ).astype(jnp.float32)
        block_out = jnp.where(is_live, middle + ffn_out, x_float)
        grad_float = grad_micro.astype(jnp.float32)
        d_out = jnp.where(is_live, grad_float, 0.0)
        d_ffn = lax.all_gather(d_out.astype(jnp.bfloat16), "head", axis=0, tiled=True)
        g_down = dot_tn(hidden, d_ffn)
        d_hidden = dot_nt(d_ffn, down_all)
        d_gate = (
            d_hidden * gate_up[1] * sigmoid_gate * (1.0 + gate_up[0] * (1.0 - sigmoid_gate))
        ).astype(jnp.bfloat16)
        d_up = (d_hidden * activated).astype(jnp.bfloat16)
        d_gate_up = jnp.stack([d_gate, d_up])
        g_gate_up = jnp.einsum(
            "ld,ilf->idf", normed_two_all, d_gate_up, preferred_element_type=jnp.float32
        )
        d_normed_two = lax.psum_scatter(
            jnp.einsum("ilf,idf->ld", d_gate_up, gate_up_all, preferred_element_type=jnp.float32),
            "head",
            scatter_dimension=0,
            tiled=True,
        )
        gain_two = jnp.sum(normed_two * d_normed_two, axis=0)
        d_middle = d_out + norm_back(d_normed_two * norm_gains[1], normed_two, inverse_two)
        d_attn = lax.all_gather(d_middle.astype(jnp.bfloat16), "head", axis=0, tiled=True)
        g_out = dot_tn(attended_flat, d_attn)
        d_attended = (
            dot_nt(d_attn, out_cols).astype(jnp.bfloat16).reshape(length, heads_here, head_dim)
        )
        d_q_rot, d_k_rot, d_v_mix = attend_back(
            q_rot, k_rot, v_mix, segment_ids, log_total, d_attended
        )
        d_query = unrotate(d_q_rot * 0.125, cosine, sine_part).astype(jnp.bfloat16)
        d_key = unrotate(d_k_rot, cosine, sine_part).astype(jnp.bfloat16)
        d_value = (0.5 * d_v_mix).astype(jnp.bfloat16)
        d_first = (0.5 * d_v_mix).reshape(length, head_cols)
        d_project = jnp.stack([d_query, d_key, d_value]).reshape(3, length, head_cols)
        g_qkv = jnp.einsum("ld,ilc->idc", normed_all, d_project, preferred_element_type=jnp.float32)
        d_normed_one = lax.psum_scatter(
            jnp.einsum(
                "ilc,idc->ld", d_project, qkv_all, preferred_element_type=jnp.float32
            ).astype(jnp.bfloat16),
            "head",
            scatter_dimension=0,
            tiled=True,
        ).astype(jnp.float32)
        gain_one = jnp.sum(normed_one * d_normed_one, axis=0)
        d_input = d_middle + norm_back(d_normed_one * norm_gains[0], normed_one, inverse_one)
        d_input = jnp.where(is_live, d_input, grad_float)
        return (
            block_out,
            d_input,
            d_first,
            (g_qkv, g_gate_up, g_out, g_down, jnp.stack([gain_one, gain_two])),
        )

    def one_turn(summed, item):
        x_micro, first_micro, grad_micro, segment_ids, slot_index = item
        weights_now = fetch_weights()
        is_live = slot_index < counts[0]
        results = micro_step(weights_now, x_micro, first_micro, grad_micro, segment_ids, is_live)
        summed = tuple((running + addend for running, addend in zip(summed, results[3])))
        return (summed, (results[0], results[1], results[2]))

    start_sums = (
        jnp.zeros((3, model_width, head_cols), jnp.float32),
        jnp.zeros((2, model_width, ffn_cols), jnp.float32),
        jnp.zeros((head_cols, model_width), jnp.float32),
        jnp.zeros((ffn_cols, model_width), jnp.float32),
        jnp.zeros((2, model_width), jnp.float32),
    )
    summed, (block_out, input_grad, first_grad) = lax.scan(
        one_turn,
        start_sums,
        (layer_input, values_first, out_grad, segments, jnp.arange(micro_count, dtype=jnp.int32)),
    )
    grad_qkv, grad_gate_up, grad_out, grad_down = (
        lax.psum(summed[0].astype(jnp.bfloat16), "seq").astype(jnp.float32),
        lax.psum(summed[1].astype(jnp.bfloat16), "seq").astype(jnp.float32),
        lax.psum(summed[2].astype(jnp.bfloat16), "seq").astype(jnp.float32),
        lax.psum(summed[3].astype(jnp.bfloat16), "seq").astype(jnp.float32),
    )
    grad_gains = lax.psum(summed[4], ("seq", "head"))
    new_qkv, wide_qkv, head_qkv, shard_qkv = left_update(
        w_qkv,
        grad_qkv,
        row_begin,
        row_part,
        stats_wide[0:3],
        roots_wide[0:3],
        stats_head[0:3],
        roots_head[0:3],
        head_dim,
    )
    new_gate_up, wide_gu, unit_gu, shard_gu = left_update(
        w_gate_up,
        grad_gate_up,
        row_begin,
        row_part,
        stats_wide[3:5],
        roots_wide[3:5],
        stats_unit[0:2],
        roots_unit[0:2],
        unit_block,
    )
    new_out, wide_out, head_out, shard_out = right_update(
        w_out,
        grad_out,
        row_begin,
        row_part,
        stats_wide[5],
        roots_wide[5],
        stats_head[3],
        roots_head[3],
        head_dim,
        OUT_RATE,
    )
    new_down, wide_down, unit_down, shard_down = right_update(
        w_down,
        grad_down,
        row_begin,
        row_part,
        stats_wide[6],
        roots_wide[6],
        stats_unit[2],
        roots_unit[2],
        unit_block,
        STEP_RATE,
    )
    new_gains = norm_gains - GAIN_RATE * grad_gains * lax.rsqrt(
        jnp.mean(grad_gains * grad_gains, axis=-1, keepdims=True) + EPSILON
    )
    new_stats_wide = jnp.concatenate([wide_qkv, wide_gu, wide_down[None]], axis=0)
    new_stats_head = jnp.concatenate([head_qkv, head_out[None]], axis=0)
    new_stats_unit = jnp.concatenate([unit_gu, unit_down[None]], axis=0)
    return (
        block_out,
        input_grad,
        first_grad,
        shard_qkv,
        shard_gu,
        shard_out,
        shard_down,
        grad_gains,
        new_qkv,
        new_gate_up,
        new_out,
        new_down,
        new_gains,
        new_stats_wide,
        wide_out,
        new_stats_head,
        new_stats_unit,
    )


def solution(mesh):
    return jax.shard_map(
        shards,
        mesh=mesh,
        in_specs=(
            P("seq", "head", None),
            P("seq", None, "head"),
            P(None, "seq", "head"),
            P(None, "seq", "head"),
            P("head", "seq"),
            P("head", "seq"),
            P(),
            P("seq", "head", None),
            P("seq", None),
            P("seq"),
            P(None, "head", "seq", None),
            P(None, "head", "seq", None),
            P(None, "head", None, None),
            P(None, "head", None, None),
            P(None, "head", None, None),
            P(None, "head", None, None),
        ),
        out_specs=(
            P("seq", "head", None),
            P("seq", "head", None),
            P("seq", None, "head"),
            P(None, "seq", "head"),
            P(None, "seq", "head"),
            P("head", "seq"),
            P("head", "seq"),
            P(),
            P(None, "seq", "head"),
            P(None, "seq", "head"),
            P("head", "seq"),
            P("head", "seq"),
            P(),
            P(None, "head", "seq", None),
            P("head", "seq", None),
            P(None, "head", None, None),
            P(None, "head", None, None),
        ),
        check_vma=False,
    )
```

profile of v0, /device:TPU:0, one launch (start us, length us, event | category | flops | bytes accessed | tf_op | source)
XLA Modules:
  0.0 1684.5 jit_solution(12292496643817199228)
XLA Ops:
  14.4 1501.6 %while.85 = (s32[]{:T(128)}, f32[3,1024,128]{1,2,0:T(8,128)}, f32[2,1024,352]{1,2,0:T(8,128)}, f32[128,1024]{1,0:T(8,128)}, f32[352,1024]{1,0:T(8,128)}, /*index...) while((s32[]{:T(128)}, f32[3,1024,128]{1,2,0:T(8,128)}, ...), condition=%wide.region_20.21_spmd.clone, body=%wide.region_0.20_spmd.clone.sunk | while | flops 10857032704 | bytes 313348704 | solution.py:360
  71.5 49.3 %reduce-scatter.5.cloned.1.call-done = f32[128,1024]{1,0:T(8,128)} async-done(((f32[1024,1024]{1,0:T(8,128)}), f32[128,1024]{1,0:T(8,128)}) %reduce-scatter.5.cloned.1.call-update) | async-done | bytes 524304 | tf_op jit(solution)/shard_map/while/body/eval_jaxpr/reduce_scatter | solution.py:267
  190.3 49.3 %reduce-scatter.7.cloned.1.call-done = f32[128,1024]{1,0:T(8,128)} async-done(((f32[1024,1024]{1,0:T(8,128)}), f32[128,1024]{1,0:T(8,128)}) %reduce-scatter.7.cloned.1.call-update) | async-done | bytes 524304 | tf_op jit(solution)/shard_map/while/body/eval_jaxpr/reduce_scatter | solution.py:305
  243.6 27.3 %all-gather.14.cloned.1.call-done = bf16[1024,1024]{1,0:T(8,128)(2,1)} async-done(((bf16[128,1024]{1,0:T(8,128)(2,1)}), bf16[1024,1024]{1,0:T(8,128)(2,1)}) %all-gather.14.cloned.1.call-update) | async-done | bytes 2097168 | tf_op jit(solution)/shard_map/while/body/eval_jaxpr/all_gather | solution.py:313
  275.6 30.9 %while.87 = (s32[]{:T(128)}, f32[1024,2,64]{0,2,1:T(8,128)S(1)}, f32[1024,2,64]{0,2,1:T(8,128)S(1)}, f32[2,512,2,64]{1,0,3,2:T(2,128)}, bf16[2,512,2,64]{1,3,2,0...) while((s32[]{:T(128)}, f32[1024,2,64]{0,2,1:T(8,128)S(1)}, ...), condition=%wide.region_14.14_spmd.clone, body=%wide.region_12.13_spmd.clone.sunk | while | flops 685768192 | bytes 38316224 | solution.py:129
  349.5 35.8 %reduce-scatter.11.cloned.1.call-done = bf16[128,1024]{1,0:T(8,128)(2,1)} async-done(((bf16[1024,1024]{1,0:T(8,128)(2,1)}), bf16[128,1024]{1,0:T(8,128)(2,1)}) %reduce-scatter.11.cloned.1.call-update) | async-done | bytes 262160 | tf_op jit(solution)/shard_map/while/body/eval_jaxpr/reduce_scatter | solution.py:285
  442.2 51.2 %reduce-scatter.5.cloned.1.call-done = f32[128,1024]{1,0:T(8,128)} async-done(((f32[1024,1024]{1,0:T(8,128)}), f32[128,1024]{1,0:T(8,128)}) %reduce-scatter.5.cloned.1.call-update) | async-done | bytes 524304 | tf_op jit(solution)/shard_map/while/body/eval_jaxpr/reduce_scatter | solution.py:267
  562.9 49.3 %reduce-scatter.7.cloned.1.call-done = f32[128,1024]{1,0:T(8,128)} async-done(((f32[1024,1024]{1,0:T(8,128)}), f32[128,1024]{1,0:T(8,128)}) %reduce-scatter.7.cloned.1.call-update) | async-done | bytes 524304 | tf_op jit(solution)/shard_map/while/body/eval_jaxpr/reduce_scatter | solution.py:305
  616.2 27.4 %all-gather.14.cloned.1.call-done = bf16[1024,1024]{1,0:T(8,128)(2,1)} async-done(((bf16[128,1024]{1,0:T(8,128)(2,1)}), bf16[1024,1024]{1,0:T(8,128)(2,1)}) %all-gather.14.cloned.1.call-update) | async-done | bytes 2097168 | tf_op jit(solution)/shard_map/while/body/eval_jaxpr/all_gather | solution.py:313
  648.2 30.9 %while.87 = (s32[]{:T(128)}, f32[1024,2,64]{0,2,1:T(8,128)S(1)}, f32[1024,2,64]{0,2,1:T(8,128)S(1)}, f32[2,512,2,64]{1,0,3,2:T(2,128)}, bf16[2,512,2,64]{1,3,2,0...) while((s32[]{:T(128)}, f32[1024,2,64]{0,2,1:T(8,128)S(1)}, ...), condition=%wide.region_14.14_spmd.clone, body=%wide.region_12.13_spmd.clone.sunk | while | flops 685768192 | bytes 38316224 | solution.py:129
  722.1 36.0 %reduce-scatter.11.cloned.1.call-done = bf16[128,1024]{1,0:T(8,128)(2,1)} async-done(((bf16[1024,1024]{1,0:T(8,128)(2,1)}), bf16[128,1024]{1,0:T(8,128)(2,1)}) %reduce-scatter.11.cloned.1.call-update) | async-done | bytes 262160 | tf_op jit(solution)/shard_map/while/body/eval_jaxpr/reduce_scatter | solution.py:285
  814.6 51.4 %reduce-scatter.5.cloned.1.call-done = f32[128,1024]{1,0:T(8,128)} async-done(((f32[1024,1024]{1,0:T(8,128)}), f32[128,1024]{1,0:T(8,128)}) %reduce-scatter.5.cloned.1.call-update) | async-done | bytes 524304 | tf_op jit(solution)/shard_map/while/body/eval_jaxpr/reduce_scatter | solution.py:267
  935.6 49.3 %reduce-scatter.7.cloned.1.call-done = f32[128,1024]{1,0:T(8,128)} async-done(((f32[1024,1024]{1,0:T(8,128)}), f32[128,1024]{1,0:T(8,128)}) %reduce-scatter.7.cloned.1.call-update) | async-done | bytes 524304 | tf_op jit(solution)/shard_map/while/body/eval_jaxpr/reduce_scatter | solution.py:305
  988.8 27.4 %all-gather.14.cloned.1.call-done = bf16[1024,1024]{1,0:T(8,128)(2,1)} async-done(((bf16[128,1024]{1,0:T(8,128)(2,1)}), bf16[1024,1024]{1,0:T(8,128)(2,1)}) %all-gather.14.cloned.1.call-update) | async-done | bytes 2097168 | tf_op jit(solution)/shard_map/while/body/eval_jaxpr/all_gather | solution.py:313
  1020.8 30.9 %while.87 = (s32[]{:T(128)}, f32[1024,2,64]{0,2,1:T(8,128)S(1)}, f32[1024,2,64]{0,2,1:T(8,128)S(1)}, f32[2,512,2,64]{1,0,3,2:T(2,128)}, bf16[2,512,2,64]{1,3,2,0...) while((s32[]{:T(128)}, f32[1024,2,64]{0,2,1:T(8,128)S(1)}, ...), condition=%wide.region_14.14_spmd.clone, body=%wide.region_12.13_spmd.clone.sunk | while | flops 685768192 | bytes 38316224 | solution.py:129
  1094.8 36.0 %reduce-scatter.11.cloned.1.call-done = bf16[128,1024]{1,0:T(8,128)(2,1)} async-done(((bf16[1024,1024]{1,0:T(8,128)(2,1)}), bf16[128,1024]{1,0:T(8,128)(2,1)}) %reduce-scatter.11.cloned.1.call-update) | async-done | bytes 262160 | tf_op jit(solution)/shard_map/while/body/eval_jaxpr/reduce_scatter | solution.py:285
  1187.4 51.5 %reduce-scatter.5.cloned.1.call-done = f32[128,1024]{1,0:T(8,128)} async-done(((f32[1024,1024]{1,0:T(8,128)}), f32[128,1024]{1,0:T(8,128)}) %reduce-scatter.5.cloned.1.call-update) | async-done | bytes 524304 | tf_op jit(solution)/shard_map/while/body/eval_jaxpr/reduce_scatter | solution.py:267
  1273.6 25.4 %all-gather.12.cloned.1.call-done = bf16[1024,1024]{1,0:T(8,128)(2,1)} async-done(((bf16[128,1024]{1,0:T(8,128)(2,1)}), bf16[1024,1024]{1,0:T(8,128)(2,1)}) %all-gather.12.cloned.1.call-update) | async-done | bytes 2097168 | tf_op jit(solution)/shard_map/while/body/eval_jaxpr/all_gather | solution.py:294
  1308.7 49.3 %reduce-scatter.7.cloned.1.call-done = f32[128,1024]{1,0:T(8,128)} async-done(((f32[1024,1024]{1,0:T(8,128)}), f32[128,1024]{1,0:T(8,128)}) %reduce-scatter.7.cloned.1.call-update) | async-done | bytes 524304 | tf_op jit(solution)/shard_map/while/body/eval_jaxpr/reduce_scatter | solution.py:305
  1362.0 27.4 %all-gather.14.cloned.1.call-done = bf16[1024,1024]{1,0:T(8,128)(2,1)} async-done(((bf16[128,1024]{1,0:T(8,128)(2,1)}), bf16[1024,1024]{1,0:T(8,128)(2,1)}) %all-gather.14.cloned.1.call-update) | async-done | bytes 2097168 | tf_op jit(solution)/shard_map/while/body/eval_jaxpr/all_gather | solution.py:313
  1393.9 30.9 %while.87 = (s32[]{:T(128)}, f32[1024,2,64]{0,2,1:T(8,128)S(1)}, f32[1024,2,64]{0,2,1:T(8,128)S(1)}, f32[2,512,2,64]{1,0,3,2:T(2,128)}, bf16[2,512,2,64]{1,3,2,0...) while((s32[]{:T(128)}, f32[1024,2,64]{0,2,1:T(8,128)S(1)}, ...), condition=%wide.region_14.14_spmd.clone, body=%wide.region_12.13_spmd.clone.sunk | while | flops 685768192 | bytes 38316224 | solution.py:129
  1467.8 36.0 %reduce-scatter.11.cloned.1.call-done = bf16[128,1024]{1,0:T(8,128)(2,1)} async-done(((bf16[1024,1024]{1,0:T(8,128)(2,1)}), bf16[128,1024]{1,0:T(8,128)(2,1)}) %reduce-scatter.11.cloned.1.call-update) | async-done | bytes 262160 | tf_op jit(solution)/shard_map/while/body/eval_jaxpr/reduce_scatter | solution.py:285
  1526.5 38.1 %psum.39 = f32[2,1024]{1,0:T(2,128)S(1)} all-reduce(f32[2,1024]{1,0:T(2,128)S(1)} %copy-done.38), channel_id=1, replica_groups=mesh['seq'=4,'head'=8] {'seq','head'}, use_global_device_ids=true, to_apply=%region_25.26 | all-reduce | flops 2048 | bytes 16384 | tf_op jit(solution)/shard_map/psum | solution.py:371
  1566.1 47.9 %all-reduce.3.cloned.1.call-done = (bf16[3,1024,128]{2,1,0:T(8,128)(2,1)}, bf16[2,1024,352]{1,2,0:T(8,128)(2,1)}, bf16[128,1024]{1,0:T(8,128)(2,1)}, bf16[352,1024]{1,0:T(8,128)(2,1)}) async-done(((bf16[3,1024,128]{2,1,0:T(8,128)(2,1)}, bf16[2,1024,352]{1,2,0:T(8,128)(2,1)}, bf16[128,1024]{1,0:T(8,128)(2,1)}, bf16[352,1024]{1,0:T(8,128)(2,1)}), (bf16[3,1024,128]{2,1,0:T(8,128)(2,1)}, ...) | async-done | bytes 3211280 | tf_op jit(solution)/shard_map/psum | solution.py:366
  (997 shorter events, 932.7 us)
Async XLA Ops:
  16.2 104.6 %reduce-scatter.5.cloned.1.call-start = ((), (), s32[]{:S(2)}) async-start(), calls=%async_computation.7 | async-start | bytes 4718592 | tf_op jit(solution)/shard_map/while/body/eval_jaxpr/reduce_scatter | solution.py:267
  71.4 78.7 %all-gather.10.cloned.1.call-start = ((), (), s32[]{:S(2)}) async-start(), calls=%async_computation.8 | async-start | bytes 2359296 | tf_op jit(solution)/shard_map/while/body/eval_jaxpr/all_gather | solution.py:276
  126.5 113.1 %reduce-scatter.7.cloned.1.call-start = ((), (), s32[]{:S(2)}) async-start(), calls=%async_computation.10 | async-start | bytes 4718592 | tf_op jit(solution)/shard_map/while/body/eval_jaxpr/reduce_scatter | solution.py:305
  190.3 80.7 %all-gather.14.cloned.1.call-start = ((), (), s32[]{:S(2)}) async-start(), calls=%async_computation.11 | async-start | bytes 2359296 | tf_op jit(solution)/shard_map/while/body/eval_jaxpr/all_gather | solution.py:313
  243.5 104.7 %reduce-scatter.9.cloned.1.call-start = ((), (), s32[]{:S(2)}) async-start(), calls=%async_computation.12 | async-start | bytes 2359296 | tf_op jit(solution)/shard_map/while/body/eval_jaxpr/reduce_scatter | solution.py:327
  389.7 103.7 %reduce-scatter.5.cloned.1.call-start = ((), (), s32[]{:S(2)}) async-start(), calls=%async_computation.7 | async-start | bytes 4718592 | tf_op jit(solution)/shard_map/while/body/eval_jaxpr/reduce_scatter | solution.py:267
  442.1 80.6 %all-gather.10.cloned.1.call-start = ((), (), s32[]{:S(2)}) async-start(), calls=%async_computation.8 | async-start | bytes 2359296 | tf_op jit(solution)/shard_map/while/body/eval_jaxpr/all_gather | solution.py:276
  499.2 113.0 %reduce-scatter.7.cloned.1.call-start = ((), (), s32[]{:S(2)}) async-start(), calls=%async_computation.10 | async-start | bytes 4718592 | tf_op jit(solution)/shard_map/while/body/eval_jaxpr/reduce_scatter | solution.py:305
  562.9 80.7 %all-gather.14.cloned.1.call-start = ((), (), s32[]{:S(2)}) async-start(), calls=%async_computation.11 | async-start | bytes 2359296 | tf_op jit(solution)/shard_map/while/body/eval_jaxpr/all_gather | solution.py:313
  616.1 104.7 %reduce-scatter.9.cloned.1.call-start = ((), (), s32[]{:S(2)}) async-start(), calls=%async_computation.12 | async-start | bytes 2359296 | tf_op jit(solution)/shard_map/while/body/eval_jaxpr/reduce_scatter | solution.py:327
  685.4 72.7 %reduce-scatter.11.cloned.1.call-start = ((), (), s32[]{:S(2)}) async-start(), calls=%async_computation.13 | async-start | bytes 2359296 | tf_op jit(solution)/shard_map/while/body/eval_jaxpr/reduce_scatter | solution.py:285
  762.5 103.6 %reduce-scatter.5.cloned.1.call-start = ((), (), s32[]{:S(2)}) async-start(), calls=%async_computation.7 | async-start | bytes 4718592 | tf_op jit(solution)/shard_map/while/body/eval_jaxpr/reduce_scatter | solution.py:267
  814.6 80.8 %all-gather.10.cloned.1.call-start = ((), (), s32[]{:S(2)}) async-start(), calls=%async_computation.8 | async-start | bytes 2359296 | tf_op jit(solution)/shard_map/while/body/eval_jaxpr/all_gather | solution.py:276
  871.8 113.0 %reduce-scatter.7.cloned.1.call-start = ((), (), s32[]{:S(2)}) async-start(), calls=%async_computation.10 | async-start | bytes 4718592 | tf_op jit(solution)/shard_map/while/body/eval_jaxpr/reduce_scatter | solution.py:305
  935.5 80.7 %all-gather.14.cloned.1.call-start = ((), (), s32[]{:S(2)}) async-start(), calls=%async_computation.11 | async-start | bytes 2359296 | tf_op jit(solution)/shard_map/while/body/eval_jaxpr/all_gather | solution.py:313
  988.7 104.7 %reduce-scatter.9.cloned.1.call-start = ((), (), s32[]{:S(2)}) async-start(), calls=%async_computation.12 | async-start | bytes 2359296 | tf_op jit(solution)/shard_map/while/body/eval_jaxpr/reduce_scatter | solution.py:327
  1058.0 72.7 %reduce-scatter.11.cloned.1.call-start = ((), (), s32[]{:S(2)}) async-start(), calls=%async_computation.13 | async-start | bytes 2359296 | tf_op jit(solution)/shard_map/while/body/eval_jaxpr/reduce_scatter | solution.py:285
  1135.1 103.8 %reduce-scatter.5.cloned.1.call-start = ((), (), s32[]{:S(2)}) async-start(), calls=%async_computation.7 | async-start | bytes 4718592 | tf_op jit(solution)/shard_map/while/body/eval_jaxpr/reduce_scatter | solution.py:267
  1187.4 81.0 %all-gather.10.cloned.1.call-start = ((), (), s32[]{:S(2)}) async-start(), calls=%async_computation.8 | async-start | bytes 2359296 | tf_op jit(solution)/shard_map/while/body/eval_jaxpr/all_gather | solution.py:276
  1244.7 113.2 %reduce-scatter.7.cloned.1.call-start = ((), (), s32[]{:S(2)}) async-start(), calls=%async_computation.10 | async-start | bytes 4718592 | tf_op jit(solution)/shard_map/while/body/eval_jaxpr/reduce_scatter | solution.py:305
  1308.6 80.7 %all-gather.14.cloned.1.call-start = ((), (), s32[]{:S(2)}) async-start(), calls=%async_computation.11 | async-start | bytes 2359296 | tf_op jit(solution)/shard_map/while/body/eval_jaxpr/all_gather | solution.py:313
  1361.9 104.7 %reduce-scatter.9.cloned.1.call-start = ((), (), s32[]{:S(2)}) async-start(), calls=%async_computation.12 | async-start | bytes 2359296 | tf_op jit(solution)/shard_map/while/body/eval_jaxpr/reduce_scatter | solution.py:327
  1431.1 72.7 %reduce-scatter.11.cloned.1.call-start = ((), (), s32[]{:S(2)}) async-start(), calls=%async_computation.13 | async-start | bytes 2359296 | tf_op jit(solution)/shard_map/while/body/eval_jaxpr/reduce_scatter | solution.py:285
  1515.9 98.1 %all-reduce.3.cloned.1.call-start = ((), (), s32[]{:S(2)}) async-start(), calls=%async_computation.4 | async-start | bytes 6422528 | tf_op jit(solution)/shard_map/psum | solution.py:366
  (212 other events, 4061.1 us)
Sparse Core Ops, SparseCore 0:
  17.4 31.8 all-gather.5
  70.9 49.8 reduce-scatter.4
  243.6 27.2 all-gather.13
  312.9 35.2 reduce-scatter.8
  351.0 34.3 reduce-scatter.10
  390.6 27.6 all-gather.5
  441.5 51.9 reduce-scatter.4
  616.2 27.2 all-gather.13
  685.5 35.2 reduce-scatter.8
  723.5 34.5 reduce-scatter.10
  763.6 27.4 all-gather.5
  814.1 51.9 reduce-scatter.4
  988.9 27.2 all-gather.13
  1058.1 35.2 reduce-scatter.8
  1096.2 34.5 reduce-scatter.10
  1136.0 27.7 all-gather.5
  1186.9 52.0 reduce-scatter.4
  1362.0 27.2 all-gather.13
  1431.2 35.2 reduce-scatter.8
  1469.2 34.5 reduce-scatter.10
Sparse Core Ops, SparseCore 1:
  73.7 29.3 all-gather.7
  122.9 27.1 all-gather.9
  152.2 28.4 all-gather.11
  190.3 49.2 reduce-scatter.6
  444.6 31.4 all-gather.7
  495.6 27.1 all-gather.9
  524.8 28.4 all-gather.11
  563.0 49.2 reduce-scatter.6
  816.9 31.4 all-gather.7
  868.2 27.1 all-gather.9
  897.4 28.4 all-gather.11
  935.6 49.2 reduce-scatter.6
  1189.7 31.6 all-gather.7
  1241.1 27.2 all-gather.9
  1270.5 28.4 all-gather.11
  1308.7 49.2 reduce-scatter.6
  1525.9 88.0 all-reduce.2
where the time goes:
time: 1690 us; the launch traced here: 1680 us
  waiting for transfers between devices  892 us (53%)
  matrix products  259 us (15%)
  blocking collectives  192 us (11%)
  local copies, waits for them, and re-layouts  153 us (9%)
  other arithmetic  152 us (9%)
  loops' own time  18.3 us (1%)
    reduce_scatter x4, waiting for transfers between devices, micro_step(): lax.psum_scatter(jnp.dot(attended_flat, out_cols, preferred_element_type=...  204 us
    reduce_scatter x4, waiting for transfers between devices, micro_step(): lax.psum_scatter(jnp.einsum('ilf,idf->ld', d_gate_up, gate_up_all, prefer...  197 us
    reduce_scatter x4, waiting for transfers between devices, micro_step(): lax.psum_scatter(jnp.dot(hidden, down_all, preferred_element_type=jnp.flo...  144 us
    all_gather x4, waiting for transfers between devices, micro_step(): lax.all_gather(d_middle.astype(jnp.bfloat16), 'head', axis=0, tiled=True)  109 us
    all_gather x4, waiting for transfers between devices, micro_step(): lax.all_gather(d_out.astype(jnp.bfloat16), 'head', axis=0, tiled=True)  101 us
    all_gather x4, blocking collectives, fetch_weights(): lax.all_gather(w_qkv.astype(jnp.bfloat16), 'seq', axis=1, tiled=True)  57.4 us
    all_gather x4, blocking collectives, fetch_weights(): lax.all_gather(w_down.astype(jnp.bfloat16), 'seq', axis=1, tiled=True)  54.7 us
    dynamic_update_slice x16, local copies, waits for them, and re-layouts, attend_back(): lax.scan(one_block, (zeros_kv, zeros_kv), (q_blocks, seg_blocks, begins,...  48.3 us
  transfers between devices with their start and end apart: 37, of which 30 were waited for; matrix products, arithmetic and copies ran while one was open for 9% of the time, Pallas kernels for 0%

commit v1 on v0

v1 whole, which is shorter than its diff:
```python
import functools

import jax
import jax.numpy as jnp
from jax import lax
from jax.experimental import pallas as pl
from jax.experimental.pallas import tpu as pltpu
from jax.sharding import PartitionSpec as P

EPSILON = 1e-06
STAT_DECAY = 0.5
STEP_RATE = 0.02
OUT_RATE = 0.1
GAIN_RATE = 0.25
AXES = ("seq", "head")
LANES = 128
BLOCK = 256
BF16 = jnp.bfloat16
F32 = jnp.float32


def dot_nt(matrix_a, matrix_b):
    return lax.dot_general(
        matrix_a, matrix_b, (((1,), (1,)), ((), ())), preferred_element_type=F32
    )


def dot_tn(matrix_a, matrix_b):
    return lax.dot_general(
        matrix_a, matrix_b, (((0,), (0,)), ((), ())), preferred_element_type=F32
    )


def dot_nn(matrix_a, matrix_b):
    return jnp.dot(matrix_a, matrix_b, preferred_element_type=F32)


def norm_back(d_normed, normed, inverse):
    return inverse * (d_normed - normed * jnp.mean(d_normed * normed, axis=-1, keepdims=True))


def position_tables(segment_ids, head_dim):
    length = segment_ids.shape[0]
    position = jnp.arange(length, dtype=jnp.int32)
    opens = jnp.concatenate([jnp.ones((1,), dtype=bool), segment_ids[1:] != segment_ids[:-1]])
    first_pos = lax.cummax(jnp.where(opens, position, 0), axis=0)
    offset = (position - first_pos).astype(F32)
    half_width = head_dim // 2
    frequency = jnp.exp(-jnp.log(10000.0) * jnp.arange(half_width, dtype=F32) / half_width)
    angle = offset[:, None] * frequency[None, :]
    cosine, sine_part = jnp.cos(angle), jnp.sin(angle)
    per_lane = LANES // head_dim
    cos_wide = jnp.concatenate([cosine, cosine] * per_lane, axis=1)
    sin_wide = jnp.concatenate([-sine_part, sine_part] * per_lane, axis=1)
    return first_pos, cos_wide, sin_wide


def swap_halves(values):
    lane = lax.broadcasted_iota(jnp.int32, values.shape, 1)
    return jnp.where((lane & 32) == 0, pltpu.roll(values, 96, 1), pltpu.roll(values, 32, 1))


def two_heads(block):
    lane = lax.broadcasted_iota(jnp.int32, block.shape, 1)
    zero = jnp.zeros_like(block)
    return jnp.concatenate(
        [jnp.where(lane < 64, block, zero), jnp.where(lane >= 64, block, zero)], axis=0
    )


def one_pair(transposed, width):
    kept = jnp.concatenate([transposed[:64, :width], transposed[64:, width:]], axis=0)
    return kept.T


def seen(first_ref, begin, key_count):
    first = first_ref[0:1, begin : begin + BLOCK]
    query = begin + lax.broadcasted_iota(jnp.int32, (1, BLOCK), 1)
    first = jnp.concatenate([first, first], axis=1)
    query = jnp.concatenate([query, query], axis=1)
    key = lax.broadcasted_iota(jnp.int32, (key_count, 2 * BLOCK), 0)
    return (key >= first) & (key <= query)


def attend_kernel(
    q_ref, k_ref, v_ref, vf_ref, cos_ref, sin_ref, first_ref, qr_ref, kr_ref, vm_ref, att_ref, lse_ref
):
    length = q_ref.shape[1]
    cosine, sine_part = cos_ref[...], sin_ref[...]
    q_raw, k_raw = q_ref[0], k_ref[0]
    qr_ref[0] = ((q_raw * cosine + swap_halves(q_raw) * sine_part) * 0.125).astype(BF16)
    kr_ref[0] = (k_raw * cosine + swap_halves(k_raw) * sine_part).astype(BF16)
    v_mix = (0.5 * v_ref[0] + 0.5 * vf_ref[0].astype(F32)).astype(BF16)
    vm_ref[0] = v_mix
    v_turned = v_mix.T
    for step in range(length // BLOCK):
        begin, keys = step * BLOCK, (step + 1) * BLOCK
        queries = two_heads(qr_ref[0, begin:keys, :])
        scores = dot_nt(kr_ref[0, :keys, :], queries)
        scores = jnp.where(seen(first_ref, begin, keys), scores, -1e30)
        top = jnp.max(scores, axis=0, keepdims=True)
        exps = jnp.exp(scores - top)
        total = jnp.sum(exps, axis=0, keepdims=True)
        chances = (exps * (1.0 / total)).astype(BF16)
        attended = dot_nn(v_turned[:, :keys], chances)
        att_ref[0, begin:keys, :] = one_pair(attended, BLOCK).astype(BF16)
        log_total = top + jnp.log(total)
        lse_ref[0, 0:1, begin:keys] = log_total[:, :BLOCK]
        lse_ref[0, 1:2, begin:keys] = log_total[:, BLOCK:]


def attend_back_kernel(
    qr_ref, kr_ref, vm_ref, att_ref, d_ref, lse_ref, cos_ref, sin_ref, first_ref,
    dq_ref, dk_ref, dv_ref, key_sum, value_sum,
):
    length = qr_ref.shape[1]
    key_sum[...] = jnp.zeros_like(key_sum)
    value_sum[...] = jnp.zeros_like(value_sum)
    k_turned = kr_ref[0].T
    cosine, sine_part = cos_ref[...], sin_ref[...]
    product = (d_ref[0].astype(F32) * att_ref[0].astype(F32)).T
    inner = [
        jnp.sum(product[:64], axis=0, keepdims=True),
        jnp.sum(product[64:], axis=0, keepdims=True),
    ]
    for step in range(length // BLOCK):
        begin, keys = step * BLOCK, (step + 1) * BLOCK
        queries = two_heads(qr_ref[0, begin:keys, :])
        d_out = two_heads(d_ref[0, begin:keys, :])
        scores = dot_nt(kr_ref[0, :keys, :], queries)
        log_total = jnp.concatenate(
            [lse_ref[0, 0:1, begin:keys], lse_ref[0, 1:2, begin:keys]], axis=1
        )
        chances = jnp.where(seen(first_ref, begin, keys), jnp.exp(scores - log_total), 0.0)
        d_chances = dot_nt(vm_ref[0, :keys, :], d_out)
        part = jnp.concatenate([inner[0][:, begin:keys], inner[1][:, begin:keys]], axis=1)
        d_scores = (chances * (d_chances - part)).astype(BF16)
        key_sum[:keys, :] += dot_nn(d_scores, queries)
        value_sum[:keys, :] += dot_nn(chances.astype(BF16), d_out)
        d_query = one_pair(dot_nn(k_turned[:, :keys], d_scores), BLOCK) * 0.125
        dq_ref[0, begin:keys, :] = (
            d_query * cosine[begin:keys] - swap_halves(d_query) * sine_part[begin:keys]
        ).astype(BF16)
    d_key = key_sum[...]
    dk_ref[0] = (d_key * cosine - swap_halves(d_key) * sine_part).astype(BF16)
    dv_ref[0] = (0.5 * value_sum[...]).astype(BF16)


def attend(project, first_values, cos_wide, sin_wide, first_pos):
    pairs, length, _ = project.shape
    part = lambda i: pl.BlockSpec((1, length, LANES), lambda p: (p, 0, i))
    table = pl.BlockSpec((length, LANES), lambda p: (0, 0))
    out = jax.ShapeDtypeStruct((pairs, length, LANES), BF16)
    return pl.pallas_call(
        attend_kernel,
        grid=(pairs,),
        in_specs=[part(0), part(1), part(2), part(0), table, table,
                  pl.BlockSpec((1, length), lambda p: (0, 0))],
        out_specs=[part(0)] * 4 + [pl.BlockSpec((1, 2, length), lambda p: (p, 0, 0))],
        out_shape=[out] * 4 + [jax.ShapeDtypeStruct((pairs, 2, length), F32)],
        compiler_params=pltpu.CompilerParams(vmem_limit_bytes=48 << 20),
        cost_estimate=pl.CostEstimate(
            flops=pairs * length * length * 128 * 8, bytes_accessed=pairs * length * 128 * 24,
            transcendentals=pairs * length * length),
    )(project, project, project, first_values, cos_wide, sin_wide, first_pos[None, :])


def attend_back(saved, d_attended, cos_wide, sin_wide, first_pos):
    q_rot, k_rot, v_mix, attended, log_total = saved
    pairs, length, _ = q_rot.shape
    part = pl.BlockSpec((1, length, LANES), lambda p: (p, 0, 0))
    table = pl.BlockSpec((length, LANES), lambda p: (0, 0))
    out = jax.ShapeDtypeStruct((pairs, length, LANES), BF16)
    return pl.pallas_call(
        attend_back_kernel,
        grid=(pairs,),
        in_specs=[part] * 5 + [pl.BlockSpec((1, 2, length), lambda p: (p, 0, 0)), table, table,
                               pl.BlockSpec((1, length), lambda p: (0, 0))],
        out_specs=[part] * 3,
        out_shape=[out] * 3,
        scratch_shapes=[pltpu.VMEM((length, LANES), F32)] * 2,
        compiler_params=pltpu.CompilerParams(vmem_limit_bytes=48 << 20),
        cost_estimate=pl.CostEstimate(
            flops=pairs * length * length * 128 * 20, bytes_accessed=pairs * length * 128 * 24,
            transcendentals=pairs * length * length),
    )(q_rot, k_rot, v_mix, attended, d_attended, log_total, cos_wide, sin_wide, first_pos[None, :])


class Links:
    def __init__(self, n_seq, n_head, slots):
        self.n_seq, self.n_head, self.slots = n_seq, n_head, slots
        self.ranks = n_head // slots
        self.slot = lax.axis_index("head") // self.ranks
        self.rank = lax.axis_index("head") % self.ranks
        self.alike = [
            [s * n_head + q * self.ranks + r for s in range(n_seq) for q in range(slots)]
            for r in range(self.ranks)
        ]

    def permute(self, value, partner):
        pairs = []
        for s in range(self.n_seq):
            for h in range(self.n_head):
                to_s, to_h = partner(s, h)
                pairs.append((s * self.n_head + h, to_s * self.n_head + to_h))
        return lax.ppermute(value, AXES, pairs)

    def swap_slots(self, value):
        got = [lax.dynamic_index_in_dim(value, self.slot, 0, keepdims=False)]
        for step in range(1, self.slots):
            piece = lax.dynamic_index_in_dim(value, self.slot ^ step, 0, keepdims=False)
            got.append(self.permute(piece, lambda s, h: (s, h ^ (step * self.ranks))))
        got = jnp.stack(got)
        return jnp.stack(
            [lax.dynamic_index_in_dim(got, self.slot ^ q, 0, keepdims=False) for q in range(self.slots)]
        )

    def gather_ranks(self, value):
        got = [value] + [
            self.permute(value, lambda s, h: (s, h ^ step)) for step in range(1, self.ranks)
        ]
        got = jnp.stack(got)
        return jnp.stack(
            [lax.dynamic_index_in_dim(got, self.rank ^ r, 0, keepdims=False) for r in range(self.ranks)]
        )

    def sum_ranks(self, value):
        total = lax.dynamic_index_in_dim(value, self.rank, 0, keepdims=False)
        for step in range(1, self.ranks):
            piece = lax.dynamic_index_in_dim(value, self.rank ^ step, 0, keepdims=False)
            got = self.permute(piece.astype(BF16), lambda s, h: (s, h ^ step))
            total = total + got.astype(F32)
        return total

    def gather_alike(self, value):
        out = lax.all_gather(value, AXES, axis=0, axis_index_groups=self.alike)
        return out.reshape((self.n_seq, self.slots) + value.shape)

    def sum_alike(self, value):
        flat = value.reshape((self.n_seq * self.slots,) + value.shape[2:])
        return lax.psum_scatter(flat, AXES, scatter_dimension=0, axis_index_groups=self.alike)

    def whole_sequence(self, own):
        both = self.gather_ranks(own)
        return jnp.swapaxes(both, 0, 1).reshape(-1, own.shape[-1])

    def own_sum(self, full):
        rows = full.shape[0] // (self.slots * self.ranks)
        parts = full.reshape(self.slots, self.ranks, rows, full.shape[-1])
        return self.sum_ranks(jnp.swapaxes(parts, 0, 1)).reshape(-1, full.shape[-1])


def left_update(weight_rows, grad, row_begin, big_stat, big_root, small_stat, small_root, width):
    members, row_part, columns = weight_rows.shape
    model_width = grad.shape[1]
    blocks = columns // width
    grad_blocks = grad.reshape(members, model_width, blocks, width)
    grad_rows = lax.dynamic_slice_in_dim(grad_blocks, row_begin, row_part, 1)
    ein = functools.partial(jnp.einsum, preferred_element_type=F32)
    big_new = STAT_DECAY * big_stat + (1.0 - STAT_DECAY) * ein(
        "nrbk,nsbk->nbrs", grad_rows, grad_blocks
    )
    small_new = STAT_DECAY * small_stat + (1.0 - STAT_DECAY) * ein(
        "nrbk,nrbl->nbkl", grad_blocks, grad_blocks
    )
    step_dir = ein("nbrs,nsbk->nrbk", big_root.astype(BF16), grad_blocks)
    step_dir = ein("nrbk,nbkl->nrbl", step_dir.astype(BF16), small_root.astype(BF16))
    step_dir = step_dir * lax.rsqrt(jnp.mean(step_dir * step_dir, axis=-1, keepdims=True) + EPSILON)
    return weight_rows - STEP_RATE * step_dir.reshape(members, row_part, columns), big_new, small_new


def right_update(weight_cols, grad, col_begin, big_stat, big_root, small_stat, small_root, width, rate):
    rows_all, col_part = weight_cols.shape
    model_width = grad.shape[1]
    blocks = rows_all // width
    grad_blocks = grad.reshape(blocks, width, model_width)
    grad_cols = lax.dynamic_slice_in_dim(grad_blocks, col_begin, col_part, 2)
    ein = functools.partial(jnp.einsum, preferred_element_type=F32)
    big_new = STAT_DECAY * big_stat + (1.0 - STAT_DECAY) * ein("bkr,bks->brs", grad_cols, grad_blocks)
    small_new = STAT_DECAY * small_stat + (1.0 - STAT_DECAY) * ein(
        "bkr,blr->bkl", grad_blocks, grad_blocks
    )
    step_dir = ein("bkl,bls->bks", small_root.astype(BF16), grad_blocks)
    step_dir = ein("bks,brs->bkr", step_dir.astype(BF16), big_root.astype(BF16))
    step_dir = step_dir * lax.rsqrt(jnp.mean(step_dir * step_dir, axis=1, keepdims=True) + EPSILON)
    return weight_cols - rate * step_dir.reshape(rows_all, col_part), big_new, small_new


def shards(
    n_seq,
    n_head,
    layer_input,
    values_first,
    w_qkv,
    w_gate_up,
    w_out,
    w_down,
    norm_gains,
    out_grad,
    segments,
    counts,
    stats_wide,
    roots_wide,
    stats_head,
    roots_head,
    stats_unit,
    roots_unit,
):
    slots, rows, width = layer_input.shape
    length = segments.shape[1]
    row_part, head_cols, ffn_cols = w_qkv.shape[1], w_qkv.shape[2], w_gate_up.shape[2]
    head_dim, unit_block = stats_head.shape[2], stats_unit.shape[2]
    links = Links(n_seq, n_head, slots)
    row_begin = lax.axis_index("seq") * row_part
    is_live = links.slot < counts[0]
    my_heads = slots * head_cols
    pairs = my_heads // LANES

    def pair_major(value):
        if head_cols == LANES:
            return value
        per = LANES // head_cols
        value = value.reshape(pairs, per, length, head_cols)
        return jnp.swapaxes(value, 1, 2).reshape(pairs, length, LANES)

    def slot_major(value):
        if head_cols == LANES:
            return value
        per = LANES // head_cols
        value = value.reshape(pairs, length, per, head_cols)
        return jnp.swapaxes(value, 1, 2).reshape(slots, length, head_cols)

    qkv_all = links.gather_alike(w_qkv.astype(BF16))
    x_own = links.swap_slots(layer_input).reshape(slots * rows, width).astype(F32)
    first_all = pair_major(links.swap_slots(values_first))
    out_all = links.gather_alike(w_out.astype(BF16))
    gate_up_all = links.gather_alike(w_gate_up.astype(BF16))
    down_all = links.gather_alike(w_down.astype(BF16))
    per = LANES // head_cols
    qkv_w = qkv_all.reshape(n_seq, pairs, per, 3, row_part, head_cols)
    qkv_w = qkv_w.transpose(1, 0, 4, 3, 2, 5).reshape(pairs, width, 3 * LANES)
    out_w = out_all.transpose(1, 2, 0, 3).reshape(my_heads, width)
    gate_up_w = gate_up_all.transpose(0, 3, 2, 1, 4).reshape(width, 2 * slots * ffn_cols)
    down_w = down_all.transpose(1, 2, 0, 3).reshape(slots * ffn_cols, width)
    units = slots * ffn_cols

    segment_ids = lax.dynamic_index_in_dim(segments, links.slot, 0, keepdims=False)
    first_pos, cos_wide, sin_wide = position_tables(segment_ids, head_dim)

    inverse_one = lax.rsqrt(jnp.mean(x_own * x_own, axis=-1, keepdims=True) + EPSILON)
    normed_one = x_own * inverse_one
    h_one = links.whole_sequence(
        (normed_one * norm_gains[0]).astype(BF16).reshape(slots, rows, width)
    )
    project = jnp.einsum("ld,pdc->plc", h_one, qkv_w, preferred_element_type=F32)
    saved = attend(project, first_all, cos_wide, sin_wide, first_pos)
    attended = jnp.swapaxes(saved[3], 0, 1).reshape(length, my_heads)
    attn_out = links.own_sum(dot_nn(attended, out_w))
    middle = x_own + attn_out
    inverse_two = lax.rsqrt(jnp.mean(middle * middle, axis=-1, keepdims=True) + EPSILON)
    normed_two = middle * inverse_two
    h_two = links.whole_sequence(
        (normed_two * norm_gains[1]).astype(BF16).reshape(slots, rows, width)
    )
    gate_up = dot_nn(h_two, gate_up_w)
    gate, up = gate_up[:, :units], gate_up[:, units:]
    sigmoid_gate = jax.nn.sigmoid(gate)
    activated = gate * sigmoid_gate
    hidden = (activated * up).astype(BF16)
    ffn_out = links.own_sum(dot_nn(hidden, down_w))
    block_delta = jnp.where(is_live, attn_out + ffn_out, 0.0).astype(BF16)
    block_out = layer_input.astype(F32) + links.swap_slots(
        block_delta.reshape(slots, rows, width)
    ).astype(F32)

    grad_own = links.swap_slots(out_grad)
    d_own = jnp.where(is_live, grad_own, jnp.zeros_like(grad_own))
    d_out = d_own.reshape(slots * rows, width).astype(F32)
    d_ffn = links.whole_sequence(d_own)
    g_down = dot_tn(hidden, d_ffn)
    sum_down = links.sum_alike(
        g_down.astype(BF16).reshape(slots, ffn_cols, n_seq, row_part).transpose(2, 0, 1, 3)
    )
    d_hidden = dot_nt(d_ffn, down_w)
    d_gate = (
        d_hidden * up * sigmoid_gate * (1.0 + gate * (1.0 - sigmoid_gate))
    ).astype(BF16)
    d_up = (d_hidden * activated).astype(BF16)
    d_gate_up = jnp.concatenate([d_gate, d_up], axis=1)
    d_normed_two = links.own_sum(dot_nt(d_gate_up, gate_up_w))
    g_gate_up = dot_tn(h_two, d_gate_up)
    sum_gate_up = links.sum_alike(
        g_gate_up.astype(BF16)
        .reshape(n_seq, row_part, 2, slots, ffn_cols)
        .transpose(0, 3, 2, 1, 4)
    )
    gain_two = jnp.sum(normed_two * d_normed_two, axis=0)
    middle_delta = norm_back(d_normed_two * norm_gains[1], normed_two, inverse_two)
    d_middle = d_out + middle_delta
    d_attn = links.whole_sequence(d_middle.astype(BF16).reshape(slots, rows, width))
    d_attended = dot_nt(d_attn, out_w).astype(BF16)
    d_query, d_key, d_value = attend_back(
        saved,
        jnp.swapaxes(d_attended.reshape(length, pairs, LANES), 0, 1),
        cos_wide,
        sin_wide,
        first_pos,
    )
    first_grad = links.swap_slots(slot_major(d_value)).astype(F32)
    g_out = dot_tn(attended, d_attn)
    sum_out = links.sum_alike(
        g_out.astype(BF16).reshape(slots, head_cols, n_seq, row_part).transpose(2, 0, 1, 3)
    )
    d_project = jnp.concatenate([d_query, d_key, d_value], axis=2)
    g_qkv = jnp.einsum("ld,plc->pdc", h_one, d_project, preferred_element_type=F32)
    sum_qkv = links.sum_alike(
        g_qkv.astype(BF16)
        .reshape(pairs, n_seq, row_part, 3, per, head_cols)
        .transpose(1, 0, 4, 3, 2, 5)
        .reshape(n_seq, slots, 3, row_part, head_cols)
    )
    d_normed_one = links.own_sum(
        jnp.einsum("plc,pdc->ld", d_project, qkv_w, preferred_element_type=F32)
    )
    gain_one = jnp.sum(normed_one * d_normed_one, axis=0)
    input_delta = middle_delta + norm_back(d_normed_one * norm_gains[0], normed_one, inverse_one)
    input_delta = jnp.where(is_live, input_delta, 0.0).astype(BF16)
    input_grad = out_grad.astype(F32) + links.swap_slots(
        input_delta.reshape(slots, rows, width)
    ).astype(F32)

    grad_gains = lax.psum(jnp.stack([gain_one, gain_two]), AXES)
    new_gains = norm_gains - GAIN_RATE * grad_gains * lax.rsqrt(
        jnp.mean(grad_gains * grad_gains, axis=-1, keepdims=True) + EPSILON
    )

    full_down = lax.all_gather(sum_down, "seq", axis=1, tiled=True)
    full_gate_up = lax.all_gather(sum_gate_up, "seq", axis=1, tiled=True)
    full_out = lax.all_gather(sum_out, "seq", axis=1, tiled=True)
    full_qkv = lax.all_gather(sum_qkv, "seq", axis=1, tiled=True)

    new_down, wide_down, unit_down = right_update(
        w_down, full_down, row_begin, stats_wide[6], roots_wide[6], stats_unit[2], roots_unit[2],
        unit_block, STEP_RATE,
    )
    new_gate_up, wide_gu, unit_gu = left_update(
        w_gate_up, full_gate_up, row_begin, stats_wide[3:5], roots_wide[3:5], stats_unit[0:2],
        roots_unit[0:2], unit_block,
    )
    new_out, wide_out, head_out = right_update(
        w_out, full_out, row_begin, stats_wide[5], roots_wide[5], stats_head[3], roots_head[3],
        head_dim, OUT_RATE,
    )
    new_qkv, wide_qkv, head_qkv = left_update(
        w_qkv, full_qkv, row_begin, stats_wide[0:3], roots_wide[0:3], stats_head[0:3],
        roots_head[0:3], head_dim,
    )
    return (
        block_out,
        input_grad,
        first_grad,
        sum_qkv.astype(F32),
        sum_gate_up.astype(F32),
        sum_out.astype(F32),
        sum_down.astype(F32),
        grad_gains,
        new_qkv,
        new_gate_up,
        new_out,
        new_down,
        new_gains,
        jnp.concatenate([wide_qkv, wide_gu, wide_down[None]], axis=0),
        wide_out,
        jnp.concatenate([head_qkv, head_out[None]], axis=0),
        jnp.concatenate([unit_gu, unit_down[None]], axis=0),
    )


def solution(mesh):
    return jax.shard_map(
        functools.partial(shards, mesh.shape["seq"], mesh.shape["head"]),
        mesh=mesh,
        in_specs=(
            P("seq", "head", None),
            P("seq", None, "head"),
            P(None, "seq", "head"),
            P(None, "seq", "head"),
            P("head", "seq"),
            P("head", "seq"),
            P(),
            P("seq", "head", None),
            P("seq", None),
            P("seq"),
            P(None, "head", "seq", None),
            P(None, "head", "seq", None),
            P(None, "head", None, None),
            P(None, "head", None, None),
            P(None, "head", None, None),
            P(None, "head", None, None),
        ),
        out_specs=(
            P("seq", "head", None),
            P("seq", "head", None),
            P("seq", None, "head"),
            P(None, "seq", "head"),
            P(None, "seq", "head"),
            P("head", "seq"),
            P("head", "seq"),
            P(),
            P(None, "seq", "head"),
            P(None, "seq", "head"),
            P("head", "seq"),
            P("head", "seq"),
            P(),
            P(None, "head", "seq", None),
            P("head", "seq", None),
            P(None, "head", None, None),
            P(None, "head", None, None),
        ),
        check_vma=False,
    )
```

time: 1690 us -> 901 us (0.53)
  waiting for transfers between devices: 892 us -> 399 us
  matrix products: 259 us -> 108 us
  blocking collectives: 192 us -> 87.3 us
  other arithmetic: 152 us -> 79.5 us
  starting transfers between devices: 1.62 us -> 42.3 us
  Pallas kernels: 0 us -> 33 us
  local copies, waits for them, and re-layouts: 153 us -> 130 us
  loops' own time: 18.3 us -> 0 us
    reduce_scatter x16 -> x4, waiting for transfers between devices: 591 us -> 131 us  [sum_alike(): lax.psum_scatter(flat, AXES, scatter_dimension=0, axis_index_groups=self....]
    dot_general x100 -> x18, matrix products: 196 us -> 69.5 us  [the longest x3 17.9 us: dot_nn(): return jnp.dot(matrix_a, matrix_b, preferred_element_type=F32)]
    ppermute x0 -> x26, waiting for transfers between devices: none -> 115 us  [permute(): return lax.ppermute(value, AXES, pairs)]
    all_gather x12 -> x3, blocking collectives: 154 us -> 40.8 us  [the longest x1 15.2 us: shards(): full_down = lax.all_gather(sum_down, 'seq', axis=1, tiled=True)]
    all_gather x20 -> x5, waiting for transfers between devices: 251 us -> 153 us  [the longest x4 142 us: gather_alike(): out = lax.all_gather(value, AXES, axis=0, axis_index_groups=self.alike)]
    dynamic_update_slice x24 -> x0, local copies, waits for them, and re-layouts: 65.1 us -> none  [the longest x16 48.3 us: attend_back(): lax.scan(one_block, (zeros_kv, zeros_kv), (q_blocks, seg_blocks, begins,...]
    reshape x8 -> x11, local copies, waits for them, and re-layouts: 4.79 us -> 57.5 us  [the longest x1 14 us: shards(): sum_gate_up = links.sum_alike(g_gate_up.astype(BF16).reshape(n_seq, row_p...]
    psum x1 -> x0, waiting for transfers between devices: 47.9 us -> none  [shards(): lax.psum(summed[0].astype(jnp.bfloat16), 'seq').astype(jnp.float32)]
  transfers between devices with their start and end apart: 37 -> 35, of which waited for: 30 -> 17; matrix products, arithmetic and copies ran while one was open for 9% -> 25% of each run, Pallas kernels for 0% -> 4%
where the time goes in v1:
time: 901 us; the launch traced here: 895 us
  waiting for transfers between devices  399 us (44%)
  local copies, waits for them, and re-layouts  130 us (14%)
  matrix products  108 us (12%)
  blocking collectives  87.3 us (10%)
  other arithmetic  79.5 us (9%)
  starting transfers between devices  42.3 us (5%)
  Pallas kernels  33 us (4%)
  between operations  16 us (2%)
    all_gather x4, waiting for transfers between devices, gather_alike(): out = lax.all_gather(value, AXES, axis=0, axis_index_groups=self.alike)  142 us
    reduce_scatter x4, waiting for transfers between devices, sum_alike(): lax.psum_scatter(flat, AXES, scatter_dimension=0, axis_index_groups=self....  131 us
    ppermute x26, waiting for transfers between devices, permute(): return lax.ppermute(value, AXES, pairs)  115 us
    psum x1, blocking collectives, shards(): grad_gains = lax.psum(jnp.stack([gain_one, gain_two]), AXES)  46.5 us
    ppermute x26, starting transfers between devices, permute(): return lax.ppermute(value, AXES, pairs)  41.9 us
    unnamed x153, local copies, waits for them, and re-layouts  25.8 us
    dot_general x3, matrix products, dot_tn(): lax.dot_general(matrix_a, matrix_b, (((0,), (0,)), ((), ())), preferred_e...  20.5 us
  transfers between devices with their start and end apart: 35, of which 17 were waited for; matrix products, arithmetic and copies ran while one was open for 25% of the time, Pallas kernels for 4%

profile of v1, /device:TPU:0, one launch (start us, length us, event | category | flops | bytes accessed | tf_op | source)
XLA Modules:
  0.0 895.3 jit_solution(1584446909295689561)
XLA Ops:
  27.0 12.9 %collective-permute-start.4 = (bf16[1024,128]{1,0:T(8,128)(2,1)}, bf16[1024,128]{1,0:T(8,128)(2,1)}, u32[]{:S(2)}, u32[]{:S(2)}) collective-permute-start(bf16[1024,128]{1,0:T(8,128)(2,1)} %get-tuple-element.93), channel_id=1, source_target_pairs={{0,2},{1,3},{2,0},{3,1},{4,6},{5,7},{6,4},{7,5},{8,10},{9,11},{10,... | collective-permute-start | bytes 786440 | tf_op jit(solution)/shard_map/ppermute | solution.py:206
  39.9 15.6 %collective-permute-done.1 = bf16[128,1024]{1,0:T(8,128)(2,1)S(1)} collective-permute-done((bf16[128,1024]{1,0:T(8,128)(2,1)S(1)}, bf16[128,1024]{1,0:T(8,128)(2,1)S(1)}, u32[]{:S(2)}, u32[]{:S(2)}) %collective-permute-start.1) | collective-permute-done | bytes 262176 | tf_op jit(solution)/shard_map/ppermute | solution.py:206
  87.4 66.7 %all-gather.14.cloned.1.call-done = bf16[48,256,128]{2,1,0:T(8,128)(2,1)} async-done(((bf16[3,256,128]{2,1,0:T(8,128)(2,1)}), bf16[48,256,128]{2,1,0:T(8,128)(2,1)}) %all-gather.14.cloned.1.call-update) | async-done | bytes 3145744 | tf_op jit(solution)/shard_map/all_gather | solution.py:236
  174.8 15.6 %shard_map.287 = (bf16[4,1024,128]{2,1,0:T(8,128)(2,1)S(1)}, bf16[4,1024,128]{2,1,0:T(8,128)(2,1)S(1)}, bf16[4,1024,128]{2,1,0:T(8,128)(2,1)S(1)}, bf16[4,1024,128]{2,1,0:T(8,128)(2,1)S(1)}, f32[4,2,1024]{2,1,0:T(2,128)S(1)}) custom-call(f32[4,1024,384]{2,1,0:T(8,128)} %convolution_bitcast_fusion.q_ref.k_ref.v_ref, ...), custom_call_target="tpu_custom_call" | custom-call | flops 4294967296 | bytes 12582912 | tf_op jit(solution)/shard_map/pallas_call | solution.py:154
  208.5 11.8 %collective-permute-done.15 = bf16[128,1024]{1,0:T(8,128)(2,1)} collective-permute-done((bf16[128,1024]{1,0:T(8,128)(2,1)}, bf16[128,1024]{1,0:T(8,128)(2,1)}, u32[]{:S(2)}, u32[]{:S(2)}) %collective-permute-start.15) | collective-permute-done | bytes 262176 | tf_op jit(solution)/shard_map/ppermute | solution.py:206
  220.3 21.1 %collective-permute-done.14 = bf16[128,1024]{1,0:T(8,128)(2,1)} collective-permute-done((bf16[128,1024]{1,0:T(8,128)(2,1)}, bf16[128,1024]{1,0:T(8,128)(2,1)}, u32[]{:S(2)}, u32[]{:S(2)}) %collective-permute-start.14) | collective-permute-done | bytes 262176 | tf_op jit(solution)/shard_map/ppermute | solution.py:206
  262.1 66.6 %all-gather.18.cloned.1.call-done = bf16[32,256,352]{1,2,0:T(8,128)(2,1)} async-done(((bf16[2,256,352]{1,2,0:T(8,128)(2,1)}), bf16[32,256,352]{1,2,0:T(8,128)(2,1)}) %all-gather.18.cloned.1.call-update) | async-done | bytes 5767184 | tf_op jit(solution)/shard_map/all_gather | solution.py:236
  338.2 9.0 %fusion.87 = f32[1024,2816]{1,0:T(8,128)} fusion(bf16[1024,1024]{1,0:T(8,128)(2,1)S(1)} %bitcast.380, bf16[1024,2816]{0,1:T(8,128)(2,1)S(1)} %bitcast.362), kind=kOutput, calls=%fused_computation.245 | convolution fusion | flops 5905580032 | bytes 19398656 | tf_op jit(solution)/shard_map/dot_general | solution.py:35
  347.1 10.4 %multiply_convert_fusion.1 = (bf16[1024,1408]{1,0:T(8,128)(2,1)}, bf16[1024,1408]{1,0:T(8,128)(2,1)}, bf16[1024,1408]{1,0:T(8,128)(2,1)}) fusion(f32[1024,2816]{1,0:T(8,128)} %fusion.87, bf16[1024,1024]{1,0:T(8,128)(2,1)S(1)} %bitcast.382, bf16[1408,1024]{1,0:T(8,128)(2,1)S(1)} %bitcast.376), kind=kOutput, calls=%fused_computation.6 | convolution fusion | flops 2974416896 | bytes 25165824 | tf_op jit(solution)/shard_map/dot_general | solution.py:23
  408.4 17.3 %shard_map.288 = (bf16[4,1024,128]{2,1,0:T(8,128)(2,1)S(1)}, bf16[4,1024,128]{2,1,0:T(8,128)(2,1)S(1)}, bf16[4,1024,128]{2,1,0:T(8,128)(2,1)S(1)}) custom-call(bf16[4,1024,128]{2,1,0:T(8,128)(2,1)S(1)} %copy-done.2, bf16[4,1024,128]{2,1,0:T(8,128)(2,1)} %copy-done.3, bf16[4,1024,128]{2,1,0:T(8,128)(2,1)} %copy-done.4, bf16[4,1024,128]{2,1,0:T(8,128)(2,1)} %copy-done, ...), custom_call_target="tpu_custom_call" | custom-call | flops 10737418240 | bytes 12582912 | tf_op jit(solution)/shard_map/pallas_call | solution.py:174
  445.1 11.1 %convolution_convert_fusion = bf16[1024,2816]{1,0:T(8,128)(2,1)} fusion(bf16[1024,1024]{1,0:T(8,128)(2,1)} %bitcast.379, bf16[1024,1408]{1,0:T(8,128)(2,1)} %get-tuple-element.42, bf16[1024,1408]{1,0:T(8,128)(2,1)} %get-tuple-element.41), kind=kOutput, calls=%fused_computation.10 | convolution fusion | flops 5919997952 | bytes 13631488 | tf_op jit(solution)/shard_map/dot_general | solution.py:29
  456.2 14.0 %reshape.632 = bf16[4,256,2,4,352]{4,3,2,1,0:T(4,128)(2,1)} reshape(bf16[1024,2816]{1,0:T(8,128)(2,1)} %convolution_convert_fusion) | data formatting | bytes 11534336 | tf_op jit(solution)/shard_map/reshape | solution.py:394
  470.2 10.6 %copy.156 = bf16[4,4,2,256,352]{3,4,2,1,0:T(8,128)(2,1)} copy(bf16[4,4,2,256,352]{4,1,2,3,0:T(4,128)(2,1)} %bitcast.335) | data formatting | bytes 11534336 | tf_op jit(solution)/shard_map/transpose | solution.py:395
  496.5 9.6 %convert.14 = bf16[7,2,256,1024]{3,2,1,0:T(8,128)(2,1)} convert(f32[7,2,256,1024]{3,2,1,0:T(8,128)} %param.27) | non-fusion elementwise | flops 3670016 | bytes 22020096 | tf_op jit(solution)/shard_map/convert.7
  527.4 26.4 %collective-permute-done.11 = bf16[128,1024]{1,0:T(8,128)(2,1)S(1)} collective-permute-done((bf16[128,1024]{1,0:T(8,128)(2,1)S(1)}, bf16[128,1024]{1,0:T(8,128)(2,1)S(1)}, u32[]{:S(2)}, u32[]{:S(2)}) %collective-permute-start.11) | collective-permute-done | bytes 262176 | tf_op jit(solution)/shard_map/ppermute | solution.py:206
  566.7 19.0 %collective-permute-done.24 = bf16[1024,128]{1,0:T(8,128)(2,1)S(1)} collective-permute-done((bf16[1024,128]{1,0:T(8,128)(2,1)S(1)}, bf16[1024,128]{1,0:T(8,128)(2,1)S(1)}, u32[]{:S(2)}, u32[]{:S(2)}) %collective-permute-start.24) | collective-permute-done | bytes 262176 | tf_op jit(solution)/shard_map/ppermute | solution.py:206
  596.0 46.5 %psum.7 = f32[2,1024]{1,0:T(2,128)S(1)} all-reduce(f32[2,1024]{1,0:T(2,128)S(1)} %pad_maximum_fusion.14), channel_id=1, replica_groups=mesh['seq'=4,'head'=8] {'seq','head'}, use_global_device_ids=true, to_apply=%region_12.13 | all-reduce | flops 2048 | bytes 16384 | tf_op jit(solution)/shard_map/psum | solution.py:432
  646.2 11.2 %all-gather.6 = bf16[1,128,1024]{2,1,0:T(8,128)(2,1)S(1)} all-gather(bf16[1,128,256]{2,1,0:T(8,128)(2,1)} %reduce-scatter.9.cloned.1.call-done), channel_id=8, replica_groups=mesh['seq'=4,'head'=8] {'seq'}, dimensions={2}, use_global_device_ids=true | all-gather | bytes 327680 | tf_op jit(solution)/shard_map/all_gather | solution.py:439
  665.7 15.2 %all-gather.7 = bf16[1,352,1024]{2,1,0:T(8,128)(2,1)S(1)} all-gather(bf16[1,352,256]{2,1,0:T(8,128)(2,1)} %reduce-scatter.11.cloned.1.call-done), channel_id=9, replica_groups=mesh['seq'=4,'head'=8] {'seq'}, dimensions={2}, use_global_device_ids=true | all-gather | bytes 901120 | tf_op jit(solution)/shard_map/all_gather | solution.py:437
  688.9 17.4 %reduce-scatter.5.cloned.1.call-done = bf16[1,3,256,128]{3,2,1,0:T(8,128)(2,1)} async-done(((bf16[16,3,256,128]{3,2,1,0:T(8,128)(2,1)}), bf16[1,3,256,128]{3,2,1,0:T(8,128)(2,1)}) %reduce-scatter.5.cloned.1.call-update) | async-done | bytes 196624 | tf_op jit(solution)/shard_map/reduce_scatter | solution.py:241
  706.3 14.4 %all-gather.4 = bf16[1,3,1024,128]{3,2,1,0:T(8,128)(2,1)} all-gather(bf16[1,3,256,128]{3,2,1,0:T(8,128)(2,1)} %reduce-scatter.5.cloned.1.call-done), channel_id=6, replica_groups=mesh['seq'=4,'head'=8] {'seq'}, dimensions={2}, use_global_device_ids=true | all-gather | bytes 983040 | tf_op jit(solution)/shard_map/all_gather | solution.py:440
  722.2 113.6 %reduce-scatter.7.cloned.1.call-done = bf16[1,2,256,352]{2,3,1,0:T(8,128)(2,1)} async-done(((bf16[16,2,256,352]{2,3,1,0:T(8,128)(2,1)}), bf16[1,2,256,352]{2,3,1,0:T(8,128)(2,1)}) %reduce-scatter.7.cloned.1.call-update) | async-done | bytes 360464 | tf_op jit(solution)/shard_map/reduce_scatter | solution.py:241
  853.8 10.8 %all-gather.22.cloned.1.call-done = bf16[1,2,1024,352]{2,3,1,0:T(8,128)(2,1)} async-done(((bf16[1,2,256,352]{2,3,1,0:T(8,128)(2,1)}), bf16[1,2,1024,352]{2,3,1,0:T(8,128)(2,1)}) %all-gather.22.cloned.1.call-update) | async-done | bytes 1441808 | tf_op jit(solution)/shard_map/all_gather | solution.py:438
  877.2 11.4 %pad_maximum_fusion = f32[6,2,256,1024]{3,2,1,0:T(8,128)} fusion(f32[1,2,256,1024]{3,2,1,0:T(8,128)S(1)} %fusion.26, f32[2,2,256,1024]{3,2,1,0:T(8,128)} %add_multiply_fusion.1, f32[3,2,256,1024]{3,2,1,0:T(8,128)} %add_multiply_fusion), kind=kLoop, calls=%fused_computation | loop fusion | flops 6291456 | bytes 25165824 | tf_op jit(solution)/shard_map/concatenate | solution.py:472
  (356 shorter events, 301.1 us)
Async XLA Ops:
  7.2 76.6 %all-gather.16.cloned.1.call-start = ((), (), s32[]{:S(2)}) async-start(), calls=%async_computation.9 | async-start | bytes 1114112 | tf_op jit(solution)/shard_map/all_gather | solution.py:236
  8.9 145.1 %all-gather.14.cloned.1.call-start = ((), (), s32[]{:S(2)}) async-start(), calls=%async_computation.8 | async-start | bytes 3342336 | tf_op jit(solution)/shard_map/all_gather | solution.py:236
  10.7 240.2 %all-gather.20.cloned.1.call-start = ((), (), s32[]{:S(2)}) async-start(), calls=%async_computation.11 | async-start | bytes 3063808 | tf_op jit(solution)/shard_map/all_gather | solution.py:236
  12.6 316.2 %all-gather.18.cloned.1.call-start = ((), (), s32[]{:S(2)}) async-start(), calls=%async_computation.10 | async-start | bytes 6127616 | tf_op jit(solution)/shard_map/all_gather | solution.py:236
  13.4 632.7 %reduce-scatter.9.cloned.1.call-start = ((), (), s32[]{:S(2)}) async-start(), calls=%async_computation.6 | async-start | bytes 1114112 | tf_op jit(solution)/shard_map/reduce_scatter | solution.py:241
  19.4 36.1 %collective-permute-start.1 = (bf16[128,1024]{1,0:T(8,128)(2,1)S(1)}, bf16[128,1024]{1,0:T(8,128)(2,1)S(1)}, u32[]{:S(2)}, u32[]{:S(2)}) collective-permute-start(bf16[128,1024]{1,0:T(8,128)(2,1)S(1)} %get-tuple-element.103), channel_id=1, source_target_pairs={{0,4},{1,5},{2,6},{3,7},{4,0},{5,1},{6,2},{7,3},{8,12},{9,13},{10,... | collective-permute-start | bytes 786440 | tf_op jit(solution)/shard_map/ppermute | solution.py:206
  19.4 36.1 %collective-permute-start = (bf16[128,1024]{1,0:T(8,128)(2,1)S(1)}, bf16[128,1024]{1,0:T(8,128)(2,1)S(1)}, u32[]{:S(2)}, u32[]{:S(2)}) collective-permute-start(bf16[128,1024]{1,0:T(8,128)(2,1)S(1)} %get-tuple-element.101), channel_id=1, source_target_pairs={{0,2},{1,3},{2,0},{3,1},{4,6},{5,7},{6,4},{7,5},{8,10},{9,11},{10,... | collective-permute-start | bytes 786440 | tf_op jit(solution)/shard_map/ppermute | solution.py:206
  20.9 44.3 %collective-permute-start.6 = (bf16[1024,128]{1,0:T(8,128)(2,1)}, bf16[1024,128]{1,0:T(8,128)(2,1)}, u32[]{:S(2)}, u32[]{:S(2)}) collective-permute-start(bf16[1024,128]{1,0:T(8,128)(2,1)} %get-tuple-element.94), channel_id=1, source_target_pairs={{0,6},{1,7},{2,4},{3,5},{4,2},{5,3},{6,0},{7,1},{8,14},{9,15},{10,... | collective-permute-start | bytes 786440 | tf_op jit(solution)/shard_map/ppermute | solution.py:206
  24.7 44.0 %collective-permute-start.5 = (bf16[1024,128]{1,0:T(8,128)(2,1)}, bf16[1024,128]{1,0:T(8,128)(2,1)}, u32[]{:S(2)}, u32[]{:S(2)}) collective-permute-start(bf16[1024,128]{1,0:T(8,128)(2,1)} %get-tuple-element.95), channel_id=1, source_target_pairs={{0,4},{1,5},{2,6},{3,7},{4,0},{5,1},{6,2},{7,3},{8,12},{9,13},{10,... | collective-permute-start | bytes 786440 | tf_op jit(solution)/shard_map/ppermute | solution.py:206
  27.0 41.7 %collective-permute-start.4 = (bf16[1024,128]{1,0:T(8,128)(2,1)}, bf16[1024,128]{1,0:T(8,128)(2,1)}, u32[]{:S(2)}, u32[]{:S(2)}) collective-permute-start(bf16[1024,128]{1,0:T(8,128)(2,1)} %get-tuple-element.93), channel_id=1, source_target_pairs={{0,2},{1,3},{2,0},{3,1},{4,6},{5,7},{6,4},{7,5},{8,10},{9,11},{10,... | collective-permute-start | bytes 786440 | tf_op jit(solution)/shard_map/ppermute | solution.py:206
  201.7 41.4 %collective-permute-start.7 = (bf16[4,128,1024]{2,1,0:T(8,128)(2,1)}, bf16[4,128,1024]{2,1,0:T(8,128)(2,1)}, u32[]{:S(2)}, u32[]{:S(2)}) collective-permute-start(bf16[4,128,1024]{2,1,0:T(8,128)(2,1)} %fusion.54), channel_id=1, source_target_pairs={{0,1},{1,0},{2,3},{3,2},{4,5},{5,4},{6,7},{7,6},{8,9},{9,8},{10,11... | collective-permute-start | bytes 3145736 | tf_op jit(solution)/shard_map/ppermute | solution.py:206
  205.3 36.1 %collective-permute-start.14 = (bf16[128,1024]{1,0:T(8,128)(2,1)}, bf16[128,1024]{1,0:T(8,128)(2,1)}, u32[]{:S(2)}, u32[]{:S(2)}) collective-permute-start(bf16[128,1024]{1,0:T(8,128)(2,1)} %get-tuple-element.79), channel_id=1, source_target_pairs={{0,4},{1,5},{2,6},{3,7},{4,0},{5,1},{6,2},{7,3},{8,12},{9,13},{10,... | collective-permute-start | bytes 786440 | tf_op jit(solution)/shard_map/ppermute | solution.py:206
  206.4 35.0 %collective-permute-start.13 = (bf16[128,1024]{1,0:T(8,128)(2,1)}, bf16[128,1024]{1,0:T(8,128)(2,1)}, u32[]{:S(2)}, u32[]{:S(2)}) collective-permute-start(bf16[128,1024]{1,0:T(8,128)(2,1)} %get-tuple-element.77), channel_id=1, source_target_pairs={{0,2},{1,3},{2,0},{3,1},{4,6},{5,7},{6,4},{7,5},{8,10},{9,11},{10,... | collective-permute-start | bytes 786440 | tf_op jit(solution)/shard_map/ppermute | solution.py:206
  384.8 280.9 %reduce-scatter.11.cloned.1.call-start = ((), (), s32[]{:S(2)}) async-start(), calls=%async_computation.7 | async-start | bytes 3063808 | tf_op jit(solution)/shard_map/reduce_scatter | solution.py:241
  402.7 303.7 %reduce-scatter.5.cloned.1.call-start = ((), (), s32[]{:S(2)}) async-start(), calls=%async_computation.4 | async-start | bytes 3342336 | tf_op jit(solution)/shard_map/reduce_scatter | solution.py:241
  445.1 390.7 %reduce-scatter.7.cloned.1.call-start = ((), (), s32[]{:S(2)}) async-start(), calls=%async_computation.5 | async-start | bytes 6127616 | tf_op jit(solution)/shard_map/reduce_scatter | solution.py:241
  480.8 383.7 %all-gather.22.cloned.1.call-start = ((), (), s32[]{:S(2)}) async-start(), calls=%async_computation.12 | async-start | bytes 1802240 | tf_op jit(solution)/shard_map/all_gather | solution.py:438
  513.6 40.3 %collective-permute-start.11 = (bf16[128,1024]{1,0:T(8,128)(2,1)S(1)}, bf16[128,1024]{1,0:T(8,128)(2,1)S(1)}, u32[]{:S(2)}, u32[]{:S(2)}) collective-permute-start(bf16[128,1024]{1,0:T(8,128)(2,1)S(1)} %get-tuple-element.86), channel_id=1, source_target_pairs={{0,4},{1,5},{2,6},{3,7},{4,0},{5,1},{6,2},{7,3},{8,12},{9,13},{10,... | collective-permute-start | bytes 786440 | tf_op jit(solution)/shard_map/ppermute | solution.py:206
  514.4 39.4 %collective-permute-start.10 = (bf16[128,1024]{1,0:T(8,128)(2,1)S(1)}, bf16[128,1024]{1,0:T(8,128)(2,1)S(1)}, u32[]{:S(2)}, u32[]{:S(2)}) collective-permute-start(bf16[128,1024]{1,0:T(8,128)(2,1)S(1)} %get-tuple-element.87), channel_id=1, source_target_pairs={{0,2},{1,3},{2,0},{3,1},{4,6},{5,7},{6,4},{7,5},{8,10},{9,11},{10,... | collective-permute-start | bytes 786440 | tf_op jit(solution)/shard_map/ppermute | solution.py:206
  520.4 67.1 %collective-permute-start.19 = (bf16[4,128,1024]{2,1,0:T(8,128)(2,1)S(1)}, bf16[4,128,1024]{2,1,0:T(8,128)(2,1)S(1)}, u32[]{:S(2)}, u32[]{:S(2)}) collective-permute-start(bf16[4,128,1024]{2,1,0:T(8,128)(2,1)S(1)} %fusion.55), channel_id=1, source_target_pairs={{0,1},{1,0},{2,3},{3,2},{4,5},{5,4},{6,7},{7,6},{8,9},{9,8},{10,11... | collective-permute-start | bytes 3145736 | tf_op jit(solution)/shard_map/ppermute | solution.py:206
  559.5 26.2 %collective-permute-start.24 = (bf16[1024,128]{1,0:T(8,128)(2,1)S(1)}, bf16[1024,128]{1,0:T(8,128)(2,1)S(1)}, u32[]{:S(2)}, u32[]{:S(2)}) collective-permute-start(bf16[1024,128]{1,0:T(8,128)(2,1)S(1)} %get-tuple-element.60), channel_id=1, source_target_pairs={{0,4},{1,5},{2,6},{3,7},{4,0},{5,1},{6,2},{7,3},{8,12},{9,13},{10,... | collective-permute-start | bytes 786440 | tf_op jit(solution)/shard_map/ppermute | solution.py:206
  591.5 51.8 %collective-permute-start.22 = (bf16[128,1024]{1,0:T(8,128)(2,1)S(1)}, bf16[128,1024]{1,0:T(8,128)(2,1)S(1)}, u32[]{:S(2)}, u32[]{:S(2)}) collective-permute-start(bf16[128,1024]{1,0:T(8,128)(2,1)S(1)} %get-tuple-element.67), channel_id=1, source_target_pairs={{0,6},{1,7},{2,4},{3,5},{4,2},{5,3},{6,0},{7,1},{8,14},{9,15},{10,... | collective-permute-start | bytes 786440 | tf_op jit(solution)/shard_map/ppermute | solution.py:206
  592.4 50.9 %collective-permute-start.21 = (bf16[128,1024]{1,0:T(8,128)(2,1)S(1)}, bf16[128,1024]{1,0:T(8,128)(2,1)S(1)}, u32[]{:S(2)}, u32[]{:S(2)}) collective-permute-start(bf16[128,1024]{1,0:T(8,128)(2,1)S(1)} %get-tuple-element.68), channel_id=1, source_target_pairs={{0,4},{1,5},{2,6},{3,7},{4,0},{5,1},{6,2},{7,3},{8,12},{9,13},{10,... | collective-permute-start | bytes 786440 | tf_op jit(solution)/shard_map/ppermute | solution.py:206
  592.5 50.9 %collective-permute-start.20 = (bf16[128,1024]{1,0:T(8,128)(2,1)S(1)}, bf16[128,1024]{1,0:T(8,128)(2,1)S(1)}, u32[]{:S(2)}, u32[]{:S(2)}) collective-permute-start(bf16[128,1024]{1,0:T(8,128)(2,1)S(1)} %get-tuple-element.69), channel_id=1, source_target_pairs={{0,2},{1,3},{2,0},{3,1},{4,6},{5,7},{6,4},{7,5},{8,10},{9,11},{10,... | collective-permute-start | bytes 786440 | tf_op jit(solution)/shard_map/ppermute | solution.py:206
  (84 other events, 1664.3 us)
Sparse Core Ops, SparseCore 0:
  11.4 72.3 all-gather.15
  87.2 66.8 all-gather.13
  156.8 79.5 all-gather.19
  239.6 89.0 all-gather.17
  384.9 76.9 reduce-scatter.8
  464.2 94.1 reduce-scatter.10
  564.1 142.1 reduce-scatter.4
  708.8 126.9 reduce-scatter.6
  837.8 26.7 all-gather.21

commit v2 on v1

--- a/solution.py
+++ b/solution.py
@@ -13,6 +13,7 @@
 OUT_RATE = 0.1
 GAIN_RATE = 0.25
 AXES = ("seq", "head")
+MESH = pl.DeviceIdType.MESH
 LANES = 128
 BLOCK = 256
 BF16 = jnp.bfloat16
@@ -186,16 +187,414 @@
     )(q_rot, k_rot, v_mix, attended, d_attended, log_total, cos_wide, sin_wide, first_pos[None, :])
 
 
+class Place:
+    def __init__(self, n_seq, n_head, slots):
+        self.n_seq, self.slots, self.ranks = n_seq, slots, n_head // slots
+        self.seq = lax.axis_index("seq")
+        head = lax.axis_index("head")
+        self.slot, self.rank = head // self.ranks, head % self.ranks
+
+    def at_slot(self, step):
+        return (self.slot + step + self.slots) % self.slots
+
+    def at_seq(self, step):
+        return (self.seq + step + self.n_seq) % self.n_seq
+
+    def device(self, seq=None, slot=None, rank=None):
+        seq = self.seq if seq is None else seq
+        slot = self.slot if slot is None else slot
+        rank = self.rank if rank is None else rank
+        return (seq, slot * self.ranks + rank)
+
+    def greet(self, with_ranks):
+        others = [self.device(slot=self.at_slot(k)) for k in range(1, self.slots)]
+        others += [self.device(seq=self.at_seq(d)) for d in range(1, self.n_seq)]
+        if with_ranks:
+            others += [
+                self.device(rank=(self.rank + j) % self.ranks) for j in range(1, self.ranks)
+            ]
+        barrier = pltpu.get_barrier_semaphore()
+        for other in others:
+            pl.semaphore_signal(barrier, inc=1, device_id=other, device_id_type=MESH)
+        pl.semaphore_wait(barrier, len(others))
+
+
+class Sender:
+    def __init__(self, send_sems, recv_sems):
+        self.send_sems, self.recv_sems, self.used = send_sems, recv_sems, 0
+
+    def start(self, src, dst, device):
+        copy = pltpu.make_async_remote_copy(
+            src_ref=src,
+            dst_ref=dst,
+            send_sem=self.send_sems.at[self.used],
+            recv_sem=self.recv_sems.at[self.used],
+            device_id=device,
+            device_id_type=MESH,
+        )
+        self.used += 1
+        copy.start()
+        return copy
+
+
+def lanes(index, width):
+    return pl.ds(pl.multiple_of(index * width, width), width)
+
+
+def gather_kernel(
+    n_seq, n_head, sections, x_ref, vf_ref, wt_ref, x_out, vf_out, w_out, send_sems, recv_sems, own_sems
+):
+    slots = x_ref.shape[0]
+    part = wt_ref.shape[1]
+    place = Place(n_seq, n_head, slots)
+    place.greet(False)
+    sender = Sender(send_sems, recv_sems)
+    mine = lanes(place.seq, part)
+
+    def swap(src, dst):
+        return [
+            sender.start(
+                src.at[place.at_slot(k)], dst.at[place.slot], place.device(slot=place.at_slot(k))
+            )
+            for k in (2, 3, 1)
+        ]
+
+    def to_slots(section):
+        rows = pl.ds(*section)
+        return [
+            sender.start(
+                wt_ref.at[rows],
+                w_out.at[place.slot, rows, mine],
+                place.device(slot=place.at_slot(k)),
+            )
+            for k in range(1, slots)
+        ]
+
+    def to_seqs(section, step):
+        rows = pl.ds(*section)
+        slot = place.at_slot(-step)
+        src = wt_ref.at[rows] if step == 0 else w_out.at[slot, rows, mine]
+        return [
+            sender.start(
+                src, w_out.at[slot, rows, mine], place.device(seq=place.at_seq(d))
+            )
+            for d in range(1, n_seq)
+        ]
+
+    own = [
+        pltpu.make_async_copy(x_ref.at[place.slot], x_out.at[place.slot], own_sems.at[0]),
+        pltpu.make_async_copy(vf_ref.at[place.slot], vf_out.at[place.slot], own_sems.at[1]),
+        pltpu.make_async_copy(wt_ref, w_out.at[place.slot, :, mine], own_sems.at[2]),
+    ]
+    x_copies = swap(x_ref, x_out)
+    copies = list(x_copies)
+    for copy in own:
+        copy.start()
+    near = to_slots(sections[0])
+    copies += near
+    copies += to_seqs(sections[0], 0)
+    copies += to_seqs(sections[1], 0)
+    received = []
+    for step, copy in enumerate(near):
+        copy.wait_recv()
+        copies += to_seqs(sections[0], step + 1)
+    received += near
+    copies += swap(vf_ref, vf_out)
+    near = to_slots(sections[1])
+    copies += near
+    for step, copy in enumerate(near):
+        copy.wait_recv()
+        copies += to_seqs(sections[1], step + 1)
+    received += near
+    for copy in copies:
+        if all(copy is not other for other in received):
+            copy.wait_recv()
+    for copy in copies:
+        copy.wait_send()
+    for copy in own:
+        copy.wait()
+
+
+def gather_inputs(n_seq, n_head, sections, layer_input, values_first, weight_rows):
+    slots = layer_input.shape[0]
+    rows, part = weight_rows.shape
+    count = 2 * (slots - 1) + len(sections) * ((slots - 1) + slots * (n_seq - 1))
+    any_space = pl.BlockSpec(memory_space=pl.ANY)
+    return pl.pallas_call(
+        functools.partial(gather_kernel, n_seq, n_head, sections),
+        in_specs=[any_space] * 3,
+        out_specs=[any_space] * 3,
+        out_shape=[
+            jax.ShapeDtypeStruct(layer_input.shape, BF16),
+            jax.ShapeDtypeStruct(values_first.shape, BF16),
+            jax.ShapeDtypeStruct((slots, rows, part * n_seq), BF16),
+        ],
+        scratch_shapes=[
+            pltpu.SemaphoreType.DMA((count,)),
+            pltpu.SemaphoreType.DMA((count,)),
+            pltpu.SemaphoreType.DMA((3,)),
+        ],
+        compiler_params=pltpu.CompilerParams(collective_id=0, has_side_effects=True),
+    )(layer_input, values_first, weight_rows)
+
+
+def reduce_kernel(
+    n_seq, n_head, chunks,
+    block_ref, input_ref, first_ref, gains_ref, grads_a, grads_b,
+    block_out, input_out, first_out, gains_out, sum_a, sum_b, full_a, full_b,
+    near_a, near_b, turn_a, turn_b, far_a, far_b, gain_seq, gain_slot, gain_rank,
+    send_sems, recv_sems, own_sems,
+):
+    slots = block_ref.shape[0]
+    place = Place(n_seq, n_head, slots)
+    place.greet(True)
+    sender = Sender(send_sems, recv_sems)
+    part = sum_a.shape[1]
+    mine = lanes(place.seq, part)
+    order = [2, 3, 1, 0]
+    parts = ((grads_b, sum_b, full_b, near_b, turn_b, far_b, chunks[1]),
+             (grads_a, sum_a, full_a, near_a, turn_a, far_a, chunks[0]))
+    copies, received = [], []
+
+    def arrive(copy):
+        copy.wait_recv()
+        received.append(copy)
+
+    def swap(src, dst):
+        return [
+            sender.start(
+                src.at[place.at_slot(k)], dst.at[place.slot], place.device(slot=place.at_slot(k))
+            )
+            for k in (2, 3, 1)
+        ]
+
+    gain_seq[place.seq] = gains_ref[...]
+    small = [
+        sender.start(gain_seq.at[place.seq], gain_seq.at[place.seq],
+                     place.device(seq=place.at_seq(d)))
+        for d in range(1, n_seq)
+    ]
+    copies += small
+
+    def to_seqs(grads, near, k):
+        slot = place.at_slot(k)
+        return [
+            sender.start(
+                grads.at[slot, :, lanes(place.at_seq(d), part)],
+                near.at[k, d - 1],
+                place.device(seq=place.at_seq(d)),
+            )
+            for d in range(1, n_seq)
+        ]
+
+    sent = {}
+    units = [(which, k) for which in range(2) for k in order]
+
+    def launch(unit):
+        which, k = unit
+        sent[unit] = to_seqs(parts[which][0], parts[which][3], k)
+        copies.extend(sent[unit])
+
+    own = [
+        pltpu.make_async_copy(src.at[place.slot], dst.at[place.slot], own_sems.at[i])
+        for i, (src, dst) in enumerate(
+            ((block_ref, block_out), (input_ref, input_out), (first_ref, first_out))
+        )
+    ]
+    for copy in own:
+        copy.start()
+    launch(units[0])
+    launch(units[1])
+    copies += swap(block_ref, block_out)
+    for copy in small:
+        arrive(copy)
+    total = gain_seq[0]
+    for i in range(1, n_seq):
+        total = total + gain_seq[i]
+    gain_slot[place.slot] = total
+    small = [
+        sender.start(gain_slot.at[place.slot], gain_slot.at[place.slot],
+                     place.device(slot=place.at_slot(k)))
+        for k in range(1, slots)
+    ]
+    copies += small
+    far_copies = {0: [], 1: []}
+    for index, unit in enumerate(units):
+        which, k = unit
+        grads, _, _, near, turn, far, chunk = parts[which]
+        if index + 2 < len(units):
+            launch(units[index + 2])
+        for copy in sent[unit]:
+            arrive(copy)
+        slot = place.at_slot(k)
+
+        def add(i, carry, grads=grads, near=near, turn=turn, slot=slot, k=k, chunk=chunk):
+            rows = pl.ds(pl.multiple_of(i * chunk, chunk), chunk)
+            value = grads[slot, rows, mine].astype(F32)
+            for d in range(n_seq - 1):
+                value = value + near[k, d, rows, :].astype(F32)
+            turn[k, rows, :] = value.astype(BF16)
+            return carry
+
+        lax.fori_loop(0, grads.shape[1] // chunk, add, 0)
+        if k != 0:
+            copy = sender.start(turn.at[k], far.at[k - 1], place.device(slot=slot))
+            copies.append(copy)
+            far_copies[which].append(copy)
+        if index == 1:
+            copies += swap(first_ref, first_out)
+        if index == 4:
+            copies += swap(input_ref, input_out)
+            for copy in small:
+                arrive(copy)
+            total = gain_slot[0]
+            for i in range(1, slots):
+                total = total + gain_slot[i]
+            gain_rank[place.rank] = total
+            small = [
+                sender.start(gain_rank.at[place.rank], gain_rank.at[place.rank],
+                             place.device(rank=(place.rank + j) % place.ranks))
+                for j in range(1, place.ranks)
+            ]
+            copies += small
+        if k == 0:
+            for copy in far_copies[which]:
+                arrive(copy)
+            _, total_ref, full, _, _, _, _ = parts[which]
+
+            def finish(i, carry, turn=turn, far=far, total_ref=total_ref, full=full, chunk=chunk):
+                rows = pl.ds(pl.multiple_of(i * chunk, chunk), chunk)
+                value = turn[0, rows, :].astype(F32)
+                for j in range(slots - 1):
+                    value = value + far[j, rows, :].astype(F32)
+                value = value.astype(BF16)
+                total_ref[rows, :] = value
+                full[rows, mine] = value
+                return carry
+
+            lax.fori_loop(0, grads.shape[1] // chunk, finish, 0)
+            copies += [
+                sender.start(total_ref, full.at[:, mine], place.device(seq=place.at_seq(d)))
+                for d in range(1, n_seq)
+            ]
+    for copy in small:
+        arrive(copy)
+    total = gain_rank[0]
+    for i in range(1, place.ranks):
+        total = total + gain_rank[i]
+    gains_out[...] = total
+    for copy in copies:
+        if all(copy is not other for other in received):
+            copy.wait_recv()
+    for copy in copies:
+        copy.wait_send()
+    for copy in own:
+        copy.wait()
+
+
+def reduce_grads(n_seq, n_head, chunks, block_delta, input_delta, first_delta, gains, grads_a, grads_b):
+    slots = block_delta.shape[0]
+    part = grads_a.shape[2] // n_seq
+    rows = (grads_a.shape[1], grads_b.shape[1])
+    ranks = n_head // slots
+    count = (
+        3 * (slots - 1) + 2 * (slots * (n_seq - 1) + (slots - 1) + (n_seq - 1))
+        + (n_seq - 1) + (slots - 1) + (ranks - 1)
+    )
+    any_space = pl.BlockSpec(memory_space=pl.ANY)
+    vmem = pl.BlockSpec(memory_space=pltpu.VMEM)
+    like = lambda value: jax.ShapeDtypeStruct(value.shape, value.dtype)
+    return pl.pallas_call(
+        functools.partial(reduce_kernel, n_seq, n_head, chunks),
+        in_specs=[any_space] * 3 + [vmem] * 3,
+        out_specs=[any_space] * 3 + [vmem] * 5,
+        out_shape=[like(block_delta), like(input_delta), like(first_delta), like(gains)]
+        + [jax.ShapeDtypeStruct((r, part), BF16) for r in rows]
+        + [jax.ShapeDtypeStruct((r, part * n_seq), BF16) for r in rows],
+        scratch_shapes=[pltpu.VMEM((slots, n_seq - 1, r, part), BF16) for r in rows]
+        + [pltpu.VMEM((slots, r, part), BF16) for r in rows]
+        + [pltpu.VMEM((slots - 1, r, part), BF16) for r in rows]
+        + [pltpu.VMEM((n,) + gains.shape, F32) for n in (n_seq, slots, ranks)]
+        + [
+            pltpu.SemaphoreType.DMA((count,)),
+            pltpu.SemaphoreType.DMA((count,)),
+            pltpu.SemaphoreType.DMA((3,)),
+        ],
+        compiler_params=pltpu.CompilerParams(
+            collective_id=1, has_side_effects=True, vmem_limit_bytes=56 << 20
+        ),
+    )(block_delta, input_delta, first_delta, gains, grads_a, grads_b)
+
+
+def shampoo_kernel(
+    stat_ref, root_ref, head_stat, head_root, unit_stat, unit_root, full_a, sum_a, full_b, sum_b,
+    wide_ref, out_right_ref, new_head, new_unit, step_a, step_b,
+):
+    step = pl.program_id(0)
+    blocks = stat_ref.shape[1]
+
+    def one(member, width, small_stat, small_root, full, total, big_out, small_out, step_out):
+        for b in range(blocks):
+            rows = pl.ds(pl.multiple_of((member * blocks + b) * width, 16), width)
+            grad, own = full[rows, :], total[rows, :]
+            big_out[0, b] = STAT_DECAY * stat_ref[0, b] + (1.0 - STAT_DECAY) * dot_tn(own, grad)
+            small_out[member, b] = STAT_DECAY * small_stat[member, b] + (
+                1.0 - STAT_DECAY
+            ) * dot_nt(grad, grad)
+            turned = dot_nn(small_root[member, b].astype(BF16), grad).astype(BF16)
+            turned = dot_nt(turned, root_ref[0, b].astype(BF16))
+            scale = lax.rsqrt(jnp.mean(turned * turned, axis=0, keepdims=True) + EPSILON)
+            step_out[rows, :] = turned * scale
+
+    head_width, unit_width = head_stat.shape[2], unit_stat.shape[2]
+    head_args = (head_width, head_stat, head_root, full_a, sum_a)
+    unit_args = (unit_width, unit_stat, unit_root, full_b, sum_b)
+
+    @pl.when(step < 3)
+    def _():
+        one(step, *head_args, wide_ref, new_head, step_a)
+
+    @pl.when((step >= 3) & (step < 6))
+    def _():
+        one(step - 3, *unit_args, wide_ref, new_unit, step_b)
+
+    @pl.when(step == 6)
+    def _():
+        one(3, *head_args, out_right_ref, new_head, step_a)
+
+
+def shampoo(stats_wide, roots_wide, stats_head, roots_head, stats_unit, roots_unit, full_a, sum_a, full_b, sum_b):
+    members, blocks, part, width = stats_wide.shape
+    member = lambda i: (jnp.where(i == 5, 6, jnp.where(i == 6, 5, i)), 0, 0, 0)
+    wide = pl.BlockSpec((1, blocks, part, width), member)
+    vmem = pl.BlockSpec(memory_space=pltpu.VMEM)
+    return pl.pallas_call(
+        shampoo_kernel,
+        grid=(members,),
+        in_specs=[wide, wide] + [vmem] * 8,
+        out_specs=[
+            pl.BlockSpec((1, blocks, part, width), lambda i: (jnp.minimum(i, 5), 0, 0, 0)),
+            pl.BlockSpec((1, blocks, part, width), lambda i: (0, 0, 0, 0)),
+            vmem, vmem, vmem, vmem,
+        ],
+        out_shape=[
+            jax.ShapeDtypeStruct((members - 1, blocks, part, width), F32),
+            jax.ShapeDtypeStruct((1, blocks, part, width), F32),
+            jax.ShapeDtypeStruct(stats_head.shape, F32),
+            jax.ShapeDtypeStruct(stats_unit.shape, F32),
+            jax.ShapeDtypeStruct(sum_a.shape, F32),
+            jax.ShapeDtypeStruct(sum_b.shape, F32),
+        ],
+        compiler_params=pltpu.CompilerParams(vmem_limit_bytes=48 << 20),
+    )(stats_wide, roots_wide, stats_head, roots_head, stats_unit, roots_unit, full_a, sum_a, full_b, sum_b)
+
+
 class Links:
     def __init__(self, n_seq, n_head, slots):
         self.n_seq, self.n_head, self.slots = n_seq, n_head, slots
         self.ranks = n_head // slots
         self.slot = lax.axis_index("head") // self.ranks
         self.rank = lax.axis_index("head") % self.ranks
-        self.alike = [
-            [s * n_head + q * self.ranks + r for s in range(n_seq) for q in range(slots)]
-            for r in range(self.ranks)
-        ]
 
     def permute(self, value, partner):
         pairs = []
@@ -232,14 +631,6 @@
             total = total + got.astype(F32)
         return total
 
-    def gather_alike(self, value):
-        out = lax.all_gather(value, AXES, axis=0, axis_index_groups=self.alike)
-        return out.reshape((self.n_seq, self.slots) + value.shape)
-
-    def sum_alike(self, value):
-        flat = value.reshape((self.n_seq * self.slots,) + value.shape[2:])
-        return lax.psum_scatter(flat, AXES, scatter_dimension=0, axis_index_groups=self.alike)
-
     def whole_sequence(self, own):
         both = self.gather_ranks(own)
         return jnp.swapaxes(both, 0, 1).reshape(-1, own.shape[-1])
@@ -248,42 +639,6 @@
         rows = full.shape[0] // (self.slots * self.ranks)
         parts = full.reshape(self.slots, self.ranks, rows, full.shape[-1])
         return self.sum_ranks(jnp.swapaxes(parts, 0, 1)).reshape(-1, full.shape[-1])
-
-
-def left_update(weight_rows, grad, row_begin, big_stat, big_root, small_stat, small_root, width):
-    members, row_part, columns = weight_rows.shape
-    model_width = grad.shape[1]
-    blocks = columns // width
-    grad_blocks = grad.reshape(members, model_width, blocks, width)
-    grad_rows = lax.dynamic_slice_in_dim(grad_blocks, row_begin, row_part, 1)
-    ein = functools.partial(jnp.einsum, preferred_element_type=F32)
-    big_new = STAT_DECAY * big_stat + (1.0 - STAT_DECAY) * ein(
-        "nrbk,nsbk->nbrs", grad_rows, grad_blocks
-    )
-    small_new = STAT_DECAY * small_stat + (1.0 - STAT_DECAY) * ein(
-        "nrbk,nrbl->nbkl", grad_blocks, grad_blocks
-    )
-    step_dir = ein("nbrs,nsbk->nrbk", big_root.astype(BF16), grad_blocks)
-    step_dir = ein("nrbk,nbkl->nrbl", step_dir.astype(BF16), small_root.astype(BF16))
-    step_dir = step_dir * lax.rsqrt(jnp.mean(step_dir * step_dir, axis=-1, keepdims=True) + EPSILON)
-    return weight_rows - STEP_RATE * step_dir.reshape(members, row_part, columns), big_new, small_new
-
-
-def right_update(weight_cols, grad, col_begin, big_stat, big_root, small_stat, small_root, width, rate):
-    rows_all, col_part = weight_cols.shape
-    model_width = grad.shape[1]
-    blocks = rows_all // width
-    grad_blocks = grad.reshape(blocks, width, model_width)
-    grad_cols = lax.dynamic_slice_in_dim(grad_blocks, col_begin, col_part, 2)
-    ein = functools.partial(jnp.einsum, preferred_element_type=F32)
-    big_new = STAT_DECAY * big_stat + (1.0 - STAT_DECAY) * ein("bkr,bks->brs", grad_cols, grad_blocks)
-    small_new = STAT_DECAY * small_stat + (1.0 - STAT_DECAY) * ein(
-        "bkr,blr->bkl", grad_blocks, grad_blocks
-    )
-    step_dir = ein("bkl,bls->bks", small_root.astype(BF16), grad_blocks)
-    step_dir = ein("bks,brs->bkr", step_dir.astype(BF16), big_root.astype(BF16))
-    step_dir = step_dir * lax.rsqrt(jnp.mean(step_dir * step_dir, axis=1, keepdims=True) + EPSILON)
-    return weight_cols - rate * step_dir.reshape(rows_all, col_part), big_new, small_new
 
 
 def shards(
@@ -309,40 +664,39 @@
     slots, rows, width = layer_input.shape
     length = segments.shape[1]
     row_part, head_cols, ffn_cols = w_qkv.shape[1], w_qkv.shape[2], w_gate_up.shape[2]
-    head_dim, unit_block = stats_head.shape[2], stats_unit.shape[2]
+    head_dim = stats_head.shape[2]
     links = Links(n_seq, n_head, slots)
-    row_begin = lax.axis_index("seq") * row_part
     is_live = links.slot < counts[0]
-    my_heads = slots * head_cols
-    pairs = my_heads // LANES
+    pairs = slots * head_cols // LANES
+    per = LANES // head_cols
+    rows_a, rows_b = 4 * head_cols, 3 * ffn_cols
 
     def pair_major(value):
-        if head_cols == LANES:
-            return value
-        per = LANES // head_cols
-        value = value.reshape(pairs, per, length, head_cols)
-        return jnp.swapaxes(value, 1, 2).reshape(pairs, length, LANES)
+        n = value.shape[2]
+        value = value.reshape(pairs, per, length, n, head_cols)
+        return value.transpose(0, 2, 3, 1, 4).reshape(pairs, length, n, LANES)
 
     def slot_major(value):
-        if head_cols == LANES:
-            return value
-        per = LANES // head_cols
-        value = value.reshape(pairs, length, per, head_cols)
-        return jnp.swapaxes(value, 1, 2).reshape(slots, length, head_cols)
-
-    qkv_all = links.gather_alike(w_qkv.astype(BF16))
-    x_own = links.swap_slots(layer_input).reshape(slots * rows, width).astype(F32)
-    first_all = pair_major(links.swap_slots(values_first))
-    out_all = links.gather_alike(w_out.astype(BF16))
-    gate_up_all = links.gather_alike(w_gate_up.astype(BF16))
-    down_all = links.gather_alike(w_down.astype(BF16))
-    per = LANES // head_cols
-    qkv_w = qkv_all.reshape(n_seq, pairs, per, 3, row_part, head_cols)
-    qkv_w = qkv_w.transpose(1, 0, 4, 3, 2, 5).reshape(pairs, width, 3 * LANES)
-    out_w = out_all.transpose(1, 2, 0, 3).reshape(my_heads, width)
-    gate_up_w = gate_up_all.transpose(0, 3, 2, 1, 4).reshape(width, 2 * slots * ffn_cols)
-    down_w = down_all.transpose(1, 2, 0, 3).reshape(slots * ffn_cols, width)
-    units = slots * ffn_cols
+        n = value.shape[2]
+        value = value.reshape(pairs, length, n, per, head_cols)
+        return value.transpose(0, 3, 1, 2, 4).reshape(slots, length, n, head_cols)
+
+    weight_rows = jnp.concatenate(
+        [
+            jnp.swapaxes(w_qkv.astype(BF16), 1, 2).reshape(3 * head_cols, row_part),
+            w_out.astype(BF16),
+            jnp.swapaxes(w_gate_up.astype(BF16), 1, 2).reshape(2 * ffn_cols, row_part),
+            w_down.astype(BF16),
+        ],
+        axis=0,
+    )
+    x_bf16, first_all, weights = gather_inputs(
+        n_seq, n_head, ((0, rows_a), (rows_a, rows_b)), layer_input, values_first, weight_rows
+    )
+    w_in, w_o = weights[:, : 3 * head_cols], weights[:, 3 * head_cols : rows_a]
+    w_gu, w_d = weights[:, rows_a : rows_a + 2 * ffn_cols], weights[:, rows_a + 2 * ffn_cols :]
+    x_own = x_bf16.reshape(slots * rows, width).astype(F32)
+    ein = functools.partial(jnp.einsum, preferred_element_type=F32)
 
     segment_ids = lax.dynamic_index_in_dim(segments, links.slot, 0, keepdims=False)
     first_pos, cos_wide, sin_wide = position_tables(segment_ids, head_dim)
@@ -352,128 +706,117 @@
     h_one = links.whole_sequence(
         (normed_one * norm_gains[0]).astype(BF16).reshape(slots, rows, width)
     )
-    project = jnp.einsum("ld,pdc->plc", h_one, qkv_w, preferred_element_type=F32)
+    project = ein("ld,qcd->qlc", h_one, w_in)
+    if per > 1:
+        project = pair_major(project.reshape(slots, length, 3, head_cols)).reshape(
+            pairs, length, 3 * LANES
+        )
+        first_all = pair_major(first_all[:, :, None])[:, :, 0]
     saved = attend(project, first_all, cos_wide, sin_wide, first_pos)
-    attended = jnp.swapaxes(saved[3], 0, 1).reshape(length, my_heads)
-    attn_out = links.own_sum(dot_nn(attended, out_w))
+    attended = saved[3]
+    if per > 1:
+        attended = slot_major(attended[:, :, None])[:, :, 0]
+    attn_out = links.own_sum(ein("qlc,qcd->ld", attended, w_o))
     middle = x_own + attn_out
     inverse_two = lax.rsqrt(jnp.mean(middle * middle, axis=-1, keepdims=True) + EPSILON)
     normed_two = middle * inverse_two
     h_two = links.whole_sequence(
         (normed_two * norm_gains[1]).astype(BF16).reshape(slots, rows, width)
     )
-    gate_up = dot_nn(h_two, gate_up_w)
-    gate, up = gate_up[:, :units], gate_up[:, units:]
+    gate_up = ein("ld,qfd->qlf", h_two, w_gu)
+    gate, up = gate_up[..., :ffn_cols], gate_up[..., ffn_cols:]
     sigmoid_gate = jax.nn.sigmoid(gate)
     activated = gate * sigmoid_gate
     hidden = (activated * up).astype(BF16)
-    ffn_out = links.own_sum(dot_nn(hidden, down_w))
+    ffn_out = links.own_sum(ein("qlf,qfd->ld", hidden, w_d))
     block_delta = jnp.where(is_live, attn_out + ffn_out, 0.0).astype(BF16)
-    block_out = layer_input.astype(F32) + links.swap_slots(
-        block_delta.reshape(slots, rows, width)
-    ).astype(F32)
 
     grad_own = links.swap_slots(out_grad)
     d_own = jnp.where(is_live, grad_own, jnp.zeros_like(grad_own))
     d_out = d_own.reshape(slots * rows, width).astype(F32)
     d_ffn = links.whole_sequence(d_own)
-    g_down = dot_tn(hidden, d_ffn)
-    sum_down = links.sum_alike(
-        g_down.astype(BF16).reshape(slots, ffn_cols, n_seq, row_part).transpose(2, 0, 1, 3)
-    )
-    d_hidden = dot_nt(d_ffn, down_w)
+    g_down = ein("qlf,ld->qfd", hidden, d_ffn)
+    d_hidden = ein("ld,qfd->qlf", d_ffn, w_d)
     d_gate = (
         d_hidden * up * sigmoid_gate * (1.0 + gate * (1.0 - sigmoid_gate))
     ).astype(BF16)
     d_up = (d_hidden * activated).astype(BF16)
-    d_gate_up = jnp.concatenate([d_gate, d_up], axis=1)
-    d_normed_two = links.own_sum(dot_nt(d_gate_up, gate_up_w))
-    g_gate_up = dot_tn(h_two, d_gate_up)
-    sum_gate_up = links.sum_alike(
-        g_gate_up.astype(BF16)
-        .reshape(n_seq, row_part, 2, slots, ffn_cols)
-        .transpose(0, 3, 2, 1, 4)
-    )
+    d_gate_up = jnp.concatenate([d_gate, d_up], axis=2)
+    d_normed_two = links.own_sum(ein("qlf,qfd->ld", d_gate_up, w_gu))
+    g_gate_up = ein("qlf,ld->qfd", d_gate_up, h_two)
+    grads_b = jnp.concatenate([g_gate_up.astype(BF16), g_down.astype(BF16)], axis=1)
     gain_two = jnp.sum(normed_two * d_normed_two, axis=0)
     middle_delta = norm_back(d_normed_two * norm_gains[1], normed_two, inverse_two)
     d_middle = d_out + middle_delta
     d_attn = links.whole_sequence(d_middle.astype(BF16).reshape(slots, rows, width))
-    d_attended = dot_nt(d_attn, out_w).astype(BF16)
-    d_query, d_key, d_value = attend_back(
-        saved,
-        jnp.swapaxes(d_attended.reshape(length, pairs, LANES), 0, 1),
-        cos_wide,
-        sin_wide,
-        first_pos,
-    )
-    first_grad = links.swap_slots(slot_major(d_value)).astype(F32)
-    g_out = dot_tn(attended, d_attn)
-    sum_out = links.sum_alike(
-        g_out.astype(BF16).reshape(slots, head_cols, n_seq, row_part).transpose(2, 0, 1, 3)
-    )
-    d_project = jnp.concatenate([d_query, d_key, d_value], axis=2)
-    g_qkv = jnp.einsum("ld,plc->pdc", h_one, d_project, preferred_element_type=F32)
-    sum_qkv = links.sum_alike(
-        g_qkv.astype(BF16)
-        .reshape(pairs, n_seq, row_part, 3, per, head_cols)
-        .transpose(1, 0, 4, 3, 2, 5)
-        .reshape(n_seq, slots, 3, row_part, head_cols)
-    )
-    d_normed_one = links.own_sum(
-        jnp.einsum("plc,pdc->ld", d_project, qkv_w, preferred_element_type=F32)
-    )
+    d_attended = ein("ld,qcd->qlc", d_attn, w_o).astype(BF16)
+    if per > 1:
+        d_attended = pair_major(d_attended[:, :, None])[:, :, 0]
+    d_project = jnp.concatenate(
+        attend_back(saved, d_attended, cos_wide, sin_wide, first_pos), axis=2
+    )
+    if per > 1:
+        d_project = slot_major(d_project.reshape(pairs, length, 3, LANES)).reshape(
+            slots, length, 3 * head_cols
+        )
+    d_value = d_project[:, :, 2 * head_cols :]
+    g_out = ein("qlc,ld->qcd", attended, d_attn)
+    g_qkv = ein("qlc,ld->qcd", d_project, h_one)
+    grads_a = jnp.concatenate([g_qkv.astype(BF16), g_out.astype(BF16)], axis=1)
+    d_normed_one = links.own_sum(ein("qlc,qcd->ld", d_project, w_in))
     gain_one = jnp.sum(normed_one * d_normed_one, axis=0)
     input_delta = middle_delta + norm_back(d_normed_one * norm_gains[0], normed_one, inverse_one)
     input_delta = jnp.where(is_live, input_delta, 0.0).astype(BF16)
-    input_grad = out_grad.astype(F32) + links.swap_slots(
-        input_delta.reshape(slots, rows, width)
-    ).astype(F32)
-
-    grad_gains = lax.psum(jnp.stack([gain_one, gain_two]), AXES)
+    gains = jnp.concatenate([gain_one.reshape(8, -1), gain_two.reshape(8, -1)], axis=0)
+
+    block_got, input_got, first_got, gains, sum_a, sum_b, full_a, full_b = reduce_grads(
+        n_seq,
+        n_head,
+        (LANES, unit_chunk(rows_b)),
+        block_delta.reshape(slots, rows, width),
+        input_delta.reshape(slots, rows, width),
+        d_value,
+        gains,
+        grads_a,
+        grads_b,
+    )
+    block_out = layer_input.astype(F32) + block_got.astype(F32)
+    input_grad = out_grad.astype(F32) + input_got.astype(F32)
+    first_grad = first_got.astype(F32)
+    grad_gains = gains.reshape(2, width)
     new_gains = norm_gains - GAIN_RATE * grad_gains * lax.rsqrt(
         jnp.mean(grad_gains * grad_gains, axis=-1, keepdims=True) + EPSILON
     )
 
-    full_down = lax.all_gather(sum_down, "seq", axis=1, tiled=True)
-    full_gate_up = lax.all_gather(sum_gate_up, "seq", axis=1, tiled=True)
-    full_out = lax.all_gather(sum_out, "seq", axis=1, tiled=True)
-    full_qkv = lax.all_gather(sum_qkv, "seq", axis=1, tiled=True)
-
-    new_down, wide_down, unit_down = right_update(
-        w_down, full_down, row_begin, stats_wide[6], roots_wide[6], stats_unit[2], roots_unit[2],
-        unit_block, STEP_RATE,
-    )
-    new_gate_up, wide_gu, unit_gu = left_update(
-        w_gate_up, full_gate_up, row_begin, stats_wide[3:5], roots_wide[3:5], stats_unit[0:2],
-        roots_unit[0:2], unit_block,
-    )
-    new_out, wide_out, head_out = right_update(
-        w_out, full_out, row_begin, stats_wide[5], roots_wide[5], stats_head[3], roots_head[3],
-        head_dim, OUT_RATE,
-    )
-    new_qkv, wide_qkv, head_qkv = left_update(
-        w_qkv, full_qkv, row_begin, stats_wide[0:3], roots_wide[0:3], stats_head[0:3],
-        roots_head[0:3], head_dim,
-    )
+    wide, out_right, new_head, new_unit, step_a, step_b = shampoo(
+        stats_wide, roots_wide, stats_head, roots_head, stats_unit, roots_unit,
+        full_a, sum_a, full_b, sum_b,
+    )
+    cut = 3 * head_cols
+    turned = lambda value, n: jnp.swapaxes(value.reshape(n, -1, row_part), 1, 2)
     return (
         block_out,
         input_grad,
         first_grad,
-        sum_qkv.astype(F32),
-        sum_gate_up.astype(F32),
-        sum_out.astype(F32),
-        sum_down.astype(F32),
+        turned(sum_a[:cut], 3).astype(F32),
+        turned(sum_b[: 2 * ffn_cols], 2).astype(F32),
+        sum_a[cut:].astype(F32),
+        sum_b[2 * ffn_cols :].astype(F32),
         grad_gains,
-        new_qkv,
-        new_gate_up,
-        new_out,
-        new_down,
+        w_qkv - STEP_RATE * turned(step_a[:cut], 3),
+        w_gate_up - STEP_RATE * turned(step_b[: 2 * ffn_cols], 2),
+        w_out - OUT_RATE * step_a[cut:],
+        w_down - STEP_RATE * step_b[2 * ffn_cols :],
         new_gains,
-        jnp.concatenate([wide_qkv, wide_gu, wide_down[None]], axis=0),
-        wide_out,
-        jnp.concatenate([head_qkv, head_out[None]], axis=0),
-        jnp.concatenate([unit_gu, unit_down[None]], axis=0),
-    )
+        wide,
+        out_right[0],
+        new_head,
+        new_unit,
+    )
+
+
+def unit_chunk(rows):
+    return max(c for c in range(16, 177, 16) if rows % c == 0)
 
 
 def solution(mesh):

time: 901 us -> 597 us (0.66)
  waiting for transfers between devices: 399 us -> 17.3 us
  Pallas kernels: 33 us -> 407 us
  local copies, waits for them, and re-layouts: 130 us -> 20.4 us
  blocking collectives: 87.3 us -> 0 us
  other arithmetic: 79.5 us -> 47.1 us
  matrix products: 108 us -> 76.2 us
  starting transfers between devices: 42.3 us -> 21.1 us
  between operations: 16 us -> 2.22 us
    pallas_call x0 -> x3, Pallas kernels: none -> 374 us  [the longest x1 189 us: reduce_grads(): pl.pallas_call(functools.partial(reduce_kernel, n_seq, n_head, chunks), i...]
    all_gather x5 -> x0, waiting for transfers between devices: 153 us -> none  [the longest x4 142 us: gather_alike(): out = lax.all_gather(value, AXES, axis=0, axis_index_groups=self.alike)]
    reduce_scatter x4 -> x0, waiting for transfers between devices: 131 us -> none  [sum_alike(): lax.psum_scatter(flat, AXES, scatter_dimension=0, axis_index_groups=self....]
    ppermute x26 -> x11, waiting for transfers between devices: 115 us -> 17.3 us  [permute(): return lax.ppermute(value, AXES, pairs)]
    reshape x11 -> x1, local copies, waits for them, and re-layouts: 57.5 us -> 0.71 us  [shards(): grad_gains = gains.reshape(2, width)]
    psum x1 -> x0, blocking collectives: 46.5 us -> none  [shards(): grad_gains = lax.psum(jnp.stack([gain_one, gain_two]), AXES)]
    all_gather x3 -> x0, blocking collectives: 40.8 us -> none  [the longest x1 15.2 us: shards(): full_down = lax.all_gather(sum_down, 'seq', axis=1, tiled=True)]
    dot_general x24 -> x12, matrix products: 108 us -> 76.2 us  [the longest x1 12.4 us: shards(): gate_up = ein('ld,qfd->qlf', h_two, w_gu)]
  transfers between devices with their start and end apart: 35 -> 11, of which waited for: 17 -> 3; matrix products, arithmetic and copies ran while one was open for 25% -> 7% of each run, Pallas kernels for 4% -> 0%
where the time goes in v2:
time: 597 us; the launch traced here: 591 us
  Pallas kernels  407 us (68%)
  matrix products  76.2 us (13%)
  other arithmetic  47.1 us (8%)
  starting transfers between devices  21.1 us (4%)
  local copies, waits for them, and re-layouts  20.4 us (3%)
  waiting for transfers between devices  17.3 us (3%)
    pallas_call x1, Pallas kernels, reduce_grads(): pl.pallas_call(functools.partial(reduce_kernel, n_seq, n_head, chunks), i...  189 us
    pallas_call x1, Pallas kernels, gather_inputs(): pl.pallas_call(functools.partial(gather_kernel, n_seq, n_head, sections),...  164 us
    ppermute x11, starting transfers between devices, permute(): return lax.ppermute(value, AXES, pairs)  21.1 us
    pallas_call x1, Pallas kernels, shampoo(): pl.pallas_call(shampoo_kernel, grid=(members,), in_specs=[wide, wide] + [...  20.8 us
    pallas_call x1, Pallas kernels, attend_back(): pl.pallas_call(attend_back_kernel, grid=(pairs,), in_specs=[part] * 5 + [...  17.5 us
    ppermute x11, waiting for transfers between devices, permute(): return lax.ppermute(value, AXES, pairs)  17.3 us
    pallas_call x1, Pallas kernels, attend(): pl.pallas_call(attend_kernel, grid=(pairs,), in_specs=[part(0), part(1),...  15.6 us
    dot_general x1, matrix products, shards(): gate_up = ein('ld,qfd->qlf', h_two, w_gu)  12.4 us
  transfers between devices with their start and end apart: 11, of which 3 were waited for; matrix products, arithmetic and copies ran while one was open for 7% of the time, Pallas kernels for 0%

profile of v2, /device:TPU:0, one launch (start us, length us, event | category | flops | bytes accessed | tf_op | source)
XLA Modules:
  0.0 591.2 jit_solution(11305746216838183293)
XLA Ops:
  5.6 164.1 %shard_map.287 = (bf16[4,128,1024]{2,1,0:T(8,128)(2,1)}, bf16[4,1024,128]{2,1,0:T(8,128)(2,1)}, bf16[4,1568,1024]{2,1,0:T(8,128)(2,1)}) custom-call(bf16[4,128,1024]{2,1,0:T(8,128)(2,1)} %x_ref.1, bf16[4,1024,128]{2,1,0:T(8,128)(2,1)} %vf_ref.1, bf16[1568,256]{1,0:T(8,128)(2,1)} %pad_maximum_fusion.8.wt_ref), custom_call_target="tpu_custom_call" | custom-call | tf_op jit(solution)/shard_map/pallas_call | solution.py:323
  178.0 8.0 %fusion.22.q_ref.k_ref.v_ref = f32[4,1024,384]{2,1,0:T(8,128)} fusion(bf16[1024,1024,1]{1,0,2:T(8,128)(2,1)S(1)} %bitcast.199, bf16[4,1568,1024]{2,1,0:T(8,128)(2,1)} %get-tuple-element.42), kind=kOutput, calls=%fused_computation.30 | convolution fusion | flops 3221225472 | bytes 11534336 | tf_op jit(solution)/shard_map/ld,qcd->qlc/dot_general | solution.py:709
  186.0 15.6 %shard_map.288 = (bf16[4,1024,128]{2,1,0:T(8,128)(2,1)S(1)}, bf16[4,1024,128]{2,1,0:T(8,128)(2,1)S(1)}, bf16[4,1024,128]{2,1,0:T(8,128)(2,1)S(1)}, bf16[4,1024,128]{2,1,0:T(8,128)(2,1)S(1)}, f32[4,2,1024]{2,1,0:T(2,128)S(1)}) custom-call(f32[4,1024,384]{2,1,0:T(8,128)} %fusion.22.q_ref.k_ref.v_ref, f32[4,1024,384]{2,1,0:T(8,128)} %fusion.22.q_ref.k_ref.v_ref, ...), custom_call_target="tpu_custom_call" | custom-call | flops 4294967296 | bytes 12582912 | tf_op jit(solution)/shard_map/pallas_call | solution.py:155
  201.6 3.3 fusion.55
  209.4 18.1 %collective-permute-start.5 = (bf16[128,1024]{1,0:T(8,128)(2,1)}, bf16[128,1024]{1,0:T(8,128)(2,1)S(1)}, u32[]{:S(2)}, u32[]{:S(2)}) collective-permute-start(bf16[128,1024]{1,0:T(8,128)(2,1)} %get-tuple-element.91), channel_id=1, source_target_pairs={{0,4},{1,5},{2,6},{3,7},{4,0},{5,1},{6,2},{7,3},{8,12},{9,13},{10,... | collective-permute-start | bytes 786440 | tf_op jit(solution)/shard_map/ppermute | solution.py:605
  229.6 5.3 collective-permute-done.5
  234.9 10.9 %collective-permute-done.4 = bf16[128,1024]{1,0:T(8,128)(2,1)S(1)} collective-permute-done((bf16[128,1024]{1,0:T(8,128)(2,1)}, bf16[128,1024]{1,0:T(8,128)(2,1)S(1)}, u32[]{:S(2)}, u32[]{:S(2)}) %collective-permute-start.4) | collective-permute-done | bytes 262176 | tf_op jit(solution)/shard_map/ppermute | solution.py:605
  254.3 12.4 %fusion.9 = f32[4,1024,704]{1,2,0:T(8,128)} fusion(bf16[1024,1024,1]{1,0,2:T(8,128)(2,1)S(1)} %bitcast.205, bf16[4,1568,1024]{2,1,0:T(8,128)(2,1)} %get-tuple-element.42), kind=kOutput, calls=%fused_computation.16 | convolution fusion | flops 5905580032 | bytes 19398656 | tf_op jit(solution)/shard_map/ld,qfd->qlf/dot_general | solution.py:726
  266.7 11.4 %fusion.2 = (bf16[4,1024,352]{1,2,0:T(8,128)(2,1)}, bf16[4,1024,352]{1,2,0:T(8,128)(2,1)}, bf16[4,1024,352]{1,2,0:T(8,128)(2,1)S(1)}) fusion(f32[4,1024,704]{1,2,0:T(8,128)} %fusion.9, bf16[1024,1024,1]{1,0,2:T(8,128)(2,1)S(1)} %bitcast.203, bf16[4,1568,1024]{2,1,0:T(8,128)(2,1)} %get-tuple-element.42), kind=kOutput, calls=%fused_computation.6 | convolution fusion | flops 2974416896 | bytes 25165824 | tf_op jit(solution)/shard_map/ld,qfd->qlf/dot_general | solution.py:739
  278.0 3.4 convolution_convert_fusion.1
  281.4 5.5 fusion.27
  289.2 8.5 %fusion.5 = f32[1024,1024,1]{1,0,2:T(8,128)S(1)} fusion(bf16[4,1568,1024]{2,1,0:T(8,128)(2,1)} %get-tuple-element.42, bf16[4,1024,352]{1,2,0:T(8,128)(2,1)S(1)} %copy-done.39, bf16[4,1024,352]{1,2,0:T(8,128)(2,1)S(1)} %copy-done.38), kind=kOutput, calls=%fused_computation.11 | convolution fusion | flops 5917114368 | bytes 15728640 | tf_op jit(solution)/shard_map/qlf,qfd->ld/dot_general | solution.py:745
  299.3 9.1 %fusion.13 = bf16[4,704,1024]{2,1,0:T(8,128)(2,1)S(1)} fusion(bf16[1024,1024,1]{1,0,2:T(8,128)(2,1)S(1)} %bitcast.206, bf16[4,1024,352]{1,2,0:T(8,128)(2,1)} %get-tuple-element.76, bf16[4,1024,352]{1,2,0:T(8,128)(2,1)} %get-tuple-element.75), kind=kOutput, calls=%fused_computation.18 | convolution fusion | flops 5919997952 | bytes 13631488 | tf_op jit(solution)/shard_map/qlf,ld->qfd/dot_general | solution.py:746
  310.1 4.0 pad_maximum_fusion.grads_b
  314.1 3.2 fusion.40.block_ref
  318.5 4.3 fusion.41.d_ref
  322.8 17.5 %shard_map.289 = (bf16[4,1024,128]{2,1,0:T(8,128)(2,1)S(1)}, bf16[4,1024,128]{2,1,0:T(8,128)(2,1)S(1)}, bf16[4,1024,128]{2,1,0:T(8,128)(2,1)S(1)}) custom-call(bf16[4,1024,128]{2,1,0:T(8,128)(2,1)S(1)} %get-tuple-element.46.qr_ref, bf16[4,1024,128]{2,1,0:T(8,128)(2,1)} %copy-done.10, bf16[4,1024,128]{2,1,0:T(8,128)(2,1)} %copy-done.11, ...), custom_call_target="tpu_custom_call" | custom-call | flops 10737418240 | bytes 12582912 | tf_op jit(solution)/shard_map/pallas_call | solution.py:175
  341.5 5.4 fusion.18
  349.5 3.7 convolution_convert_fusion
  353.2 2.4 pad_maximum_fusion.2.grads_a
  357.0 2.2 fusion.35.input_ref
  359.2 188.7 %shard_map.290 = (bf16[4,128,1024]{2,1,0:T(8,128)(2,1)}, bf16[4,128,1024]{2,1,0:T(8,128)(2,1)}, bf16[4,1024,128]{2,1,0:T(8,128)(2,1)}, f32[16,128]{1,0:T(8,128)}...) custom-call(bf16[4,128,1024]{2,1,0:T(8,128)(2,1)} %fusion.40.block_r, ...), custom_call_target="tpu_custom_call" | custom-call | tf_op jit(solution)/shard_map/pallas_call | solution.py:507
  557.7 20.8 %shard_map.291 = (f32[6,2,256,1024]{3,2,1,0:T(8,128)}, f32[1,2,256,1024]{3,2,1,0:T(8,128)}, f32[4,2,64,64]{3,2,1,0:T(8,128)}, f32[3,2,176,176]{3,2,1,0:T(8,128)}...) custom-call(f32[7,2,256,1024]{3,2,1,0:T(8,128)} %stat_ref.1, f32[7,2,256,1024]{3,2,1,0:T(8,128)} %root_ref.1, ...), custom_call_target="tpu_custom_call" | custom-call | tf_op jit(solution)/shard_map/pallas_call | solution.py:571
  582.1 3.1 convert_add_fusion.2
  (176 shorter events, 58.2 us)
Async XLA Ops:
  172.8 4.0 collective-permute-start
  178.0 8.1 %copy-start.23 = (bf16[4,2,128,1024]{3,2,1,0:T(8,128)(2,1)}, bf16[4,2,128,1024]{3,2,1,0:T(8,128)(2,1)S(1)}, u32[]{:S(2)}) copy-start(bf16[4,2,128,1024]{3,2,1,0:T(8,128)(2,1)S(1)} %copy.56) | copy-start | bytes 6291460
  208.1 38.3 %collective-permute-start.1 = (bf16[4,128,1024]{2,1,0:T(8,128)(2,1)}, bf16[4,128,1024]{2,1,0:T(8,128)(2,1)}, u32[]{:S(2)}, u32[]{:S(2)}) collective-permute-start(bf16[4,128,1024]{2,1,0:T(8,128)(2,1)} %fusion.42), channel_id=1, source_target_pairs={{0,1},{1,0},{2,3},{3,2},{4,5},{5,4},{6,7},{7,6},{8,9},{9,8},{10,11... | collective-permute-start | bytes 3145736 | tf_op jit(solution)/shard_map/ppermute | solution.py:605
  209.4 25.5 %collective-permute-start.5 = (bf16[128,1024]{1,0:T(8,128)(2,1)}, bf16[128,1024]{1,0:T(8,128)(2,1)S(1)}, u32[]{:S(2)}, u32[]{:S(2)}) collective-permute-start(bf16[128,1024]{1,0:T(8,128)(2,1)} %get-tuple-element.91), channel_id=1, source_target_pairs={{0,4},{1,5},{2,6},{3,7},{4,0},{5,1},{6,2},{7,3},{8,12},{9,13},{10,... | collective-permute-start | bytes 786440 | tf_op jit(solution)/shard_map/ppermute | solution.py:605
  227.5 18.4 %collective-permute-start.4 = (bf16[128,1024]{1,0:T(8,128)(2,1)}, bf16[128,1024]{1,0:T(8,128)(2,1)S(1)}, u32[]{:S(2)}, u32[]{:S(2)}) collective-permute-start(bf16[128,1024]{1,0:T(8,128)(2,1)} %get-tuple-element.92), channel_id=1, source_target_pairs={{0,2},{1,3},{2,0},{3,1},{4,6},{5,7},{6,4},{7,5},{8,10},{9,11},{10,... | collective-permute-start | bytes 786440 | tf_op jit(solution)/shard_map/ppermute | solution.py:605
  227.5 18.4 %collective-permute-start.6 = (bf16[128,1024]{1,0:T(8,128)(2,1)}, bf16[128,1024]{1,0:T(8,128)(2,1)S(1)}, u32[]{:S(2)}, u32[]{:S(2)}) collective-permute-start(bf16[128,1024]{1,0:T(8,128)(2,1)} %get-tuple-element.93), channel_id=1, source_target_pairs={{0,6},{1,7},{2,4},{3,5},{4,2},{5,3},{6,0},{7,1},{8,14},{9,15},{10,... | collective-permute-start | bytes 786440 | tf_op jit(solution)/shard_map/ppermute | solution.py:605
  246.3 4.4 collective-permute-start.7
  250.4 2.7 collective-permute-start.2
  254.2 12.4 %copy-start.27 = (bf16[4,2,128,1024]{3,2,1,0:T(8,128)(2,1)}, bf16[4,2,128,1024]{3,2,1,0:T(8,128)(2,1)S(1)}, u32[]{:S(2)}) copy-start(bf16[4,2,128,1024]{3,2,1,0:T(8,128)(2,1)S(1)} %copy.60) | copy-start | bytes 6291460
  281.4 7.8 %copy-start.38 = (bf16[4,1024,352]{1,2,0:T(8,128)(2,1)S(1)}, bf16[4,1024,352]{1,2,0:T(8,128)(2,1)}, u32[]{:S(2)}) copy-start(bf16[4,1024,352]{1,2,0:T(8,128)(2,1)} %get-tuple-element.75) | copy-start | bytes 8650756
  281.4 7.8 %copy-start.39 = (bf16[4,1024,352]{1,2,0:T(8,128)(2,1)S(1)}, bf16[4,1024,352]{1,2,0:T(8,128)(2,1)}, u32[]{:S(2)}) copy-start(bf16[4,1024,352]{1,2,0:T(8,128)(2,1)} %get-tuple-element.76) | copy-start | bytes 8650756
  288.2 25.9 %collective-permute-start.3 = (bf16[4,128,1024]{2,1,0:T(8,128)(2,1)}, bf16[4,128,1024]{2,1,0:T(8,128)(2,1)}, u32[]{:S(2)}, u32[]{:S(2)}) collective-permute-start(bf16[4,128,1024]{2,1,0:T(8,128)(2,1)} %fusion.44), channel_id=1, source_target_pairs={{0,1},{1,0},{2,3},{3,2},{4,5},{5,4},{6,7},{7,6},{8,9},{9,8},{10,11... | collective-permute-start | bytes 3145736 | tf_op jit(solution)/shard_map/ppermute | solution.py:605
  297.9 10.5 %collective-permute-start.8 = (bf16[4,128,1024]{2,1,0:T(8,128)(2,1)S(1)}, bf16[4,128,1024]{2,1,0:T(8,128)(2,1)S(1)}, u32[]{:S(2)}, u32[]{:S(2)}) collective-permute-start(bf16[4,128,1024]{2,1,0:T(8,128)(2,1)S(1)} %fusion.43), channel_id=1, source_target_pairs={{0,1},{1,0},{2,3},{3,2},{4,5},{5,4},{6,7},{7,6},{8,9},{9,8},{10,11... | collective-permute-start | bytes 3145736 | tf_op jit(solution)/shard_map/ppermute | solution.py:605
  309.9 7.5 %collective-permute-start.9 = (bf16[4,128,1024]{2,1,0:T(8,128)(2,1)S(1)}, bf16[4,128,1024]{2,1,0:T(8,128)(2,1)S(1)}, u32[]{:S(2)}, u32[]{:S(2)}) collective-permute-start(bf16[4,128,1024]{2,1,0:T(8,128)(2,1)S(1)} %add_convert_fusion), channel_id=1, source_target_pairs={{0,1},{1,0},{2,3},{3,2},{4,5},{5,4},{6,7},{7,6},{8,9},{9,8},{10,11... | collective-permute-start | bytes 3145736 | tf_op jit(solution)/shard_map/ppermute | solution.py:605
  341.5 6.0 %copy-start.26 = (bf16[4,2,128,1024]{3,2,1,0:T(8,128)(2,1)S(1)}, bf16[4,2,128,1024]{3,2,1,0:T(8,128)(2,1)}, u32[]{:S(2)}) copy-start(bf16[4,2,128,1024]{3,2,1,0:T(8,128)(2,1)} %copy-done.25) | copy-start | bytes 6291460
  347.2 8.4 %collective-permute-start.10 = (bf16[4,128,1024]{2,1,0:T(8,128)(2,1)S(1)}, bf16[4,128,1024]{2,1,0:T(8,128)(2,1)S(1)}, u32[]{:S(2)}, u32[]{:S(2)}) collective-permute-start(bf16[4,128,1024]{2,1,0:T(8,128)(2,1)S(1)} %fusion.45), channel_id=1, source_target_pairs={{0,1},{1,0},{2,3},{3,2},{4,5},{5,4},{6,7},{7,6},{8,9},{9,8},{10,11... | collective-permute-start | bytes 3145736 | tf_op jit(solution)/shard_map/ppermute | solution.py:605
  359.2 196.2 %copy-start.3 = (f32[3,2,176,176]{3,2,1,0:T(8,128)S(1)}, f32[3,2,176,176]{3,2,1,0:T(8,128)}, u32[]{:S(2)}) copy-start(f32[3,2,176,176]{3,2,1,0:T(8,128)} %unit_root.1) | copy-start | bytes 2230276
  359.2 196.2 %copy-start.6 = (f32[4,2,64,64]{3,2,1,0:T(8,128)S(1)}, f32[4,2,64,64]{3,2,1,0:T(8,128)}, u32[]{:S(2)}) copy-start(f32[4,2,64,64]{3,2,1,0:T(8,128)} %head_stat.1) | copy-start | bytes 393220
  359.2 196.2 %copy-start.7 = (f32[4,2,64,64]{3,2,1,0:T(8,128)S(1)}, f32[4,2,64,64]{3,2,1,0:T(8,128)}, u32[]{:S(2)}) copy-start(f32[4,2,64,64]{3,2,1,0:T(8,128)} %head_root.1) | copy-start | bytes 393220
  547.9 7.6 %copy-start.1 = (bf16[1056,256]{1,0:T(8,128)(2,1)S(1)}, bf16[1056,256]{1,0:T(8,128)(2,1)}, u32[]{:S(2)}) copy-start(bf16[1056,256]{1,0:T(8,128)(2,1)} %get-tuple-element.57.sum_b) | copy-start | bytes 1622020
  547.9 7.6 %copy-start.2 = (f32[3,2,176,176]{3,2,1,0:T(8,128)S(1)}, f32[3,2,176,176]{3,2,1,0:T(8,128)}, u32[]{:S(2)}) copy-start(f32[3,2,176,176]{3,2,1,0:T(8,128)} %unit_stat.1) | copy-start | bytes 2230276
  549.6 40.7 %copy-start.36 = (f32[2,1024]{1,0:T(2,128)}, f32[2,1024]{1,0:T(2,128)S(1)}, u32[]{:S(2)}) copy-start(f32[2,1024]{1,0:T(2,128)S(1)} %reshape.471) | copy-start | bytes 24580
  557.7 20.8 %copy-start.34 = (f32[128,256]{1,0:T(8,128)S(1)}, f32[128,256]{1,0:T(8,128)}, u32[]{:S(2)}) copy-start(f32[128,256]{1,0:T(8,128)} %param.20) | copy-start | bytes 393220
  557.7 21.6 %copy-start.30 = (f32[352,256]{1,0:T(8,128)S(1)}, f32[352,256]{1,0:T(8,128)}, u32[]{:S(2)}) copy-start(f32[352,256]{1,0:T(8,128)} %param.21) | copy-start | bytes 1081348
  (27 other events, 66.5 us)

commit v3 on v2

--- a/solution.py
+++ b/solution.py
@@ -83,33 +83,6 @@
     return (key >= first) & (key <= query)
 
 
-def attend_kernel(
-    q_ref, k_ref, v_ref, vf_ref, cos_ref, sin_ref, first_ref, qr_ref, kr_ref, vm_ref, att_ref, lse_ref
-):
-    length = q_ref.shape[1]
-    cosine, sine_part = cos_ref[...], sin_ref[...]
-    q_raw, k_raw = q_ref[0], k_ref[0]
-    qr_ref[0] = ((q_raw * cosine + swap_halves(q_raw) * sine_part) * 0.125).astype(BF16)
-    kr_ref[0] = (k_raw * cosine + swap_halves(k_raw) * sine_part).astype(BF16)
-    v_mix = (0.5 * v_ref[0] + 0.5 * vf_ref[0].astype(F32)).astype(BF16)
-    vm_ref[0] = v_mix
-    v_turned = v_mix.T
-    for step in range(length // BLOCK):
-        begin, keys = step * BLOCK, (step + 1) * BLOCK
-        queries = two_heads(qr_ref[0, begin:keys, :])
-        scores = dot_nt(kr_ref[0, :keys, :], queries)
-        scores = jnp.where(seen(first_ref, begin, keys), scores, -1e30)
-        top = jnp.max(scores, axis=0, keepdims=True)
-        exps = jnp.exp(scores - top)
-        total = jnp.sum(exps, axis=0, keepdims=True)
-        chances = (exps * (1.0 / total)).astype(BF16)
-        attended = dot_nn(v_turned[:, :keys], chances)
-        att_ref[0, begin:keys, :] = one_pair(attended, BLOCK).astype(BF16)
-        log_total = top + jnp.log(total)
-        lse_ref[0, 0:1, begin:keys] = log_total[:, :BLOCK]
-        lse_ref[0, 1:2, begin:keys] = log_total[:, BLOCK:]
-
-
 def attend_back_kernel(
     qr_ref, kr_ref, vm_ref, att_ref, d_ref, lse_ref, cos_ref, sin_ref, first_ref,
     dq_ref, dk_ref, dv_ref, key_sum, value_sum,
@@ -119,7 +92,7 @@
     value_sum[...] = jnp.zeros_like(value_sum)
     k_turned = kr_ref[0].T
     cosine, sine_part = cos_ref[...], sin_ref[...]
-    product = (d_ref[0].astype(F32) * att_ref[0].astype(F32)).T
+    product = (d_ref[0].astype(F32) * att_ref[...].astype(F32)).T
     inner = [
         jnp.sum(product[:64], axis=0, keepdims=True),
         jnp.sum(product[64:], axis=0, keepdims=True),
@@ -147,25 +120,6 @@
     dv_ref[0] = (0.5 * value_sum[...]).astype(BF16)
 
 
-def attend(project, first_values, cos_wide, sin_wide, first_pos):
-    pairs, length, _ = project.shape
-    part = lambda i: pl.BlockSpec((1, length, LANES), lambda p: (p, 0, i))
-    table = pl.BlockSpec((length, LANES), lambda p: (0, 0))
-    out = jax.ShapeDtypeStruct((pairs, length, LANES), BF16)
-    return pl.pallas_call(
-        attend_kernel,
-        grid=(pairs,),
-        in_specs=[part(0), part(1), part(2), part(0), table, table,
-                  pl.BlockSpec((1, length), lambda p: (0, 0))],
-        out_specs=[part(0)] * 4 + [pl.BlockSpec((1, 2, length), lambda p: (p, 0, 0))],
-        out_shape=[out] * 4 + [jax.ShapeDtypeStruct((pairs, 2, length), F32)],
-        compiler_params=pltpu.CompilerParams(vmem_limit_bytes=48 << 20),
-        cost_estimate=pl.CostEstimate(
-            flops=pairs * length * length * 128 * 8, bytes_accessed=pairs * length * 128 * 24,
-            transcendentals=pairs * length * length),
-    )(project, project, project, first_values, cos_wide, sin_wide, first_pos[None, :])
-
-
 def attend_back(saved, d_attended, cos_wide, sin_wide, first_pos):
     q_rot, k_rot, v_mix, attended, log_total = saved
     pairs, length, _ = q_rot.shape
@@ -175,7 +129,8 @@
     return pl.pallas_call(
         attend_back_kernel,
         grid=(pairs,),
-        in_specs=[part] * 5 + [pl.BlockSpec((1, 2, length), lambda p: (p, 0, 0)), table, table,
+        in_specs=[part] * 3 + [pl.BlockSpec((length, LANES), lambda p: (0, p)), part,
+                               pl.BlockSpec((1, 2, length), lambda p: (p, 0, 0)), table, table,
                                pl.BlockSpec((1, length), lambda p: (0, 0))],
         out_specs=[part] * 3,
         out_shape=[out] * 3,
@@ -199,6 +154,26 @@
 
     def at_seq(self, step):
         return (self.seq + step + self.n_seq) % self.n_seq
+
+    @property
+    def line(self):
+        return self.slots == 4 and self.n_seq == 4
+
+    def source(self, step):
+        if not self.line:
+            return self.at_slot(-step)
+        upper = self.slot // 2
+        inner = (self.slot + upper) % 2
+        near = step + inner * (1 - 2 * step) * (1 - step // 2)
+        return near + upper * (3 - 2 * near)
+
+    @property
+    def beside(self):
+        return self.seq + 1 - 2 * (self.seq % 2)
+
+    @property
+    def across(self):
+        return self.seq + 2 - 4 * (self.seq // 2)
 
     def device(self, seq=None, slot=None, rank=None):
         seq = self.seq if seq is None else seq
@@ -223,12 +198,12 @@
     def __init__(self, send_sems, recv_sems):
         self.send_sems, self.recv_sems, self.used = send_sems, recv_sems, 0
 
-    def start(self, src, dst, device):
+    def start(self, src, dst, device, recv=None):
         copy = pltpu.make_async_remote_copy(
             src_ref=src,
             dst_ref=dst,
             send_sem=self.send_sems.at[self.used],
-            recv_sem=self.recv_sems.at[self.used],
+            recv_sem=self.recv_sems.at[self.used] if recv is None else recv,
             device_id=device,
             device_id_type=MESH,
         )
@@ -241,101 +216,372 @@
     return pl.ds(pl.multiple_of(index * width, width), width)
 
 
-def gather_kernel(
-    n_seq, n_head, sections, x_ref, vf_ref, wt_ref, x_out, vf_out, w_out, send_sems, recv_sems, own_sems
+def forward_kernel(
+    n_seq, n_head, head_cols,
+    x_ref, vf_ref, wt_ref, gains_ref, cos_ref, sin_ref, first_ref,
+    x_out, h_one, q_out, k_out, v_out, att_out, lse_out, w_a, w_b, middle, h_two,
+    vf_all, away, back, sems, z_recv, v_recv, own_sems,
 ):
-    slots = x_ref.shape[0]
+    slots, rows, width = x_ref.shape
     part = wt_ref.shape[1]
+    rows_a = w_a.shape[1]
     place = Place(n_seq, n_head, slots)
-    place.greet(False)
-    sender = Sender(send_sems, recv_sems)
+    ranks = place.ranks
+    length = slots * ranks * rows
+    per = LANES // head_cols
+    pairs = slots // per
     mine = lanes(place.seq, part)
-
-    def swap(src, dst):
+    sections = {"a": (w_a, pl.ds(0, rows_a)), "b": (w_b, pl.ds(rows_a, wt_ref.shape[0] - rows_a))}
+    ids = {}
+    elsewhere = place.device(seq=place.at_seq(1))
+
+    def index(name):
+        return ids.setdefault(name, len(ids))
+
+    def remote(name, src, dst, device, recv=None):
+        i = index(name)
+        return pltpu.make_async_remote_copy(
+            src_ref=src, dst_ref=dst, send_sem=sems.at[0, i],
+            recv_sem=sems.at[1, i] if recv is None else recv,
+            device_id=device, device_id_type=MESH,
+        )
+
+    def x_copy(k):
+        to = place.at_slot(k)
+        return remote(("x", k), x_ref.at[to], x_out.at[place.slot], place.device(slot=to))
+
+    def v_copy(k):
+        to = place.at_slot(k)
+        return remote(("v", k), vf_ref.at[to], vf_all.at[place.slot], place.device(slot=to),
+                      v_recv.at[place.slot])
+
+    def v_wait(source):
+        pltpu.make_async_remote_copy(
+            src_ref=vf_ref.at[0], dst_ref=vf_all.at[source], send_sem=sems.at[0, 0],
+            recv_sem=v_recv.at[source], device_id=elsewhere, device_id_type=MESH,
+        ).wait_recv()
+
+    def piece(sec, step):
+        ref, at = sections[sec]
+        return wt_ref.at[at] if step == 0 else ref.at[step, :, mine]
+
+    def z_copy(name, sec, step, to, to_step):
+        ref, _ = sections[sec]
+        which = 0 if sec == "a" else 1
+        return remote((name, sec, step), piece(sec, step), ref.at[to_step, :, mine],
+                      place.device(slot=to), z_recv.at[which, to_step])
+
+    def z_wait(sec, step):
+        ref, _ = sections[sec]
+        which = 0 if sec == "a" else 1
+        pltpu.make_async_remote_copy(
+            src_ref=piece(sec, 0), dst_ref=ref.at[step, :, mine], send_sem=sems.at[0, 0],
+            recv_sem=z_recv.at[which, step], device_id=elsewhere, device_id_type=MESH,
+        ).wait_recv()
+
+    slot = place.slot
+    upper = slot // 2
+    inner = (slot + upper) % 2
+
+    def z_start_own(sec):
+        if not place.line:
+            for k in range(1, slots):
+                z_copy(("z", k), sec, 0, place.at_slot(k), k).start()
+            return
+        @pl.when(slot < 3)
+        def _():
+            to = slot + 1
+            z_copy("up", sec, 0, to, 1 + (to == 2).astype(jnp.int32)).start()
+
+        @pl.when(slot > 0)
+        def _():
+            to = slot - 1
+            z_copy("down", sec, 0, to, 1 + (to == 1).astype(jnp.int32)).start()
+
+    def z_own_sends(sec):
+        if not place.line:
+            for k in range(1, slots):
+                z_copy(("z", k), sec, 0, place.at_slot(k), k).wait_send()
+            return
+
+        @pl.when(slot < 3)
+        def _():
+            z_copy("up", sec, 0, slot + 1, 1).wait_send()
+
+        @pl.when(slot > 0)
+        def _():
+            z_copy("down", sec, 0, slot - 1, 1).wait_send()
+
+    def z_relay(sec, step):
+        if step == 1:
+            return z_copy("on", sec, step, slot + 1 - 2 * upper, 3)
+        return z_copy("on", sec, step, slot - 1 + 2 * upper, step)
+
+    def near_copy(sec, step):
+        ref, _ = sections[sec]
+        dst = ref.at[step, :, mine]
+        if not place.line:
+            return [
+                remote(("xy", d, sec, step), piece(sec, step), dst, place.device(seq=place.at_seq(d)))
+                for d in range(1, n_seq)
+            ]
         return [
-            sender.start(
-                src.at[place.at_slot(k)], dst.at[place.slot], place.device(slot=place.at_slot(k))
-            )
-            for k in (2, 3, 1)
+            remote(("xy", 0, sec, step), piece(sec, step), dst, place.device(seq=place.beside)),
+            remote(("xy", 1, sec, step), piece(sec, step), dst, place.device(seq=place.across)),
         ]
 
-    def to_slots(section):
-        rows = pl.ds(*section)
-        return [
-            sender.start(
-                wt_ref.at[rows],
-                w_out.at[place.slot, rows, mine],
-                place.device(slot=place.at_slot(k)),
-            )
-            for k in range(1, slots)
-        ]
-
-    def to_seqs(section, step):
-        rows = pl.ds(*section)
-        slot = place.at_slot(-step)
-        src = wt_ref.at[rows] if step == 0 else w_out.at[slot, rows, mine]
-        return [
-            sender.start(
-                src, w_out.at[slot, rows, mine], place.device(seq=place.at_seq(d))
-            )
-            for d in range(1, n_seq)
-        ]
-
+    def far_copy(sec, step, which):
+        ref, at = sections[sec]
+        half = at.size // 2
+        cut = pl.ds(which * half, half)
+        source = place.beside if which == 0 else place.across
+        to = place.across if which == 0 else place.beside
+        where = ref.at[step, cut, lanes(source, part)]
+        return remote(("far", which, sec, step), where, where, place.device(seq=to))
+
+    def z_event(sec, step):
+        z_wait(sec, step)
+        if place.line:
+            @pl.when(inner == 1)
+            def _():
+                z_relay(sec, step).start()
+        for copy in near_copy(sec, step):
+            copy.start()
+
+    def xy_event(sec, step):
+        for which, copy in enumerate(near_copy(sec, step)):
+            copy.wait_recv()
+            if place.line:
+                far_copy(sec, step, which).start()
+
+    def done_event(sec, step):
+        if place.line:
+            for which in range(2):
+                far_copy(sec, step, which).wait_recv()
+
+    def position(p, rank):
+        return pl.ds(pl.multiple_of((p * ranks + rank) * rows, rows), rows)
+
+    def share(name, ref, p, j):
+        where = ref.at[position(p, place.rank), :]
+        return remote((name, p, j), where, where, place.device(rank=(place.rank + j) % ranks))
+
+    place.greet(True)
+    for k in (2, 3, 1):
+        x_copy(k).start()
     own = [
-        pltpu.make_async_copy(x_ref.at[place.slot], x_out.at[place.slot], own_sems.at[0]),
-        pltpu.make_async_copy(vf_ref.at[place.slot], vf_out.at[place.slot], own_sems.at[1]),
-        pltpu.make_async_copy(wt_ref, w_out.at[place.slot, :, mine], own_sems.at[2]),
+        pltpu.make_async_copy(x_ref.at[slot], x_out.at[slot], own_sems.at[0]),
+        pltpu.make_async_copy(wt_ref.at[sections["a"][1]], w_a.at[0, :, mine], own_sems.at[1]),
+        pltpu.make_async_copy(wt_ref.at[sections["b"][1]], w_b.at[0, :, mine], own_sems.at[2]),
+        pltpu.make_async_copy(vf_ref.at[slot], vf_all.at[slot], own_sems.at[3]),
     ]
-    x_copies = swap(x_ref, x_out)
-    copies = list(x_copies)
     for copy in own:
         copy.start()
-    near = to_slots(sections[0])
-    copies += near
-    copies += to_seqs(sections[0], 0)
-    copies += to_seqs(sections[1], 0)
-    received = []
-    for step, copy in enumerate(near):
-        copy.wait_recv()
-        copies += to_seqs(sections[0], step + 1)
-    received += near
-    copies += swap(vf_ref, vf_out)
-    near = to_slots(sections[1])
-    copies += near
-    for step, copy in enumerate(near):
-        copy.wait_recv()
-        copies += to_seqs(sections[1], step + 1)
-    received += near
-    for copy in copies:
-        if all(copy is not other for other in received):
-            copy.wait_recv()
-    for copy in copies:
-        copy.wait_send()
-    for copy in own:
-        copy.wait()
-
-
-def gather_inputs(n_seq, n_head, sections, layer_input, values_first, weight_rows):
-    slots = layer_input.shape[0]
-    rows, part = weight_rows.shape
-    count = 2 * (slots - 1) + len(sections) * ((slots - 1) + slots * (n_seq - 1))
+    z_start_own("a")
+    for copy in near_copy("a", 0):
+        copy.start()
+    xy_event("a", 0)
+    for copy in near_copy("b", 0):
+        copy.start()
+    z_event("a", 1)
+    for k in range(1, slots):
+        x_copy(k).wait_recv()
+    own[0].wait()
+    for k in range(1, slots):
+        v_copy(k).start()
+
+    for p in range(slots):
+        x = x_out[p].astype(F32)
+        normed = x * lax.rsqrt(jnp.mean(x * x, axis=-1, keepdims=True) + EPSILON)
+        h_one[position(p, place.rank), :] = (normed * gains_ref[0:1, :]).astype(BF16)
+        for j in range(1, ranks):
+            share("h1", h_one, p, j).start()
+    xy_event("a", 1)
+    z_event("a", 2)
+    z_start_own("b")
+    own[1].wait()
+    own[3].wait()
+    done_event("a", 0)
+    for p in range(slots):
+        for j in range(1, ranks):
+            share("h1", h_one, p, j).wait_recv()
+    events = {
+        (0, 1): [lambda: xy_event("a", 2)],
+        (0, 3): [lambda: z_event("a", 3)],
+        (1, 0): [lambda: done_event("a", 1)],
+        (1, 1): [lambda: xy_event("b", 0)],
+        (1, 2): [lambda: xy_event("a", 3)],
+        (1, 3): [lambda: z_event("b", 1)],
+        (2, 0): [lambda: done_event("a", 2)],
+        (2, 1): [lambda: z_event("b", 2)],
+        (2, 3): [lambda: xy_event("b", 1)],
+        (3, 0): [lambda: done_event("a", 3)],
+        (3, 1): [lambda: z_event("b", 3)],
+        (3, 3): [lambda: xy_event("b", 2)],
+    }
+    if per > 1:
+        xy_event("a", 2)
+        z_event("a", 3)
+        xy_event("a", 3)
+        xy_event("b", 0)
+        for step in range(1, slots):
+            done_event("a", step)
+            v_wait(place.source(step))
+            z_event("b", step)
+            xy_event("b", step)
+        events = {}
+
+    def one_pair_of_heads(j, carry):
+        def pump(point):
+            for (step, at), todo in events.items():
+                if at == point:
+                    @pl.when(j == step)
+                    def _(todo=todo):
+                        for act in todo:
+                            act()
+
+        pump(0)
+        if per == 1:
+            @pl.when(j > 0)
+            def _():
+                v_wait(place.source(j))
+            w_in = w_a[j, : 3 * head_cols, :]
+            first = vf_all[place.source(j)]
+        else:
+            w_in = jnp.concatenate(
+                [
+                    w_a[j * per + u, i * head_cols : (i + 1) * head_cols, :]
+                    for i in range(3)
+                    for u in range(per)
+                ],
+                axis=0,
+            )
+            first = jnp.concatenate([vf_all[place.source(j * per + u)] for u in range(per)], axis=1)
+        half = length // 2
+        for part_at in range(2):
+            at = slice(part_at * half, (part_at + 1) * half)
+            project = dot_nt(h_one[at, :], w_in)
+            cosine, sine_part = cos_ref[at, :], sin_ref[at, :]
+            q_raw, k_raw = project[:, :LANES], project[:, LANES : 2 * LANES]
+            q_out[j, at, :] = ((q_raw * cosine + swap_halves(q_raw) * sine_part) * 0.125).astype(BF16)
+            k_out[j, at, :] = (k_raw * cosine + swap_halves(k_raw) * sine_part).astype(BF16)
+            v_out[j, at, :] = (0.5 * project[:, 2 * LANES :] + 0.5 * first[at].astype(F32)).astype(BF16)
+        pump(1)
+        v_turned = v_out[j].T
+        for step in range(length // BLOCK):
+            begin, keys = step * BLOCK, (step + 1) * BLOCK
+            queries = two_heads(q_out[j, begin:keys, :])
+            scores = dot_nt(k_out[j, :keys, :], queries)
+            scores = jnp.where(seen(first_ref, begin, keys), scores, -1e30)
+            top = jnp.max(scores, axis=0, keepdims=True)
+            exps = jnp.exp(scores - top)
+            total = jnp.sum(exps, axis=0, keepdims=True)
+            chances = (exps * (1.0 / total)).astype(BF16)
+            attended = dot_nn(v_turned[:, :keys], chances)
+            att_out[begin:keys, lanes(j, LANES)] = one_pair(attended, BLOCK).astype(BF16)
+            log_total = top + jnp.log(total)
+            lse_out[j, 0:1, begin:keys] = log_total[:, :BLOCK]
+            lse_out[j, 1:2, begin:keys] = log_total[:, BLOCK:]
+            if step == length // BLOCK // 2 - 1:
+                pump(2)
+        pump(3)
+        return carry
+
+    lax.fori_loop(0, pairs, one_pair_of_heads, 0)
+
+    w_o = w_a[:, 3 * head_cols :, :].reshape(slots * head_cols, width)
+
+    def away_copy(p, j):
+        return remote(("away", p, j), away.at[j - 1, p], back.at[j - 1, p],
+                      place.device(rank=(place.rank + j) % ranks))
+
+    for p in range(slots):
+        for j in range(1, ranks):
+            at = position(p, (place.rank + j) % ranks)
+            away[j - 1, p] = dot_nn(att_out[at, :], w_o).astype(BF16)
+            away_copy(p, j).start()
+    if per == 1:
+        xy_event("b", 3)
+    for p in range(slots):
+        middle[p] = x_out[p].astype(F32) + dot_nn(att_out[position(p, place.rank), :], w_o)
+    for p in range(slots):
+        value = middle[p]
+        for j in range(1, ranks):
+            away_copy(p, j).wait_recv()
+            value = value + back[j - 1, p].astype(F32)
+        middle[p] = value
+        normed = value * lax.rsqrt(jnp.mean(value * value, axis=-1, keepdims=True) + EPSILON)
+        h_two[position(p, place.rank), :] = (normed * gains_ref[1:2, :]).astype(BF16)
+        for j in range(1, ranks):
+            share("h2", h_two, p, j).start()
+    for p in range(slots):
+        for j in range(1, ranks):
+            share("h2", h_two, p, j).wait_recv()
+    for step in range(slots):
+        done_event("b", step)
+    for p in range(slots):
+        for j in range(1, ranks):
+            share("h1", h_one, p, j).wait_send()
+            share("h2", h_two, p, j).wait_send()
+            away_copy(p, j).wait_send()
+    for k in range(1, slots):
+        x_copy(k).wait_send()
+        v_copy(k).wait_send()
+    for sec in ("a", "b"):
+        z_own_sends(sec)
+        for step in range(slots):
+            for copy in near_copy(sec, step):
+                copy.wait_send()
+            if place.line:
+                for which in range(2):
+                    far_copy(sec, step, which).wait_send()
+                if step > 0:
+                    @pl.when(inner == 1)
+                    def _(sec=sec, step=step):
+                        z_relay(sec, step).wait_send()
+    own[2].wait()
+
+
+def forward_part(n_seq, n_head, head_cols, layer_input, values_first, weight_rows, gains, cos_wide, sin_wide, first_pos):
+    slots, rows, width = layer_input.shape
+    all_rows, part = weight_rows.shape
+    ranks = n_head // slots
+    length = slots * ranks * rows
+    rows_a = 4 * head_cols
+    pairs = slots * head_cols // LANES
+    count = 2 * (slots - 1) + 2 * (2 + 4 * slots + slots * n_seq) + 3 * slots * ranks
     any_space = pl.BlockSpec(memory_space=pl.ANY)
+    vmem = pl.BlockSpec(memory_space=pltpu.VMEM)
+    shape = jax.ShapeDtypeStruct
+    heads = shape((pairs, length, LANES), BF16)
     return pl.pallas_call(
-        functools.partial(gather_kernel, n_seq, n_head, sections),
-        in_specs=[any_space] * 3,
-        out_specs=[any_space] * 3,
+        functools.partial(forward_kernel, n_seq, n_head, head_cols),
+        in_specs=[any_space] * 3 + [vmem] * 4,
+        out_specs=[vmem] * 8 + [any_space] + [vmem] * 2,
         out_shape=[
-            jax.ShapeDtypeStruct(layer_input.shape, BF16),
-            jax.ShapeDtypeStruct(values_first.shape, BF16),
-            jax.ShapeDtypeStruct((slots, rows, part * n_seq), BF16),
+            shape(layer_input.shape, BF16),
+            shape((length, width), BF16),
+            heads, heads, heads,
+            shape((length, slots * head_cols), BF16),
+            shape((pairs, 2, length), F32),
+            shape((slots, rows_a, width), BF16),
+            shape((slots, all_rows - rows_a, width), BF16),
+            shape(layer_input.shape, F32),
+            shape((length, width), BF16),
         ],
         scratch_shapes=[
-            pltpu.SemaphoreType.DMA((count,)),
-            pltpu.SemaphoreType.DMA((count,)),
-            pltpu.SemaphoreType.DMA((3,)),
+            pltpu.VMEM(values_first.shape, BF16),
+            pltpu.VMEM((ranks - 1, slots, rows, width), BF16),
+            pltpu.VMEM((ranks - 1, slots, rows, width), BF16),
+            pltpu.SemaphoreType.DMA((2, count)),
+            pltpu.SemaphoreType.DMA((2, slots)),
+            pltpu.SemaphoreType.DMA((slots,)),
+            pltpu.SemaphoreType.DMA((4,)),
         ],
-        compiler_params=pltpu.CompilerParams(collective_id=0, has_side_effects=True),
-    )(layer_input, values_first, weight_rows)
+        compiler_params=pltpu.CompilerParams(
+            collective_id=0, has_side_effects=True, vmem_limit_bytes=60 << 20
+        ),
+    )(layer_input, values_first, weight_rows, gains, cos_wide, sin_wide, first_pos[None, :])
 
 
 def reduce_kernel(
@@ -343,7 +589,7 @@
     block_ref, input_ref, first_ref, gains_ref, grads_a, grads_b,
     block_out, input_out, first_out, gains_out, sum_a, sum_b, full_a, full_b,
     near_a, near_b, turn_a, turn_b, far_a, far_b, gain_seq, gain_slot, gain_rank,
-    send_sems, recv_sems, own_sems,
+    send_sems, recv_sems, own_sems, far_recv, first_recv,
 ):
     slots = block_ref.shape[0]
     place = Place(n_seq, n_head, slots)
@@ -377,10 +623,9 @@
     copies += small
 
     def to_seqs(grads, near, k):
-        slot = place.at_slot(k)
         return [
             sender.start(
-                grads.at[slot, :, lanes(place.at_seq(d), part)],
+                grads.at[k, :, lanes(place.at_seq(d), part)],
                 near.at[k, d - 1],
                 place.device(seq=place.at_seq(d)),
             )
@@ -396,9 +641,13 @@
         copies.extend(sent[unit])
 
     own = [
-        pltpu.make_async_copy(src.at[place.slot], dst.at[place.slot], own_sems.at[i])
+        pltpu.make_async_copy(src, dst.at[place.slot], own_sems.at[i])
         for i, (src, dst) in enumerate(
-            ((block_ref, block_out), (input_ref, input_out), (first_ref, first_out))
+            (
+                (block_ref.at[place.slot], block_out),
+                (input_ref.at[place.slot], input_out),
+                (first_ref.at[0], first_out),
+            )
         )
     ]
     for copy in own:
@@ -418,7 +667,7 @@
         for k in range(1, slots)
     ]
     copies += small
-    far_copies = {0: [], 1: []}
+    elsewhere = place.device(seq=place.at_seq(1))
     for index, unit in enumerate(units):
         which, k = unit
         grads, _, _, near, turn, far, chunk = parts[which]
@@ -426,11 +675,10 @@
             launch(units[index + 2])
         for copy in sent[unit]:
             arrive(copy)
-        slot = place.at_slot(k)
-
-        def add(i, carry, grads=grads, near=near, turn=turn, slot=slot, k=k, chunk=chunk):
+
+        def add(i, carry, grads=grads, near=near, turn=turn, k=k, chunk=chunk):
             rows = pl.ds(pl.multiple_of(i * chunk, chunk), chunk)
-            value = grads[slot, rows, mine].astype(F32)
+            value = grads[k, rows, mine].astype(F32)
             for d in range(n_seq - 1):
                 value = value + near[k, d, rows, :].astype(F32)
             turn[k, rows, :] = value.astype(BF16)
@@ -438,11 +686,20 @@
 
         lax.fori_loop(0, grads.shape[1] // chunk, add, 0)
         if k != 0:
-            copy = sender.start(turn.at[k], far.at[k - 1], place.device(slot=slot))
+            copy = sender.start(
+                turn.at[k], far.at[place.slot], place.device(slot=place.source(k)),
+                far_recv.at[which, place.slot],
+            )
             copies.append(copy)
-            far_copies[which].append(copy)
+            received.append(copy)
         if index == 1:
-            copies += swap(first_ref, first_out)
+            for j in range(1, slots):
+                copy = sender.start(
+                    first_ref.at[j], first_out.at[place.slot],
+                    place.device(slot=place.source(j)), first_recv.at[place.slot],
+                )
+                copies.append(copy)
+                received.append(copy)
         if index == 4:
             copies += swap(input_ref, input_out)
             for copy in small:
@@ -458,15 +715,19 @@
             ]
             copies += small
         if k == 0:
-            for copy in far_copies[which]:
-                arrive(copy)
+            for j in range(1, slots):
+                source = place.at_slot(j)
+                pltpu.make_async_remote_copy(
+                    src_ref=turn.at[0], dst_ref=far.at[source], send_sem=send_sems.at[0],
+                    recv_sem=far_recv.at[which, source], device_id=elsewhere, device_id_type=MESH,
+                ).wait_recv()
             _, total_ref, full, _, _, _, _ = parts[which]
 
             def finish(i, carry, turn=turn, far=far, total_ref=total_ref, full=full, chunk=chunk):
                 rows = pl.ds(pl.multiple_of(i * chunk, chunk), chunk)
                 value = turn[0, rows, :].astype(F32)
-                for j in range(slots - 1):
-                    value = value + far[j, rows, :].astype(F32)
+                for j in range(1, slots):
+                    value = value + far[place.at_slot(j), rows, :].astype(F32)
                 value = value.astype(BF16)
                 total_ref[rows, :] = value
                 full[rows, mine] = value
@@ -486,6 +747,12 @@
     for copy in copies:
         if all(copy is not other for other in received):
             copy.wait_recv()
+    for j in range(1, slots):
+        source = place.at_slot(j)
+        pltpu.make_async_remote_copy(
+            src_ref=first_ref.at[0], dst_ref=first_out.at[source], send_sem=send_sems.at[0],
+            recv_sem=first_recv.at[source], device_id=elsewhere, device_id_type=MESH,
+        ).wait_recv()
     for copy in copies:
         copy.wait_send()
     for copy in own:
@@ -513,12 +780,14 @@
         + [jax.ShapeDtypeStruct((r, part * n_seq), BF16) for r in rows],
         scratch_shapes=[pltpu.VMEM((slots, n_seq - 1, r, part), BF16) for r in rows]
         + [pltpu.VMEM((slots, r, part), BF16) for r in rows]
-        + [pltpu.VMEM((slots - 1, r, part), BF16) for r in rows]
+        + [pltpu.VMEM((slots, r, part), BF16) for r in rows]
         + [pltpu.VMEM((n,) + gains.shape, F32) for n in (n_seq, slots, ranks)]
         + [
             pltpu.SemaphoreType.DMA((count,)),
             pltpu.SemaphoreType.DMA((count,)),
             pltpu.SemaphoreType.DMA((3,)),
+            pltpu.SemaphoreType.DMA((2, slots)),
+            pltpu.SemaphoreType.DMA((slots,)),
         ],
         compiler_params=pltpu.CompilerParams(
             collective_id=1, has_side_effects=True, vmem_limit_bytes=56 << 20
@@ -690,46 +959,32 @@
         ],
         axis=0,
     )
-    x_bf16, first_all, weights = gather_inputs(
-        n_seq, n_head, ((0, rows_a), (rows_a, rows_b)), layer_input, values_first, weight_rows
-    )
-    w_in, w_o = weights[:, : 3 * head_cols], weights[:, 3 * head_cols : rows_a]
-    w_gu, w_d = weights[:, rows_a : rows_a + 2 * ffn_cols], weights[:, rows_a + 2 * ffn_cols :]
-    x_own = x_bf16.reshape(slots * rows, width).astype(F32)
-    ein = functools.partial(jnp.einsum, preferred_element_type=F32)
-
     segment_ids = lax.dynamic_index_in_dim(segments, links.slot, 0, keepdims=False)
     first_pos, cos_wide, sin_wide = position_tables(segment_ids, head_dim)
-
+    x_bf16, h_one, q_rot, k_rot, v_mix, attended, log_total, weights_a, weights_b, middle, h_two = (
+        forward_part(
+            n_seq, n_head, head_cols, layer_input, values_first, weight_rows, norm_gains,
+            cos_wide, sin_wide, first_pos,
+        )
+    )
+    w_in, w_o = weights_a[:, : 3 * head_cols], weights_a[:, 3 * head_cols :]
+    w_gu, w_d = weights_b[:, : 2 * ffn_cols], weights_b[:, 2 * ffn_cols :]
+    x_own = x_bf16.reshape(slots * rows, width).astype(F32)
+    middle = middle.reshape(slots * rows, width)
+    ein = functools.partial(jnp.einsum, preferred_element_type=F32)
     inverse_one = lax.rsqrt(jnp.mean(x_own * x_own, axis=-1, keepdims=True) + EPSILON)
     normed_one = x_own * inverse_one
-    h_one = links.whole_sequence(
-        (normed_one * norm_gains[0]).astype(BF16).reshape(slots, rows, width)
-    )
-    project = ein("ld,qcd->qlc", h_one, w_in)
-    if per > 1:
-        project = pair_major(project.reshape(slots, length, 3, head_cols)).reshape(
-            pairs, length, 3 * LANES
-        )
-        first_all = pair_major(first_all[:, :, None])[:, :, 0]
-    saved = attend(project, first_all, cos_wide, sin_wide, first_pos)
-    attended = saved[3]
-    if per > 1:
-        attended = slot_major(attended[:, :, None])[:, :, 0]
-    attn_out = links.own_sum(ein("qlc,qcd->ld", attended, w_o))
-    middle = x_own + attn_out
     inverse_two = lax.rsqrt(jnp.mean(middle * middle, axis=-1, keepdims=True) + EPSILON)
     normed_two = middle * inverse_two
-    h_two = links.whole_sequence(
-        (normed_two * norm_gains[1]).astype(BF16).reshape(slots, rows, width)
-    )
+    saved = (q_rot, k_rot, v_mix, attended, log_total)
+    attended = jnp.swapaxes(attended.reshape(length, slots, head_cols), 0, 1)
     gate_up = ein("ld,qfd->qlf", h_two, w_gu)
     gate, up = gate_up[..., :ffn_cols], gate_up[..., ffn_cols:]
     sigmoid_gate = jax.nn.sigmoid(gate)
     activated = gate * sigmoid_gate
     hidden = (activated * up).astype(BF16)
     ffn_out = links.own_sum(ein("qlf,qfd->ld", hidden, w_d))
-    block_delta = jnp.where(is_live, attn_out + ffn_out, 0.0).astype(BF16)
+    block_delta = jnp.where(is_live, middle - x_own + ffn_out, 0.0).astype(BF16)
 
     grad_own = links.swap_slots(out_grad)
     d_own = jnp.where(is_live, grad_own, jnp.zeros_like(grad_own))

time: 597 us -> 517 us (0.87)
  Pallas kernels: 407 us -> 383 us
  waiting for transfers between devices: 17.3 us -> 0.02 us
  matrix products: 76.2 us -> 60.3 us
  starting transfers between devices: 21.1 us -> 6.88 us
    pallas_call x3 -> x2, Pallas kernels: 197 us -> 175 us  [the longest x1 158 us: forward_part(): pl.pallas_call(functools.partial(forward_kernel, n_seq, n_head, head_cols...]
    ppermute x11 -> x8, waiting for transfers between devices: 17.3 us -> 0.02 us  [permute(): return lax.ppermute(value, AXES, pairs)]
    ppermute x11 -> x8, starting transfers between devices: 21.1 us -> 6.88 us  [permute(): return lax.ppermute(value, AXES, pairs)]
    dot_general x2 -> x0, matrix products: 11.3 us -> none  [the longest x1 8.04 us: shards(): project = ein('ld,qcd->qlc', h_one, w_in)]
  transfers between devices with their start and end apart: 11 -> 8, of which waited for: 3 -> 0; matrix products, arithmetic and copies ran while one was open for 7% -> 11% of each run, Pallas kernels for 0% -> 34%
where the time goes in v3:
time: 517 us; the launch traced here: 513 us
  Pallas kernels  383 us (74%)
  matrix products  60.3 us (12%)
  other arithmetic  42.2 us (8%)
  local copies, waits for them, and re-layouts  17.9 us (3%)
  starting transfers between devices  6.88 us (1%)
    pallas_call x1, Pallas kernels, reduce_grads(): pl.pallas_call(functools.partial(reduce_kernel, n_seq, n_head, chunks), i...  187 us
    pallas_call x1, Pallas kernels, forward_part(): pl.pallas_call(functools.partial(forward_kernel, n_seq, n_head, head_cols...  158 us
    pallas_call x1, Pallas kernels, shampoo(): pl.pallas_call(shampoo_kernel, grid=(members,), in_specs=[wide, wide] + [...  20.7 us
    pallas_call x1, Pallas kernels, attend_back(): pl.pallas_call(attend_back_kernel, grid=(pairs,), in_specs=[part] * 3 + [...  17.4 us
    dot_general x1, matrix products, shards(): gate_up = ein('ld,qfd->qlf', h_two, w_gu)  11.7 us
  transfers between devices with their start and end apart: 8, of which 0 were waited for; matrix products, arithmetic and copies ran while one was open for 11% of the time, Pallas kernels for 34%

profile of v3, /device:TPU:0, one launch (start us, length us, event | category | flops | bytes accessed | tf_op | source)
XLA Modules:
  0.0 512.7 jit_solution(9097107313428826495)
XLA Ops:
  0.7 2.1 constant_dynamic-slice_fusion.4
  2.8 5.0 collective-permute-start.3
  10.1 1.9 fusion.46
  12.0 1.8 pad_maximum_fusion.9
  14.8 157.8 %shard_map.287 = (bf16[4,128,1024]{2,1,0:T(8,128)(2,1)}, bf16[1024,1024]{1,0:T(8,128)(2,1)}, bf16[4,1024,128]{2,1,0:T(8,128)(2,1)}, bf16[4,1024,128]{2,1,0:T(8,1...) custom-call(bf16[4,128,1024]{2,1,0:T(8,128)(2,1)} %x_ref.1, ...), custom_call_target="tpu_custom_call" | custom-call | tf_op jit(solution)/shard_map/pallas_call | solution.py:557
  174.2 1.8 multiply_reduce_fusion.2
  180.9 11.7 %fusion.9 = f32[4,1024,704]{1,2,0:T(8,128)} fusion(bf16[4,1056,1024]{2,1,0:T(8,128)(2,1)} %get-tuple-element.47, bf16[1024,1024]{1,0:T(8,128)(2,1)S(1)} %copy-done.39), kind=kOutput, calls=%fused_computation.16 | convolution fusion | flops 5905580032 | bytes 19398656 | tf_op jit(solution)/shard_map/ld,qfd->qlf/dot_general | solution.py:981
  194.0 9.3 %fusion.2 = (bf16[4,1024,352]{1,2,0:T(8,128)(2,1)S(1)}, bf16[4,1024,352]{1,2,0:T(8,128)(2,1)S(1)}, bf16[4,1024,352]{1,2,0:T(8,128)(2,1)S(1)}) fusion(f32[4,1024,704]{1,2,0:T(8,128)} %fusion.9, bf16[1024,1024,1]{1,0,2:T(8,128)(2,1)S(1)} %bitcast.166, bf16[4,1056,1024]{2,1,0:T(8,128)(2,1)} %get-tuple-element.47), kind=kOutput, calls=%fused_computation.6 | convolution fusion | flops 2974416896 | bytes 25165824 | tf_op jit(solution)/shard_map/ld,qfd->qlf/dot_general | solution.py:994
  203.3 6.4 %fusion.21 = f32[1024,1024,1]{1,0,2:T(8,128)S(1)} fusion(bf16[4,1024,352]{1,2,0:T(8,128)(2,1)S(1)} %get-tuple-element.81, bf16[4,1056,1024]{2,1,0:T(8,128)(2,1)} %get-tuple-element.47), kind=kOutput, calls=%fused_computation.29 | convolution fusion | flops 2952790016 | bytes 9961472 | tf_op jit(solution)/shard_map/qlf,qfd->ld/dot_general | solution.py:986
  209.8 3.4 convolution_convert_fusion.1
  213.2 8.3 %fusion.5 = f32[1024,1024,1]{1,0,2:T(8,128)S(1)} fusion(bf16[4,1056,1024]{2,1,0:T(8,128)(2,1)} %get-tuple-element.47, bf16[4,1024,352]{1,2,0:T(8,128)(2,1)S(1)} %get-tuple-element.80, bf16[4,1024,352]{1,2,0:T(8,128)(2,1)S(1)} %get-tuple-element.79), kind=kOutput, calls=%fused_computation.11 | convolution fusion | flops 5917114368 | bytes 15728640 | tf_op jit(solution)/shard_map/qlf,qfd->ld/dot_general | solution.py:1000
  223.4 8.5 %fusion.13 = bf16[4,704,1024]{2,1,0:T(8,128)(2,1)S(1)} fusion(bf16[4,1024,352]{1,2,0:T(8,128)(2,1)} %copy-done.40, bf16[4,1024,352]{1,2,0:T(8,128)(2,1)S(1)} %get-tuple-element.79, bf16[1024,1024]{1,0:T(8,128)(2,1)S(1)} %copy-done.39), kind=kOutput, calls=%fused_computation.18 | convolution fusion | flops 5919997952 | bytes 13631488 | tf_op jit(solution)/shard_map/qlf,ld->qfd/dot_general | solution.py:1001
  233.7 3.8 pad_maximum_fusion.grads_b
  238.7 4.3 fusion.37.d_ref
  243.0 17.4 %shard_map.288 = (bf16[4,1024,128]{2,1,0:T(8,128)(2,1)S(1)}, bf16[4,1024,128]{2,1,0:T(8,128)(2,1)S(1)}, bf16[4,1024,128]{2,1,0:T(8,128)(2,1)S(1)}) custom-call(bf16[4,1024,128]{2,1,0:T(8,128)(2,1)S(1)} %copy-done.11, bf16[4,1024,128]{2,1,0:T(8,128)(2,1)} %get-tuple-element.50.kr_ref, bf16[4,1024,128]{2,1,0:T(8,128)(2,1)} %get-tuple-element.51.vm_ref, ...), custom_call_target="tpu_custom_call" | custom-call | flops 10737418240 | bytes 12582912 | tf_op jit(solution)/shard_map/pallas_call | solution.py:129
  263.0 3.4 fusion.14
  267.0 3.7 convolution_convert_fusion
  272.0 2.4 pad_maximum_fusion.2.grads_a
  276.6 3.8 fusion.28
  280.5 187.0 %shard_map.289 = (bf16[4,128,1024]{2,1,0:T(8,128)(2,1)}, bf16[4,128,1024]{2,1,0:T(8,128)(2,1)}, bf16[4,1024,128]{2,1,0:T(8,128)(2,1)}, f32[16,128]{1,0:T(8,128)}...) custom-call(bf16[4,128,1024]{2,1,0:T(8,128)(2,1)} %get-tuple-element, ...), custom_call_target="tpu_custom_call" | custom-call | tf_op jit(solution)/shard_map/pallas_call | solution.py:774
  467.5 1.7 slice.75
  470.7 1.7 slice.76
  476.3 20.7 %shard_map.290 = (f32[6,2,256,1024]{3,2,1,0:T(8,128)}, f32[1,2,256,1024]{3,2,1,0:T(8,128)}, f32[4,2,64,64]{3,2,1,0:T(8,128)}, f32[3,2,176,176]{3,2,1,0:T(8,128)}...) custom-call(f32[7,2,256,1024]{3,2,1,0:T(8,128)} %stat_ref.1, f32[7,2,256,1024]{3,2,1,0:T(8,128)} %root_ref.1, ...), custom_call_target="tpu_custom_call" | custom-call | tf_op jit(solution)/shard_map/pallas_call | solution.py:840
  501.6 2.9 convert_add_fusion.1
  (158 shorter events, 39.2 us)
Async XLA Ops:
  0.7 7.8 %copy-start.25 = (f32[352,256]{1,0:T(8,128)S(1)}, f32[352,256]{1,0:T(8,128)}, u32[]{:S(2)}) copy-start(f32[352,256]{1,0:T(8,128)} %param.21) | copy-start | bytes 1081348
  0.7 7.8 %copy-start.17 = (f32[2,256,352]{1,2,0:T(8,128)S(1)}, f32[2,256,352]{1,2,0:T(8,128)}, u32[]{:S(2)}) copy-start(f32[2,256,352]{1,2,0:T(8,128)} %param.19) | copy-start | bytes 2162692
  0.7 7.9 %copy-start.32 = (f32[128,256]{1,0:T(8,128)S(1)}, f32[128,256]{1,0:T(8,128)}, u32[]{:S(2)}) copy-start(f32[128,256]{1,0:T(8,128)} %param.20) | copy-start | bytes 393220
  0.7 7.9 %copy-start.23 = (f32[3,256,128]{2,1,0:T(8,128)S(1)}, f32[3,256,128]{2,1,0:T(8,128)}, u32[]{:S(2)}) copy-start(f32[3,256,128]{2,1,0:T(8,128)} %param.18) | copy-start | bytes 1179652
  0.7 8.0 %copy-start.35 = (s32[4,1024]{1,0:T(4,128)S(1)}, s32[4,1024]{1,0:T(4,128)}, u32[]{:S(2)}) copy-start(s32[4,1024]{1,0:T(4,128)} %param.24) | copy-start | bytes 49156
  2.8 175.2 %collective-permute-start.3 = (bf16[128,1024]{1,0:T(8,128)(2,1)}, bf16[128,1024]{1,0:T(8,128)(2,1)}, u32[]{:S(2)}, u32[]{:S(2)}) collective-permute-start(bf16[128,1024]{1,0:T(8,128)(2,1)} %get-tuple-element.95), channel_id=1, source_target_pairs={{0,6},{1,7},{2,4},{3,5},{4,2},{5,3},{6,0},{7,1},{8,14},{9,15},{10,... | collective-permute-start | bytes 786440 | tf_op jit(solution)/shard_map/ppermute | solution.py:874
  7.9 170.2 %collective-permute-start.2 = (bf16[128,1024]{1,0:T(8,128)(2,1)S(1)}, bf16[128,1024]{1,0:T(8,128)(2,1)}, u32[]{:S(2)}, u32[]{:S(2)}) collective-permute-start(bf16[128,1024]{1,0:T(8,128)(2,1)S(1)} %get-tuple-element.93), channel_id=1, source_target_pairs={{0,4},{1,5},{2,6},{3,7},{4,0},{5,1},{6,2},{7,3},{8,12},{9,13},{10,... | collective-permute-start | bytes 786440 | tf_op jit(solution)/shard_map/ppermute | solution.py:874
  7.9 170.2 %collective-permute-start.1 = (bf16[128,1024]{1,0:T(8,128)(2,1)S(1)}, bf16[128,1024]{1,0:T(8,128)(2,1)}, u32[]{:S(2)}, u32[]{:S(2)}) collective-permute-start(bf16[128,1024]{1,0:T(8,128)(2,1)S(1)} %get-tuple-element.94), channel_id=1, source_target_pairs={{0,2},{1,3},{2,0},{3,1},{4,6},{5,7},{6,4},{7,5},{8,10},{9,11},{10,... | collective-permute-start | bytes 786440 | tf_op jit(solution)/shard_map/ppermute | solution.py:874
  179.6 13.2 %collective-permute-start.4 = (bf16[4,128,1024]{2,1,0:T(8,128)(2,1)S(1)}, bf16[4,128,1024]{2,1,0:T(8,128)(2,1)S(1)}, u32[]{:S(2)}, u32[]{:S(2)}) collective-permute-start(bf16[4,128,1024]{2,1,0:T(8,128)(2,1)S(1)} %maximum_select_fusion.1), channel_id=1, source_target_pairs={{0,1},{1,0},{2,3},{3,2},{4,5},{5,4},{6,7},{7,6},{8,9},{9,8},{10,11... | collective-permute-start | bytes 3145736 | tf_op jit(solution)/shard_map/ppermute | solution.py:874
  203.3 9.9 %copy-start.40 = (bf16[4,1024,352]{1,2,0:T(8,128)(2,1)}, bf16[4,1024,352]{1,2,0:T(8,128)(2,1)S(1)}, u32[]{:S(2)}) copy-start(bf16[4,1024,352]{1,2,0:T(8,128)(2,1)S(1)} %get-tuple-element.80) | copy-start | bytes 8650756
  209.8 12.0 %copy-start.18 = (f32[1024,1024,1]{1,0,2:T(8,128)}, f32[1024,1024,1]{1,0,2:T(8,128)S(1)}, u32[]{:S(2)}) copy-start(f32[1024,1024,1]{1,0,2:T(8,128)S(1)} %fusion.21) | copy-start | bytes 12582916
  221.6 10.3 %collective-permute-start.5 = (bf16[4,128,1024]{2,1,0:T(8,128)(2,1)S(1)}, bf16[4,128,1024]{2,1,0:T(8,128)(2,1)S(1)}, u32[]{:S(2)}, u32[]{:S(2)}) collective-permute-start(bf16[4,128,1024]{2,1,0:T(8,128)(2,1)S(1)} %fusion.38), channel_id=1, source_target_pairs={{0,1},{1,0},{2,3},{3,2},{4,5},{5,4},{6,7},{7,6},{8,9},{9,8},{10,11... | collective-permute-start | bytes 3145736 | tf_op jit(solution)/shard_map/ppermute | solution.py:874
  222.9 9.0 %copy-start.13 = (f32[4,128,1024]{2,1,0:T(8,128)S(1)}, f32[4,128,1024]{2,1,0:T(8,128)}, u32[]{:S(2)}) copy-start(f32[4,128,1024]{2,1,0:T(8,128)} %get-tuple-element.45) | copy-start | bytes 6291460
  222.9 53.0 %collective-permute-start = (bf16[4,128,1024]{2,1,0:T(8,128)(2,1)}, bf16[4,128,1024]{2,1,0:T(8,128)(2,1)}, u32[]{:S(2)}, u32[]{:S(2)}) collective-permute-start(bf16[4,128,1024]{2,1,0:T(8,128)(2,1)} %fusion.39), channel_id=1, source_target_pairs={{0,1},{1,0},{2,3},{3,2},{4,5},{5,4},{6,7},{7,6},{8,9},{9,8},{10,11... | collective-permute-start | bytes 3145736 | tf_op jit(solution)/shard_map/ppermute | solution.py:874
  233.5 4.0 collective-permute-start.6
  266.6 7.8 %collective-permute-start.7 = (bf16[4,128,1024]{2,1,0:T(8,128)(2,1)S(1)}, bf16[4,128,1024]{2,1,0:T(8,128)(2,1)S(1)}, u32[]{:S(2)}, u32[]{:S(2)}) collective-permute-start(bf16[4,128,1024]{2,1,0:T(8,128)(2,1)S(1)} %fusion.40), channel_id=1, source_target_pairs={{0,1},{1,0},{2,3},{3,2},{4,5},{5,4},{6,7},{7,6},{8,9},{9,8},{10,11... | collective-permute-start | bytes 3145736 | tf_op jit(solution)/shard_map/ppermute | solution.py:874
  280.4 193.7 %copy-start.5 = (f32[3,2,176,176]{3,2,1,0:T(8,128)S(1)}, f32[3,2,176,176]{3,2,1,0:T(8,128)}, u32[]{:S(2)}) copy-start(f32[3,2,176,176]{3,2,1,0:T(8,128)} %unit_root.1) | copy-start | bytes 2230276
  280.4 193.7 %copy-start.8 = (f32[4,2,64,64]{3,2,1,0:T(8,128)S(1)}, f32[4,2,64,64]{3,2,1,0:T(8,128)}, u32[]{:S(2)}) copy-start(f32[4,2,64,64]{3,2,1,0:T(8,128)} %head_stat.1) | copy-start | bytes 393220
  280.4 193.7 %copy-start.9 = (f32[4,2,64,64]{3,2,1,0:T(8,128)S(1)}, f32[4,2,64,64]{3,2,1,0:T(8,128)}, u32[]{:S(2)}) copy-start(f32[4,2,64,64]{3,2,1,0:T(8,128)} %head_root.1) | copy-start | bytes 393220
  467.4 6.7 %copy-start.1 = (bf16[1056,256]{1,0:T(8,128)(2,1)S(1)}, bf16[1056,256]{1,0:T(8,128)(2,1)}, u32[]{:S(2)}) copy-start(bf16[1056,256]{1,0:T(8,128)(2,1)} %get-tuple-element.63.sum_b) | copy-start | bytes 1622020
  467.4 6.7 %copy-start.4 = (f32[3,2,176,176]{3,2,1,0:T(8,128)S(1)}, f32[3,2,176,176]{3,2,1,0:T(8,128)}, u32[]{:S(2)}) copy-start(f32[3,2,176,176]{3,2,1,0:T(8,128)} %unit_stat.1) | copy-start | bytes 2230276
  497.0 4.5 copy-start.15
  499.4 5.1 %copy-start.16 = (bf16[4,128,1024]{2,1,0:T(8,128)(2,1)S(1)}, bf16[4,128,1024]{2,1,0:T(8,128)(2,1)}, u32[]{:S(2)}) copy-start(bf16[4,128,1024]{2,1,0:T(8,128)(2,1)} %param.23) | copy-start | bytes 3145732
  500.2 11.5 %copy-start.34 = (f32[2,1024]{1,0:T(2,128)}, f32[2,1024]{1,0:T(2,128)S(1)}, u32[]{:S(2)}) copy-start(f32[2,1024]{1,0:T(2,128)S(1)} %reshape.401) | copy-start | bytes 24580
  (25 other events, 75.6 us)

commit v4 on v3

--- a/solution.py
+++ b/solution.py
@@ -218,9 +218,10 @@
 
 def forward_kernel(
     n_seq, n_head, head_cols,
-    x_ref, vf_ref, wt_ref, gains_ref, cos_ref, sin_ref, first_ref,
-    x_out, h_one, q_out, k_out, v_out, att_out, lse_out, w_a, w_b, middle, h_two,
-    vf_all, away, back, sems, z_recv, v_recv, own_sems,
+    x_ref, vf_ref, wt_ref, g_ref, gains_ref, cos_ref, sin_ref, first_ref, live_ref,
+    x_res, h_one_res, q_res, k_res, v_res, att_res, lse_out, w_a_res, w_b, middle_res, h_two_res, g_res, e_res,
+    x_out, h_one, q_out, k_out, v_out, att_out, w_a, middle, h_two, g_out, e_all,
+    vf_all, away, back, sems, z_recv, v_recv, own_sems, res_sems,
 ):
     slots, rows, width = x_ref.shape
     part = wt_ref.shape[1]
@@ -250,6 +251,10 @@
         to = place.at_slot(k)
         return remote(("x", k), x_ref.at[to], x_out.at[place.slot], place.device(slot=to))
 
+    def g_copy(k):
+        to = place.at_slot(k)
+        return remote(("g", k), g_ref.at[to], g_out.at[place.slot], place.device(slot=to))
+
     def v_copy(k):
         to = place.at_slot(k)
         return remote(("v", k), vf_ref.at[to], vf_all.at[place.slot], place.device(slot=to),
@@ -366,24 +371,39 @@
         where = ref.at[position(p, place.rank), :]
         return remote((name, p, j), where, where, place.device(rank=(place.rank + j) % ranks))
 
+    results = {
+        "x": (x_out, x_res), "h1": (h_one, h_one_res), "q": (q_out, q_res), "k": (k_out, k_res),
+        "v": (v_out, v_res), "att": (att_out, att_res), "a": (w_a, w_a_res),
+        "mid": (middle, middle_res), "h2": (h_two, h_two_res), "g": (g_out, g_res),
+        "e": (e_all, e_res),
+    }
+
+    def result(name):
+        src, dst = results[name]
+        return pltpu.make_async_copy(src, dst, res_sems.at[list(results).index(name)])
+
     place.greet(True)
-    for k in (2, 3, 1):
-        x_copy(k).start()
     own = [
         pltpu.make_async_copy(x_ref.at[slot], x_out.at[slot], own_sems.at[0]),
         pltpu.make_async_copy(wt_ref.at[sections["a"][1]], w_a.at[0, :, mine], own_sems.at[1]),
         pltpu.make_async_copy(wt_ref.at[sections["b"][1]], w_b.at[0, :, mine], own_sems.at[2]),
         pltpu.make_async_copy(vf_ref.at[slot], vf_all.at[slot], own_sems.at[3]),
+        pltpu.make_async_copy(g_ref.at[slot], g_out.at[slot], own_sems.at[4]),
     ]
+    for sec in ("a", "b"):
+        for copy in near_copy(sec, 0):
+            copy.start()
+        z_start_own(sec)
+    for k in (2, 3, 1):
+        x_copy(k).start()
     for copy in own:
         copy.start()
-    z_start_own("a")
-    for copy in near_copy("a", 0):
-        copy.start()
     xy_event("a", 0)
-    for copy in near_copy("b", 0):
-        copy.start()
     z_event("a", 1)
+    xy_event("b", 0)
+    z_event("a", 2)
+    xy_event("a", 1)
+    z_event("b", 1)
     for k in range(1, slots):
         x_copy(k).wait_recv()
     own[0].wait()
@@ -396,39 +416,39 @@
         h_one[position(p, place.rank), :] = (normed * gains_ref[0:1, :]).astype(BF16)
         for j in range(1, ranks):
             share("h1", h_one, p, j).start()
-    xy_event("a", 1)
-    z_event("a", 2)
-    z_start_own("b")
+    xy_event("a", 2)
+    z_event("b", 2)
+    xy_event("b", 1)
+    z_event("a", 3)
     own[1].wait()
     own[3].wait()
     done_event("a", 0)
     for p in range(slots):
         for j in range(1, ranks):
             share("h1", h_one, p, j).wait_recv()
+    result("x").start()
+    result("h1").start()
+
+    def g_event():
+        for k in range(1, slots):
+            g_copy(k).start()
+
     events = {
-        (0, 1): [lambda: xy_event("a", 2)],
-        (0, 3): [lambda: z_event("a", 3)],
+        (0, 1): [lambda: xy_event("a", 3)],
+        (0, 3): [lambda: z_event("b", 3), g_event],
         (1, 0): [lambda: done_event("a", 1)],
-        (1, 1): [lambda: xy_event("b", 0)],
-        (1, 2): [lambda: xy_event("a", 3)],
-        (1, 3): [lambda: z_event("b", 1)],
+        (1, 3): [lambda: xy_event("b", 2)],
         (2, 0): [lambda: done_event("a", 2)],
-        (2, 1): [lambda: z_event("b", 2)],
-        (2, 3): [lambda: xy_event("b", 1)],
         (3, 0): [lambda: done_event("a", 3)],
-        (3, 1): [lambda: z_event("b", 3)],
-        (3, 3): [lambda: xy_event("b", 2)],
     }
     if per > 1:
-        xy_event("a", 2)
-        z_event("a", 3)
         xy_event("a", 3)
-        xy_event("b", 0)
+        z_event("b", 3)
+        g_event()
+        xy_event("b", 2)
         for step in range(1, slots):
             done_event("a", step)
             v_wait(place.source(step))
-            z_event("b", step)
-            xy_event("b", step)
         events = {}
 
     def one_pair_of_heads(j, carry):
@@ -488,6 +508,8 @@
         return carry
 
     lax.fori_loop(0, pairs, one_pair_of_heads, 0)
+    for name in ("q", "k", "v", "att", "a"):
+        result(name).start()
 
     w_o = w_a[:, 3 * head_cols :, :].reshape(slots * head_cols, width)
 
@@ -500,8 +522,6 @@
             at = position(p, (place.rank + j) % ranks)
             away[j - 1, p] = dot_nn(att_out[at, :], w_o).astype(BF16)
             away_copy(p, j).start()
-    if per == 1:
-        xy_event("b", 3)
     for p in range(slots):
         middle[p] = x_out[p].astype(F32) + dot_nn(att_out[position(p, place.rank), :], w_o)
     for p in range(slots):
@@ -514,11 +534,27 @@
         h_two[position(p, place.rank), :] = (normed * gains_ref[1:2, :]).astype(BF16)
         for j in range(1, ranks):
             share("h2", h_two, p, j).start()
+    result("mid").start()
+    own[4].wait()
+    for k in range(1, slots):
+        g_copy(k).wait_recv()
+    result("g").start()
+    for p in range(slots):
+        e_all[position(p, place.rank), :] = (g_out[p].astype(F32) * live_ref[...]).astype(BF16)
+        for j in range(1, ranks):
+            share("e", e_all, p, j).start()
     for p in range(slots):
         for j in range(1, ranks):
             share("h2", h_two, p, j).wait_recv()
+            share("e", e_all, p, j).wait_recv()
+            share("e", e_all, p, j).wait_send()
+    result("h2").start()
+    result("e").start()
+    xy_event("b", 3)
     for step in range(slots):
         done_event("b", step)
+    for name in results:
+        result(name).wait()
     for p in range(slots):
         for j in range(1, ranks):
             share("h1", h_one, p, j).wait_send()
@@ -527,6 +563,7 @@
     for k in range(1, slots):
         x_copy(k).wait_send()
         v_copy(k).wait_send()
+        g_copy(k).wait_send()
     for sec in ("a", "b"):
         z_own_sends(sec)
         for step in range(slots):
@@ -542,22 +579,25 @@
     own[2].wait()
 
 
-def forward_part(n_seq, n_head, head_cols, layer_input, values_first, weight_rows, gains, cos_wide, sin_wide, first_pos):
+def forward_part(
+    n_seq, n_head, head_cols, layer_input, values_first, weight_rows, out_grad, gains,
+    cos_wide, sin_wide, first_pos, live,
+):
     slots, rows, width = layer_input.shape
     all_rows, part = weight_rows.shape
     ranks = n_head // slots
     length = slots * ranks * rows
     rows_a = 4 * head_cols
     pairs = slots * head_cols // LANES
-    count = 2 * (slots - 1) + 2 * (2 + 4 * slots + slots * n_seq) + 3 * slots * ranks
+    count = 3 * (slots - 1) + 2 * (2 + 4 * slots + slots * n_seq) + 4 * slots * ranks
     any_space = pl.BlockSpec(memory_space=pl.ANY)
     vmem = pl.BlockSpec(memory_space=pltpu.VMEM)
     shape = jax.ShapeDtypeStruct
     heads = shape((pairs, length, LANES), BF16)
     return pl.pallas_call(
         functools.partial(forward_kernel, n_seq, n_head, head_cols),
-        in_specs=[any_space] * 3 + [vmem] * 4,
-        out_specs=[vmem] * 8 + [any_space] + [vmem] * 2,
+        in_specs=[any_space] * 4 + [vmem] * 5,
+        out_specs=[any_space] * 6 + [vmem] + [any_space] * 6,
         out_shape=[
             shape(layer_input.shape, BF16),
             shape((length, width), BF16),
@@ -568,20 +608,589 @@
             shape((slots, all_rows - rows_a, width), BF16),
             shape(layer_input.shape, F32),
             shape((length, width), BF16),
+            shape(layer_input.shape, BF16),
+            shape((length, width), BF16),
         ],
         scratch_shapes=[
+            pltpu.VMEM(layer_input.shape, BF16),
+            pltpu.VMEM((length, width), BF16),
+            pltpu.VMEM(heads.shape, BF16),
+            pltpu.VMEM(heads.shape, BF16),
+            pltpu.VMEM(heads.shape, BF16),
+            pltpu.VMEM((length, slots * head_cols), BF16),
+            pltpu.VMEM((slots, rows_a, width), BF16),
+            pltpu.VMEM(layer_input.shape, F32),
+            pltpu.VMEM((length, width), BF16),
+            pltpu.VMEM(layer_input.shape, BF16),
+            pltpu.VMEM((length, width), BF16),
             pltpu.VMEM(values_first.shape, BF16),
             pltpu.VMEM((ranks - 1, slots, rows, width), BF16),
             pltpu.VMEM((ranks - 1, slots, rows, width), BF16),
             pltpu.SemaphoreType.DMA((2, count)),
             pltpu.SemaphoreType.DMA((2, slots)),
             pltpu.SemaphoreType.DMA((slots,)),
-            pltpu.SemaphoreType.DMA((4,)),
+            pltpu.SemaphoreType.DMA((5,)),
+            pltpu.SemaphoreType.DMA((11,)),
         ],
         compiler_params=pltpu.CompilerParams(
             collective_id=0, has_side_effects=True, vmem_limit_bytes=60 << 20
         ),
-    )(layer_input, values_first, weight_rows, gains, cos_wide, sin_wide, first_pos[None, :])
+    )(
+        layer_input, values_first, weight_rows, out_grad, gains, cos_wide, sin_wide,
+        first_pos[None, :], live,
+    )
+
+
+def backward_kernel(
+    n_seq, n_head, head_cols,
+    wa_ref, wb_ref, h_one_ref, h_two_ref, x_ref, mid_ref, g_ref, q_ref, k_ref, v_ref, att_ref, e_ref,
+    lse_ref, gains_ref, cos_ref, sin_ref, first_ref, live_ref,
+    block_out, input_out, first_out, gains_out, sum_a, sum_b, full_a, full_b,
+    w_a, w_b, normed_all, e_all, x_own, middle, g_own, q_all, k_all, v_all, att_all,
+    acc_one, acc_two, hidden, d_gate, d_project, away, back, delta_own,
+    near_a, near_b, next_a, next_b, far_a, far_b,
+    gain_sum, gain_seq, gain_slot, gain_rank,
+    sems, near_sems, next_sems, far_sems, first_sems, load_sems, own_sems,
+):
+    slots, rows_b, width = w_b.shape
+    rows_a = w_a.shape[1]
+    ffn_cols = rows_b // 3
+    ranks = n_head // slots
+    rows = x_own.shape[1]
+    length = slots * ranks * rows
+    part = width // n_seq
+    place = Place(n_seq, n_head, slots)
+    slot = place.slot
+    beside, across = place.beside, place.across
+    corner = 3 - place.seq
+    mine = lanes(place.seq, part)
+    other = 1 - place.rank
+    elsewhere = place.device(seq=beside)
+    ids = {}
+    sections = {
+        "a": (0, w_a, near_a, next_a, far_a, sum_a, full_a, 128),
+        "b": (1, w_b, near_b, next_b, far_b, sum_b, full_b, rows_b // 6),
+    }
+
+    def remote(name, src, dst, device, send=None, recv=None):
+        if send is None:
+            i = ids.setdefault(name, len(ids))
+            send, recv = sems.at[0, i], sems.at[1, i]
+        return pltpu.make_async_remote_copy(
+            src_ref=src, dst_ref=dst, send_sem=send, recv_sem=recv,
+            device_id=device, device_id_type=MESH,
+        )
+
+    def position(p, rank):
+        return pl.ds(pl.multiple_of((p * ranks + rank) * rows, rows), rows)
+
+    def halves(sec):
+        half = sections[sec][1].shape[1] // 2
+        return pl.ds(0, half), pl.ds(half, half)
+
+    def near_copies(sec, k):
+        i, grads, near = sections[sec][:3]
+        upper, lower = halves(sec)
+        plan = (
+            (upper, beside, beside), (upper, corner, beside),
+            (lower, across, across), (lower, corner, across),
+        )
+        return [
+            remote(None, grads.at[k, cut, lanes(quarter, part)], near.at[k, n],
+                   place.device(seq=to), near_sems.at[0, i, k, n], near_sems.at[1, i, k, n])
+            for n, (cut, quarter, to) in enumerate(plan)
+        ]
+
+    def next_copies(sec, k):
+        i, grads, _, then = sections[sec][:4]
+        upper, lower = halves(sec)
+        plan = ((upper, across), (lower, beside))
+        return [
+            remote(None, grads.at[k, cut, lanes(to, part)], then.at[k, n],
+                   place.device(seq=to), next_sems.at[0, i, k, n], next_sems.at[1, i, k, n])
+            for n, (cut, to) in enumerate(plan)
+        ]
+
+    def far_copy(sec, k):
+        i, grads = sections[sec][:2]
+        far = sections[sec][4]
+        return remote(None, grads.at[k, :, mine], far.at[slot], place.device(slot=place.source(k)),
+                      far_sems.at[0, i, k], far_sems.at[1, i, slot])
+
+    def add_rows(sec, k, begin, where, addend):
+        grads, strip = sections[sec][1], sections[sec][7]
+
+        def one(i, carry):
+            at = pl.ds(pl.multiple_of(begin + i * strip, 16), strip)
+            value = grads[k, at, where].astype(F32)
+            value = value + addend[pl.ds(pl.multiple_of(i * strip, 16), strip), :].astype(F32)
+            grads[k, at, where] = value.astype(BF16)
+            return carry
+
+        lax.fori_loop(0, addend.shape[0] // strip, one, 0)
+
+    def launch(sec, k):
+        for copy in near_copies(sec, k):
+            copy.start()
+
+    def second(sec, k):
+        near = sections[sec][2]
+        half = near.shape[2]
+        came = near_copies(sec, k)
+        onward = next_copies(sec, k)
+        came[1].wait_recv()
+        add_rows(sec, k, 0, lanes(across, part), near.at[k, 1])
+        onward[0].start()
+        came[3].wait_recv()
+        add_rows(sec, k, half, lanes(beside, part), near.at[k, 3])
+        onward[1].start()
+        came[0].wait_recv()
+        add_rows(sec, k, 0, mine, near.at[k, 0])
+        came[2].wait_recv()
+        add_rows(sec, k, half, mine, near.at[k, 2])
+
+    def third(sec, k, sends):
+        then = sections[sec][3]
+        half = then.shape[2]
+        for n, copy in enumerate(next_copies(sec, k)):
+            copy.wait_recv()
+            add_rows(sec, k, n * half, mine, then.at[k, n])
+        if sends:
+            far_copy(sec, k).start()
+
+    def gather_copies(sec):
+        total, full = sections[sec][5:7]
+        half = total.shape[0] // 2
+        near = [
+            remote(("full", sec, n), total, full.at[:, mine], place.device(seq=to))
+            for n, to in enumerate((beside, across))
+        ]
+        far = []
+        for n, (source, to) in enumerate(((beside, across), (across, beside))):
+            where = full.at[pl.ds(n * half, half), lanes(source, part)]
+            far.append(remote(("relay", sec, n), where, where, place.device(seq=to)))
+        return near, far
+
+    def own_copy(sec):
+        i = sections[sec][0]
+        return pltpu.make_async_copy(
+            sections[sec][5], sections[sec][6].at[:, mine], own_sems.at[3 + i]
+        )
+
+    def finish(sec):
+        i, grads = sections[sec][:2]
+        far, total, _, strip = sections[sec][4:]
+        for j in range(1, slots):
+            source = place.at_slot(j)
+            remote(None, grads.at[0, :, mine], far.at[source], elsewhere,
+                   far_sems.at[0, i, 0], far_sems.at[1, i, source]).wait_recv()
+
+        def one(r, carry):
+            at = pl.ds(pl.multiple_of(r * strip, 16), strip)
+            value = grads[0, at, mine].astype(F32)
+            for j in range(1, slots):
+                value = value + far[place.at_slot(j), at, :].astype(F32)
+            total[at, :] = value.astype(BF16)
+            return carry
+
+        lax.fori_loop(0, total.shape[0] // strip, one, 0)
+        own_copy(sec).start()
+        for copy in gather_copies(sec)[0]:
+            copy.start()
+
+    def relay(sec):
+        near, far = gather_copies(sec)
+        for n in range(2):
+            near[n].wait_recv()
+            far[n].start()
+
+    loads = {
+        "h2": (h_two_ref, normed_all), "e": (e_ref, e_all), "h1": (h_one_ref, normed_all),
+        "a": (wa_ref, w_a), "x": (x_ref, x_own), "mid": (mid_ref, middle),
+        "g": (g_ref, g_own), "q": (q_ref, q_all), "k": (k_ref, k_all), "v": (v_ref, v_all),
+        "att": (att_ref, att_all),
+    }
+
+    def load(name):
+        src, dst = loads[name]
+        return pltpu.make_async_copy(src, dst, load_sems.at[slots + list(loads).index(name)])
+
+    def load_b(k):
+        return pltpu.make_async_copy(wb_ref.at[k], w_b.at[k], load_sems.at[k])
+
+    load_b(slots - 1).start()
+    load("h2").start()
+    load("e").start()
+    for k in reversed(range(slots - 1)):
+        load_b(k).start()
+    for name in loads:
+        if name not in ("h1", "h2", "e"):
+            load(name).start()
+    place.greet(True)
+    load("h2").wait()
+    load("e").wait()
+
+    strip = length // 2
+    key_sum, value_sum = acc_two.at[:, :LANES], acc_two.at[:, LANES : 2 * LANES]
+
+    def units(i, carry):
+        k = slots - 1 - i
+        load_b(k).wait()
+
+        def strips(n, carry):
+            at = pl.ds(pl.multiple_of(n * strip, strip), strip)
+            inner = normed_all[at, :]
+            gate = dot_nt(inner, w_b[k, :ffn_cols, :])
+            up = dot_nt(inner, w_b[k, ffn_cols : 2 * ffn_cols, :])
+            sigmoid_gate = 1.0 / (1.0 + jnp.exp(-gate))
+            activated = gate * sigmoid_gate
+            hid = (activated * up).astype(BF16)
+            hidden[at, :] = hid
+            d_hidden = dot_nt(e_all[at, :], w_b[k, 2 * ffn_cols :, :])
+            dg = (d_hidden * up * sigmoid_gate * (1.0 + gate * (1.0 - sigmoid_gate))).astype(BF16)
+            du = (d_hidden * activated).astype(BF16)
+            d_gate[at, :] = dg
+            d_project[at, :ffn_cols] = du
+            out = dot_nn(hid, w_b[k, 2 * ffn_cols :, :])
+            d_in = dot_nn(dg, w_b[k, :ffn_cols, :]) + dot_nn(du, w_b[k, ffn_cols : 2 * ffn_cols, :])
+
+            @pl.when(i == 0)
+            def _():
+                acc_one[at, :] = out
+                acc_two[at, :] = d_in
+
+            @pl.when(i > 0)
+            def _():
+                acc_one[at, :] += out
+                acc_two[at, :] += d_in
+
+            return carry
+
+        lax.fori_loop(0, length // strip, strips, 0)
+        w_b[k, 2 * ffn_cols :, :] = dot_tn(hidden[...], e_all[...]).astype(BF16)
+        w_b[k, :ffn_cols, :] = dot_tn(d_gate[...], normed_all[...]).astype(BF16)
+        w_b[k, ffn_cols : 2 * ffn_cols, :] = dot_tn(d_project[:, :ffn_cols], normed_all[...]).astype(BF16)
+        launch("b", k)
+
+        @pl.when(i > 0)
+        def _():
+            second("b", k + 1)
+
+        @pl.when(i > 1)
+        def _():
+            third("b", k + 2, True)
+
+        return carry
+
+    lax.fori_loop(0, slots, units, 0)
+    load("h1").start()
+
+    def away_copy(n, p):
+        return remote(("away", n, p), away.at[n, p], back.at[n, p], place.device(rank=other))
+
+    def share(p):
+        where = e_all.at[position(p, place.rank), :]
+        return remote(("share", p), where, where, place.device(rank=other))
+
+    for n, acc in ((1, acc_two), (0, acc_one)):
+        for p in range(slots):
+            away[n, p] = acc[position(p, other), :].astype(BF16)
+            away_copy(n, p).start()
+    for name in ("x", "mid", "g"):
+        load(name).wait()
+    live = live_ref[...]
+    gain_sum[...] = jnp.zeros_like(gain_sum)
+    for p in range(slots):
+        value = middle[p]
+        inverse = lax.rsqrt(jnp.mean(value * value, axis=-1, keepdims=True) + EPSILON)
+        normed = value * inverse
+        away_copy(1, p).wait_recv()
+        d_normed = acc_two[position(p, place.rank), :] + back[1, p].astype(F32)
+        gain_sum[1:2, :] += jnp.sum(normed * d_normed, axis=0, keepdims=True)
+        delta = norm_back(d_normed * gains_ref[1:2, :], normed, inverse)
+        away_copy(0, p).wait_recv()
+        out = acc_one[position(p, place.rank), :] + back[0, p].astype(F32)
+        delta_own[p] = ((value - x_own[p].astype(F32) + out) * live).astype(BF16)
+        middle[p] = delta
+        e_all[position(p, place.rank), :] = (g_own[p].astype(F32) * live + delta).astype(BF16)
+        share(p).start()
+
+    def swap(name, src, dst):
+        return [
+            remote((name, j), src.at[place.at_slot(j)], dst.at[slot],
+                   place.device(slot=place.at_slot(j)))
+            for j in (2, 3, 1)
+        ]
+
+    def keep(n, src, dst):
+        return pltpu.make_async_copy(src, dst.at[slot], own_sems.at[n])
+
+    for copy in swap("block", delta_own, block_out):
+        copy.start()
+    keep(0, delta_own.at[slot], block_out).start()
+    for name in ("a", "h1", "q", "k", "v", "att"):
+        load(name).wait()
+    for p in range(slots):
+        share(p).wait_recv()
+
+    def first_copy(k):
+        return remote(None, v_all.at[k], first_out.at[slot],
+                      place.device(slot=place.source(k)),
+                      first_sems.at[0, k], first_sems.at[1, slot])
+
+    def heads(i, carry):
+        k = slots - 1 - i
+        lane = lanes(k, LANES)
+        d_att = dot_nt(e_all[...], w_a[k, 3 * head_cols :, :]).astype(BF16)
+        product = (d_att.astype(F32) * att_all[:, lane].astype(F32)).T
+        inner = [
+            jnp.sum(product[:64], axis=0, keepdims=True),
+            jnp.sum(product[64:], axis=0, keepdims=True),
+        ]
+        key_sum[...] = jnp.zeros_like(key_sum)
+        value_sum[...] = jnp.zeros_like(value_sum)
+        k_turned = k_all[k].T
+        for step in range(length // BLOCK):
+            begin, keys = step * BLOCK, (step + 1) * BLOCK
+            queries = two_heads(q_all[k, begin:keys, :])
+            d_out = two_heads(d_att[begin:keys, :])
+            scores = dot_nt(k_all[k, :keys, :], queries)
+            log_total = jnp.concatenate(
+                [lse_ref[k, 0:1, begin:keys], lse_ref[k, 1:2, begin:keys]], axis=1
+            )
+            chances = jnp.where(seen(first_ref, begin, keys), jnp.exp(scores - log_total), 0.0)
+            d_chances = dot_nt(v_all[k, :keys, :], d_out)
+            rest = jnp.concatenate([inner[0][:, begin:keys], inner[1][:, begin:keys]], axis=1)
+            d_scores = (chances * (d_chances - rest)).astype(BF16)
+            key_sum[:keys, :] += dot_nn(d_scores, queries)
+            value_sum[:keys, :] += dot_nn(chances.astype(BF16), d_out)
+            d_query = one_pair(dot_nn(k_turned[:, :keys], d_scores), BLOCK) * 0.125
+            d_project[begin:keys, :LANES] = (
+                d_query * cos_ref[begin:keys, :] - swap_halves(d_query) * sin_ref[begin:keys, :]
+            ).astype(BF16)
+        d_key = key_sum[...]
+        d_project[:, LANES : 2 * LANES] = (
+            d_key * cos_ref[...] - swap_halves(d_key) * sin_ref[...]
+        ).astype(BF16)
+        d_value = (0.5 * value_sum[...]).astype(BF16)
+        d_project[:, 2 * LANES :] = d_value
+        v_all[k] = d_value
+
+        @pl.when(k > 0)
+        def _():
+            first_copy(k).start()
+
+        @pl.when(k == 0)
+        def _():
+            keep(2, v_all.at[0], first_out).start()
+
+        for n in range(2):
+            at = pl.ds(n * strip, strip)
+            d_in = dot_nn(d_project[at, :], w_a[k, : 3 * head_cols, :])
+
+            @pl.when(i == 0)
+            def _():
+                acc_one[at, :] = d_in
+
+            @pl.when(i > 0)
+            def _():
+                acc_one[at, :] += d_in
+
+        w_a[k, : 3 * head_cols, :] = dot_tn(d_project[...], normed_all[...]).astype(BF16)
+        w_a[k, 3 * head_cols :, :] = dot_tn(att_all[:, lane], e_all[...]).astype(BF16)
+        launch("a", k)
+
+        @pl.when(i == 0)
+        def _():
+            second("b", 0)
+            third("b", 1, True)
+
+        @pl.when(i == 1)
+        def _():
+            third("b", 0, False)
+            second("a", 3)
+
+        @pl.when(i == 2)
+        def _():
+            second("a", 2)
+            third("a", 3, True)
+
+        @pl.when(i == 3)
+        def _():
+            finish("b")
+            second("a", 1)
+            third("a", 2, True)
+
+        return carry
+
+    lax.fori_loop(0, slots, heads, 0)
+
+    for copy in swap("block", delta_own, block_out):
+        copy.wait_send()
+    keep(0, delta_own.at[slot], block_out).wait()
+    for p in range(slots):
+        away_copy(0, p).wait_send()
+        away[0, p] = acc_one[position(p, other), :].astype(BF16)
+        remote(("again", p), away.at[0, p], back.at[0, p], place.device(rank=other)).start()
+    for p in range(slots):
+        value = x_own[p].astype(F32)
+        inverse = lax.rsqrt(jnp.mean(value * value, axis=-1, keepdims=True) + EPSILON)
+        normed = value * inverse
+        remote(("again", p), away.at[0, p], back.at[0, p], place.device(rank=other)).wait_recv()
+        d_normed = acc_one[position(p, place.rank), :] + back[0, p].astype(F32)
+        gain_sum[0:1, :] += jnp.sum(normed * d_normed, axis=0, keepdims=True)
+        delta = norm_back(d_normed * gains_ref[0:1, :], normed, inverse)
+        delta_own[p] = ((middle[p] + delta) * live).astype(BF16)
+    for copy in swap("input", delta_own, input_out):
+        copy.start()
+    keep(1, delta_own.at[slot], input_out).start()
+
+    def gain_copies(level):
+        if level == 0:
+            return [
+                remote(("gain", 0, d), gain_seq.at[place.seq], gain_seq.at[place.seq],
+                       place.device(seq=place.at_seq(d)))
+                for d in range(1, n_seq)
+            ]
+        if level == 1:
+            return [
+                remote(("gain", 1, j), gain_slot.at[slot], gain_slot.at[slot],
+                       place.device(slot=place.at_slot(j)))
+                for j in range(1, slots)
+            ]
+        return [
+            remote(("gain", 2, 0), gain_rank.at[place.rank], gain_rank.at[place.rank],
+                   place.device(rank=other))
+        ]
+
+    def gain_step(level):
+        value = gain_sum[...]
+        if level > 0:
+            for copy in gain_copies(level - 1):
+                copy.wait_recv()
+            held = (gain_seq, gain_slot, gain_rank)[level - 1]
+            value = held[0]
+            for j in range(1, held.shape[0]):
+                value = value + held[j]
+        if level == 3:
+            gains_out[...] = value
+            return
+        target = (gain_seq, gain_slot, gain_rank)[level]
+        target[(place.seq, slot, place.rank)[level]] = value
+        for copy in gain_copies(level):
+            copy.start()
+
+    gain_step(0)
+    relay("b")
+    second("a", 0)
+    gain_step(1)
+    third("a", 1, True)
+    gain_step(2)
+    third("a", 0, False)
+    gain_step(3)
+    finish("a")
+    relay("a")
+    for sec in ("b", "a"):
+        near, far = gather_copies(sec)
+        for copy in far:
+            copy.wait_recv()
+            copy.wait_send()
+        for copy in near:
+            copy.wait_send()
+        own_copy(sec).wait()
+        for k in range(slots):
+            for copy in near_copies(sec, k) + next_copies(sec, k):
+                copy.wait_send()
+            if k > 0:
+                far_copy(sec, k).wait_send()
+    for copy in swap("block", delta_own, block_out):
+        copy.wait_recv()
+    for copy in swap("input", delta_own, input_out):
+        copy.wait()
+    for j in range(1, slots):
+        source = place.at_slot(j)
+        remote(None, v_all.at[0], first_out.at[source], elsewhere,
+               first_sems.at[0, 0], first_sems.at[1, source]).wait_recv()
+        first_copy(j).wait_send()
+    for p in range(slots):
+        away_copy(1, p).wait_send()
+        remote(("again", p), away.at[0, p], back.at[0, p], place.device(rank=other)).wait_send()
+        share(p).wait_send()
+    for level in range(3):
+        for copy in gain_copies(level):
+            copy.wait_send()
+    keep(1, delta_own.at[slot], input_out).wait()
+    keep(2, v_all.at[0], first_out).wait()
+
+
+def backward_part(n_seq, n_head, head_cols, saved, gains, tables, live):
+    (
+        x_own, h_one, q_rot, k_rot, v_mix, attended, log_total, weights_a, weights_b, middle, h_two,
+        grad_own, e_all,
+    ) = saved
+    cos_wide, sin_wide, first_pos = tables
+    slots, rows, width = x_own.shape
+    length = h_one.shape[0]
+    rows_a, rows_b = weights_a.shape[1], weights_b.shape[1]
+    part = width // n_seq
+    ranks = n_head // slots
+    any_space = pl.BlockSpec(memory_space=pl.ANY)
+    vmem = pl.BlockSpec(memory_space=pltpu.VMEM)
+    shape = jax.ShapeDtypeStruct
+    like = lambda value: pltpu.VMEM(value.shape, value.dtype)
+    count = 2 * 4 + 2 * slots + slots + 2 * (slots - 1) + n_seq + slots + 4
+    sem = pltpu.SemaphoreType.DMA
+    return pl.pallas_call(
+        functools.partial(backward_kernel, n_seq, n_head, head_cols),
+        in_specs=[any_space] * 12 + [vmem] * 6,
+        out_specs=[any_space] * 3 + [vmem] * 3 + [any_space] * 2,
+        out_shape=[
+            shape(x_own.shape, BF16),
+            shape(x_own.shape, BF16),
+            shape((slots, length, head_cols), BF16),
+            shape((8, width), F32),
+            shape((rows_a, part), BF16),
+            shape((rows_b, part), BF16),
+            shape((rows_a, width), BF16),
+            shape((rows_b, width), BF16),
+        ],
+        scratch_shapes=[
+            like(weights_a), like(weights_b), like(h_two), like(e_all), like(x_own), like(middle),
+            like(grad_own),
+            like(q_rot), like(k_rot), like(v_mix), like(attended),
+            pltpu.VMEM((length, width), F32),
+            pltpu.VMEM((length, width), F32),
+            pltpu.VMEM((length, rows_b // 3), BF16),
+            pltpu.VMEM((length, rows_b // 3), BF16),
+            pltpu.VMEM((length, 3 * LANES), BF16),
+            pltpu.VMEM((2, slots, rows, width), BF16),
+            pltpu.VMEM((2, slots, rows, width), BF16),
+            like(x_own),
+            pltpu.VMEM((slots, 4, rows_a // 2, part), BF16),
+            pltpu.VMEM((slots, 4, rows_b // 2, part), BF16),
+            pltpu.VMEM((slots, 2, rows_a // 2, part), BF16),
+            pltpu.VMEM((slots, 2, rows_b // 2, part), BF16),
+            pltpu.VMEM((slots, rows_a, part), BF16),
+            pltpu.VMEM((slots, rows_b, part), BF16),
+            pltpu.VMEM((8, width), F32),
+            pltpu.VMEM((n_seq, 8, width), F32),
+            pltpu.VMEM((slots, 8, width), F32),
+            pltpu.VMEM((ranks, 8, width), F32),
+            sem((2, count)),
+            sem((2, 2, slots, 4)),
+            sem((2, 2, slots, 2)),
+            sem((2, 2, slots)),
+            sem((2, slots)),
+            sem((slots + 11,)),
+            sem((5,)),
+        ],
+        compiler_params=pltpu.CompilerParams(
+            collective_id=2, has_side_effects=True, vmem_limit_bytes=64 << 20
+        ),
+    )(
+        weights_a, weights_b, h_one, h_two, x_own, middle, grad_own, q_rot, k_rot, v_mix, attended,
+        e_all, log_total, gains, cos_wide, sin_wide, first_pos[None, :], live,
+    )
 
 
 def reduce_kernel(
@@ -910,6 +1519,96 @@
         return self.sum_ranks(jnp.swapaxes(parts, 0, 1)).reshape(-1, full.shape[-1])
 
 
+def backward_plain(n_seq, n_head, head_cols, ffn_cols, links, saved, gains, tables, is_live):
+    (
+        x_bf16, h_one, q_rot, k_rot, v_mix, attended, log_total, weights_a, weights_b, middle,
+        h_two, grad_own, d_ffn,
+    ) = saved
+    cos_wide, sin_wide, first_pos = tables
+    slots, rows, width = x_bf16.shape
+    length = h_one.shape[0]
+    rows_a, rows_b = weights_a.shape[1], weights_b.shape[1]
+    pairs = slots * head_cols // LANES
+    per = LANES // head_cols
+
+    def pair_major(value):
+        n = value.shape[2]
+        value = value.reshape(pairs, per, length, n, head_cols)
+        return value.transpose(0, 2, 3, 1, 4).reshape(pairs, length, n, LANES)
+
+    def slot_major(value):
+        n = value.shape[2]
+        value = value.reshape(pairs, length, n, per, head_cols)
+        return value.transpose(0, 3, 1, 2, 4).reshape(slots, length, n, head_cols)
+
+    w_in, w_o = weights_a[:, : 3 * head_cols], weights_a[:, 3 * head_cols :]
+    w_gu, w_d = weights_b[:, : 2 * ffn_cols], weights_b[:, 2 * ffn_cols :]
+    x_own = x_bf16.reshape(slots * rows, width).astype(F32)
+    middle = middle.reshape(slots * rows, width)
+    ein = functools.partial(jnp.einsum, preferred_element_type=F32)
+    inverse_one = lax.rsqrt(jnp.mean(x_own * x_own, axis=-1, keepdims=True) + EPSILON)
+    normed_one = x_own * inverse_one
+    inverse_two = lax.rsqrt(jnp.mean(middle * middle, axis=-1, keepdims=True) + EPSILON)
+    normed_two = middle * inverse_two
+    saved = (q_rot, k_rot, v_mix, attended, log_total)
+    attended = jnp.swapaxes(attended.reshape(length, slots, head_cols), 0, 1)
+    gate_up = ein("ld,qfd->qlf", h_two, w_gu)
+    gate, up = gate_up[..., :ffn_cols], gate_up[..., ffn_cols:]
+    sigmoid_gate = jax.nn.sigmoid(gate)
+    activated = gate * sigmoid_gate
+    hidden = (activated * up).astype(BF16)
+    ffn_out = links.own_sum(ein("qlf,qfd->ld", hidden, w_d))
+    block_delta = jnp.where(is_live, middle - x_own + ffn_out, 0.0).astype(BF16)
+
+    d_own = jnp.where(is_live, grad_own, jnp.zeros_like(grad_own))
+    d_out = d_own.reshape(slots * rows, width).astype(F32)
+    g_down = ein("qlf,ld->qfd", hidden, d_ffn)
+    d_hidden = ein("ld,qfd->qlf", d_ffn, w_d)
+    d_gate = (
+        d_hidden * up * sigmoid_gate * (1.0 + gate * (1.0 - sigmoid_gate))
+    ).astype(BF16)
+    d_up = (d_hidden * activated).astype(BF16)
+    d_gate_up = jnp.concatenate([d_gate, d_up], axis=2)
+    d_normed_two = links.own_sum(ein("qlf,qfd->ld", d_gate_up, w_gu))
+    g_gate_up = ein("qlf,ld->qfd", d_gate_up, h_two)
+    grads_b = jnp.concatenate([g_gate_up.astype(BF16), g_down.astype(BF16)], axis=1)
+    gain_two = jnp.sum(normed_two * d_normed_two, axis=0)
+    middle_delta = norm_back(d_normed_two * gains[1], normed_two, inverse_two)
+    d_middle = d_out + middle_delta
+    d_attn = links.whole_sequence(d_middle.astype(BF16).reshape(slots, rows, width))
+    d_attended = ein("ld,qcd->qlc", d_attn, w_o).astype(BF16)
+    if per > 1:
+        d_attended = pair_major(d_attended[:, :, None])[:, :, 0]
+    d_project = jnp.concatenate(
+        attend_back(saved, d_attended, cos_wide, sin_wide, first_pos), axis=2
+    )
+    if per > 1:
+        d_project = slot_major(d_project.reshape(pairs, length, 3, LANES)).reshape(
+            slots, length, 3 * head_cols
+        )
+    d_value = d_project[:, :, 2 * head_cols :]
+    g_out = ein("qlc,ld->qcd", attended, d_attn)
+    g_qkv = ein("qlc,ld->qcd", d_project, h_one)
+    grads_a = jnp.concatenate([g_qkv.astype(BF16), g_out.astype(BF16)], axis=1)
+    d_normed_one = links.own_sum(ein("qlc,qcd->ld", d_project, w_in))
+    gain_one = jnp.sum(normed_one * d_normed_one, axis=0)
+    input_delta = middle_delta + norm_back(d_normed_one * gains[0], normed_one, inverse_one)
+    input_delta = jnp.where(is_live, input_delta, 0.0).astype(BF16)
+    gain_rows = jnp.concatenate([gain_one.reshape(8, -1), gain_two.reshape(8, -1)], axis=0)
+
+    return reduce_grads(
+        n_seq,
+        n_head,
+        (LANES, unit_chunk(rows_b)),
+        block_delta.reshape(slots, rows, width),
+        input_delta.reshape(slots, rows, width),
+        d_value,
+        gain_rows,
+        grads_a,
+        grads_b,
+    )
+
+
 def shards(
     n_seq,
     n_head,
@@ -940,16 +1639,6 @@
     per = LANES // head_cols
     rows_a, rows_b = 4 * head_cols, 3 * ffn_cols
 
-    def pair_major(value):
-        n = value.shape[2]
-        value = value.reshape(pairs, per, length, n, head_cols)
-        return value.transpose(0, 2, 3, 1, 4).reshape(pairs, length, n, LANES)
-
-    def slot_major(value):
-        n = value.shape[2]
-        value = value.reshape(pairs, length, n, per, head_cols)
-        return value.transpose(0, 3, 1, 2, 4).reshape(slots, length, n, head_cols)
-
     weight_rows = jnp.concatenate(
         [
             jnp.swapaxes(w_qkv.astype(BF16), 1, 2).reshape(3 * head_cols, row_part),
@@ -961,84 +1650,26 @@
     )
     segment_ids = lax.dynamic_index_in_dim(segments, links.slot, 0, keepdims=False)
     first_pos, cos_wide, sin_wide = position_tables(segment_ids, head_dim)
-    x_bf16, h_one, q_rot, k_rot, v_mix, attended, log_total, weights_a, weights_b, middle, h_two = (
-        forward_part(
-            n_seq, n_head, head_cols, layer_input, values_first, weight_rows, norm_gains,
-            cos_wide, sin_wide, first_pos,
+    live = jnp.full((1, width), is_live, F32)
+    saved = forward_part(
+        n_seq, n_head, head_cols, layer_input, values_first, weight_rows, out_grad, norm_gains,
+        cos_wide, sin_wide, first_pos, live,
+    )
+    tables = (cos_wide, sin_wide, first_pos)
+    if n_seq == 4 and slots == 4 and links.ranks == 2 and per == 1:
+        block_got, input_got, first_got, gains, sum_a, sum_b, full_a, full_b = backward_part(
+            n_seq, n_head, head_cols, saved, norm_gains, tables, live
         )
-    )
-    w_in, w_o = weights_a[:, : 3 * head_cols], weights_a[:, 3 * head_cols :]
-    w_gu, w_d = weights_b[:, : 2 * ffn_cols], weights_b[:, 2 * ffn_cols :]
-    x_own = x_bf16.reshape(slots * rows, width).astype(F32)
-    middle = middle.reshape(slots * rows, width)
-    ein = functools.partial(jnp.einsum, preferred_element_type=F32)
-    inverse_one = lax.rsqrt(jnp.mean(x_own * x_own, axis=-1, keepdims=True) + EPSILON)
-    normed_one = x_own * inverse_one
-    inverse_two = lax.rsqrt(jnp.mean(middle * middle, axis=-1, keepdims=True) + EPSILON)
-    normed_two = middle * inverse_two
-    saved = (q_rot, k_rot, v_mix, attended, log_total)
-    attended = jnp.swapaxes(attended.reshape(length, slots, head_cols), 0, 1)
-    gate_up = ein("ld,qfd->qlf", h_two, w_gu)
-    gate, up = gate_up[..., :ffn_cols], gate_up[..., ffn_cols:]
-    sigmoid_gate = jax.nn.sigmoid(gate)
-    activated = gate * sigmoid_gate
-    hidden = (activated * up).astype(BF16)
-    ffn_out = links.own_sum(ein("qlf,qfd->ld", hidden, w_d))
-    block_delta = jnp.where(is_live, middle - x_own + ffn_out, 0.0).astype(BF16)
-
-    grad_own = links.swap_slots(out_grad)
-    d_own = jnp.where(is_live, grad_own, jnp.zeros_like(grad_own))
-    d_out = d_own.reshape(slots * rows, width).astype(F32)
-    d_ffn = links.whole_sequence(d_own)
-    g_down = ein("qlf,ld->qfd", hidden, d_ffn)
-    d_hidden = ein("ld,qfd->qlf", d_ffn, w_d)
-    d_gate = (
-        d_hidden * up * sigmoid_gate * (1.0 + gate * (1.0 - sigmoid_gate))
-    ).astype(BF16)
-    d_up = (d_hidden * activated).astype(BF16)
-    d_gate_up = jnp.concatenate([d_gate, d_up], axis=2)
-    d_normed_two = links.own_sum(ein("qlf,qfd->ld", d_gate_up, w_gu))
-    g_gate_up = ein("qlf,ld->qfd", d_gate_up, h_two)
-    grads_b = jnp.concatenate([g_gate_up.astype(BF16), g_down.astype(BF16)], axis=1)
-    gain_two = jnp.sum(normed_two * d_normed_two, axis=0)
-    middle_delta = norm_back(d_normed_two * norm_gains[1], normed_two, inverse_two)
-    d_middle = d_out + middle_delta
-    d_attn = links.whole_sequence(d_middle.astype(BF16).reshape(slots, rows, width))
-    d_attended = ein("ld,qcd->qlc", d_attn, w_o).astype(BF16)
-    if per > 1:
-        d_attended = pair_major(d_attended[:, :, None])[:, :, 0]
-    d_project = jnp.concatenate(
-        attend_back(saved, d_attended, cos_wide, sin_wide, first_pos), axis=2
-    )
-    if per > 1:
-        d_project = slot_major(d_project.reshape(pairs, length, 3, LANES)).reshape(
-            slots, length, 3 * head_cols
+        gains = gains[:2]
+    else:
+        block_got, input_got, first_got, gains, sum_a, sum_b, full_a, full_b = backward_plain(
+            n_seq, n_head, head_cols, ffn_cols, links, saved, norm_gains, tables, is_live
         )
-    d_value = d_project[:, :, 2 * head_cols :]
-    g_out = ein("qlc,ld->qcd", attended, d_attn)
-    g_qkv = ein("qlc,ld->qcd", d_project, h_one)
-    grads_a = jnp.concatenate([g_qkv.astype(BF16), g_out.astype(BF16)], axis=1)
-    d_normed_one = links.own_sum(ein("qlc,qcd->ld", d_project, w_in))
-    gain_one = jnp.sum(normed_one * d_normed_one, axis=0)
-    input_delta = middle_delta + norm_back(d_normed_one * norm_gains[0], normed_one, inverse_one)
-    input_delta = jnp.where(is_live, input_delta, 0.0).astype(BF16)
-    gains = jnp.concatenate([gain_one.reshape(8, -1), gain_two.reshape(8, -1)], axis=0)
-
-    block_got, input_got, first_got, gains, sum_a, sum_b, full_a, full_b = reduce_grads(
-        n_seq,
-        n_head,
-        (LANES, unit_chunk(rows_b)),
-        block_delta.reshape(slots, rows, width),
-        input_delta.reshape(slots, rows, width),
-        d_value,
-        gains,
-        grads_a,
-        grads_b,
-    )
+        gains = gains.reshape(2, width)
     block_out = layer_input.astype(F32) + block_got.astype(F32)
     input_grad = out_grad.astype(F32) + input_got.astype(F32)
     first_grad = first_got.astype(F32)
-    grad_gains = gains.reshape(2, width)
+    grad_gains = gains
     new_gains = norm_gains - GAIN_RATE * grad_gains * lax.rsqrt(
         jnp.mean(grad_gains * grad_gains, axis=-1, keepdims=True) + EPSILON
     )

time: 517 us -> 392 us (0.76)
  matrix products: 60.3 us -> 0 us
  Pallas kernels: 383 us -> 360 us
  other arithmetic: 42.2 us -> 24.3 us
  local copies, waits for them, and re-layouts: 17.9 us -> 5.63 us
  starting transfers between devices: 6.88 us -> 0 us
    dot_general x10 -> x0, matrix products: 60.3 us -> none  [the longest x1 11.7 us: shards(): gate_up = ein('ld,qfd->qlf', h_two, w_gu)]
    pallas_call x1, Pallas kernels: 158 us -> 139 us  [forward_part(): pl.pallas_call(functools.partial(forward_kernel, n_seq, n_head, head_cols...]
    ppermute x8 -> x0, starting transfers between devices: 6.88 us -> none  [permute(): return lax.ppermute(value, AXES, pairs)]
    concatenate x3 -> x0, other arithmetic: 6.76 us -> none  [the longest x1 3.76 us: shards(): jnp.concatenate([g_gate_up.astype(BF16), g_down.astype(BF16)], axis=1)]
    pallas_call x2 -> x1, Pallas kernels: 204 us -> 201 us  [backward_part(): pl.pallas_call(functools.partial(backward_kernel, n_seq, n_head, head_col...]
  transfers between devices with their start and end apart: 8 -> 0, of which waited for: 0 -> 0; matrix products, arithmetic and copies ran while one was open for 11% -> 0% of each run, Pallas kernels for 34% -> 0%
where the time goes in v4:
time: 392 us
  Pallas kernels  360 us (92%)
  other arithmetic  24.3 us (6%)
  local copies, waits for them, and re-layouts  5.63 us (1%)
    pallas_call x1, Pallas kernels, backward_part(): pl.pallas_call(functools.partial(backward_kernel, n_seq, n_head, head_col...  201 us
    pallas_call x1, Pallas kernels, forward_part(): pl.pallas_call(functools.partial(forward_kernel, n_seq, n_head, head_cols...  139 us
    pallas_call x1, Pallas kernels, shampoo(): pl.pallas_call(shampoo_kernel, grid=(members,), in_specs=[wide, wide] + [...  21 us

profile of v4, /device:TPU:0, one launch (start us, length us, event | category | flops | bytes accessed | tf_op | source)
XLA Modules:
  0.0 391.7 jit_solution(10069399045703360040)
XLA Ops:
  1.4 0.9 compare_reduce_fusion
  4.1 0.9 convert_element_type.63
  5.1 1.0 convert_element_type.65
  6.1 1.0 convert_bitcast_fusion.1
  7.3 0.9 pad_maximum_fusion.wt_ref
  8.2 1.9 fusion
  10.1 1.8 pad_maximum_fusion.1
  12.0 138.6 %shard_map.287 = (bf16[4,128,1024]{2,1,0:T(8,128)(2,1)}, bf16[1024,1024]{1,0:T(8,128)(2,1)}, bf16[4,1024,128]{2,1,0:T(8,128)(2,1)}, bf16[4,1024,128]{2,1,0:T(8,1...) custom-call(bf16[4,128,1024]{2,1,0:T(8,128)(2,1)} %x_ref.1, ...), custom_call_target="tpu_custom_call" | custom-call | tf_op jit(solution)/shard_map/pallas_call | solution.py:597
  150.6 200.6 %shard_map.288 = (bf16[4,128,1024]{2,1,0:T(8,128)(2,1)}, bf16[4,128,1024]{2,1,0:T(8,128)(2,1)}, bf16[4,1024,128]{2,1,0:T(8,128)(2,1)}, f32[8,1024]{1,0:T(8,128)}...) custom-call(bf16[4,512,1024]{2,1,0:T(8,128)(2,1)} %get-tuple-element, ...), custom_call_target="tpu_custom_call" | custom-call | tf_op jit(solution)/shard_map/pallas_call | solution.py:1143
  351.3 1.0 multiply_reduce_fusion
  352.3 1.4 multiply_subtract_fusion.2
  353.7 1.5 slice_convert_fusion.1
  355.2 0.9 slice.46
  356.1 0.9 copy.41
  357.0 1.7 slice_convert_fusion
  358.7 1.0 slice.47
  359.7 0.9 convert_bitcast_fusion
  360.6 1.7 convert_add_fusion.1
  362.7 1.7 convert_add_fusion
  364.5 1.5 convert_element_type.71
  365.9 0.8 copy-done.1
  367.1 21.0 %shard_map.289 = (f32[6,2,256,1024]{3,2,1,0:T(8,128)}, f32[1,2,256,1024]{3,2,1,0:T(8,128)}, f32[4,2,64,64]{3,2,1,0:T(8,128)}, f32[3,2,176,176]{3,2,1,0:T(8,128)}...) custom-call(f32[7,2,256,1024]{3,2,1,0:T(8,128)} %stat_ref.1, f32[7,2,256,1024]{3,2,1,0:T(8,128)} %root_ref.1, ...), custom_call_target="tpu_custom_call" | custom-call | tf_op jit(solution)/shard_map/pallas_call | solution.py:1449
  389.1 0.8 bitcast_subtract_fusion
  390.8 1.0 sub.29
  (51 shorter events, 4.7 us)
Async XLA Ops:
  0.7 6.6 %copy-start.9 = (f32[2,256,352]{1,2,0:T(8,128)S(1)}, f32[2,256,352]{1,2,0:T(8,128)}, u32[]{:S(2)}) copy-start(f32[2,256,352]{1,2,0:T(8,128)} %param.19) | copy-start | bytes 2162692
  351.3 9.4 %copy-start.7 = (bf16[4,128,1024]{2,1,0:T(8,128)(2,1)S(1)}, bf16[4,128,1024]{2,1,0:T(8,128)(2,1)}, u32[]{:S(2)}) copy-start(bf16[4,128,1024]{2,1,0:T(8,128)(2,1)} %x_ref.1) | copy-start | bytes 3145732
  351.3 9.4 %copy-start.15 = (bf16[4,128,1024]{2,1,0:T(8,128)(2,1)S(1)}, bf16[4,128,1024]{2,1,0:T(8,128)(2,1)}, u32[]{:S(2)}) copy-start(bf16[4,128,1024]{2,1,0:T(8,128)(2,1)} %get-tuple-element.57) | copy-start | bytes 3145732
  352.3 10.0 %copy-start.17 = (f32[2,1024]{1,0:T(2,128)}, f32[2,1024]{1,0:T(2,128)S(1)}, u32[]{:S(2)}) copy-start(f32[2,1024]{1,0:T(2,128)S(1)} %get-tuple-element.72) | copy-start | bytes 24580
  360.6 1.7 copy-start.8
  360.6 2.1 copy-start.14
  362.7 1.7 copy-start.13
  362.7 3.2 copy-start.4
  362.7 3.2 copy-start.5
  362.7 3.2 copy-start.6
  364.4 1.5 copy-start
  364.4 2.3 copy-start.1
  364.4 2.6 copy-start.2
  364.5 2.6 copy-start.3
  367.1 21.0 %copy-start.16 = (f32[128,256]{1,0:T(8,128)S(1)}, f32[128,256]{1,0:T(8,128)}, u32[]{:S(2)}) copy-start(f32[128,256]{1,0:T(8,128)} %param.20) | copy-start | bytes 393220
  388.1 1.0 copy-start.11
  388.1 1.8 copy-start.12
  388.8 2.0 copy-start.10

commit v5 on v4

--- a/solution.py
+++ b/solution.py
@@ -15,7 +15,7 @@
 AXES = ("seq", "head")
 MESH = pl.DeviceIdType.MESH
 LANES = 128
-BLOCK = 256
+BLOCK = 128
 BF16 = jnp.bfloat16
 F32 = jnp.float32
 
@@ -74,12 +74,16 @@
     return kept.T
 
 
-def seen(first_ref, begin, key_count):
+def first_key(begin, length):
+    return max(0, (begin - length // 2 + 1) // BLOCK * BLOCK)
+
+
+def seen(first_ref, begin, low, key_count):
     first = first_ref[0:1, begin : begin + BLOCK]
     query = begin + lax.broadcasted_iota(jnp.int32, (1, BLOCK), 1)
     first = jnp.concatenate([first, first], axis=1)
     query = jnp.concatenate([query, query], axis=1)
-    key = lax.broadcasted_iota(jnp.int32, (key_count, 2 * BLOCK), 0)
+    key = low + lax.broadcasted_iota(jnp.int32, (key_count, 2 * BLOCK), 0)
     return (key >= first) & (key <= query)
 
 
@@ -99,19 +103,20 @@
     ]
     for step in range(length // BLOCK):
         begin, keys = step * BLOCK, (step + 1) * BLOCK
+        low = first_key(begin, length)
         queries = two_heads(qr_ref[0, begin:keys, :])
         d_out = two_heads(d_ref[0, begin:keys, :])
-        scores = dot_nt(kr_ref[0, :keys, :], queries)
+        scores = dot_nt(kr_ref[0, low:keys, :], queries)
         log_total = jnp.concatenate(
             [lse_ref[0, 0:1, begin:keys], lse_ref[0, 1:2, begin:keys]], axis=1
         )
-        chances = jnp.where(seen(first_ref, begin, keys), jnp.exp(scores - log_total), 0.0)
-        d_chances = dot_nt(vm_ref[0, :keys, :], d_out)
+        chances = jnp.where(seen(first_ref, begin, low, keys - low), jnp.exp(scores - log_total), 0.0)
+        d_chances = dot_nt(vm_ref[0, low:keys, :], d_out)
         part = jnp.concatenate([inner[0][:, begin:keys], inner[1][:, begin:keys]], axis=1)
         d_scores = (chances * (d_chances - part)).astype(BF16)
-        key_sum[:keys, :] += dot_nn(d_scores, queries)
-        value_sum[:keys, :] += dot_nn(chances.astype(BF16), d_out)
-        d_query = one_pair(dot_nn(k_turned[:, :keys], d_scores), BLOCK) * 0.125
+        key_sum[low:keys, :] += dot_nn(d_scores, queries)
+        value_sum[low:keys, :] += dot_nn(chances.astype(BF16), d_out)
+        d_query = one_pair(dot_nn(k_turned[:, low:keys], d_scores), BLOCK) * 0.125
         dq_ref[0, begin:keys, :] = (
             d_query * cosine[begin:keys] - swap_halves(d_query) * sine_part[begin:keys]
         ).astype(BF16)
@@ -217,11 +222,11 @@
 
 
 def forward_kernel(
-    n_seq, n_head, head_cols,
+    n_seq, n_head, head_cols, early,
     x_ref, vf_ref, wt_ref, g_ref, gains_ref, cos_ref, sin_ref, first_ref, live_ref,
-    x_res, h_one_res, q_res, k_res, v_res, att_res, lse_out, w_a_res, w_b, middle_res, h_two_res, g_res, e_res,
-    x_out, h_one, q_out, k_out, v_out, att_out, w_a, middle, h_two, g_out, e_all,
-    vf_all, away, back, sems, z_recv, v_recv, own_sems, res_sems,
+    x_res, h_one_res, q_res, k_res, v_res, att_res, lse_out, w_a_res, w_b_res, middle_res, h_two_res, g_res, e_res,
+    ffn_res, x_out, h_one, q_out, k_out, v_out, att_out, w_a, middle, h_two, g_out, e_all,
+    vf_all, away, back, w_b, ffn, sems, z_recv, v_recv, own_sems, res_sems,
 ):
     slots, rows, width = x_ref.shape
     part = wt_ref.shape[1]
@@ -256,7 +261,7 @@
         return remote(("g", k), g_ref.at[to], g_out.at[place.slot], place.device(slot=to))
 
     def v_copy(k):
-        to = place.at_slot(k)
+        to = place.source(k) if place.line else place.at_slot(k)
         return remote(("v", k), vf_ref.at[to], vf_all.at[place.slot], place.device(slot=to),
                       v_recv.at[place.slot])
 
@@ -375,8 +380,10 @@
         "x": (x_out, x_res), "h1": (h_one, h_one_res), "q": (q_out, q_res), "k": (k_out, k_res),
         "v": (v_out, v_res), "att": (att_out, att_res), "a": (w_a, w_a_res),
         "mid": (middle, middle_res), "h2": (h_two, h_two_res), "g": (g_out, g_res),
-        "e": (e_all, e_res),
+        "e": (e_all, e_res), "ffn": (ffn, ffn_res),
     }
+    for step in range(slots):
+        results["b", step] = (w_b.at[step], w_b_res.at[step])
 
     def result(name):
         src, dst = results[name]
@@ -390,25 +397,47 @@
         pltpu.make_async_copy(vf_ref.at[slot], vf_all.at[slot], own_sems.at[3]),
         pltpu.make_async_copy(g_ref.at[slot], g_out.at[slot], own_sems.at[4]),
     ]
+    def v_event(*steps):
+        for k in steps:
+            v_copy(k).start()
+
+    def g_event():
+        for k in range(1, slots):
+            g_copy(k).start()
+
+    def inside(kind, sec, step):
+        @pl.when(inner == 1)
+        def _():
+            kind(sec, step)
+
+    def outside(kind, sec, step):
+        @pl.when(inner == 0)
+        def _():
+            kind(sec, step)
+
+    z_start_own("a")
+    if place.line:
+        z_start_own("b")
+    for k in (2, 3, 1):
+        x_copy(k).start()
+    v_event(1)
     for sec in ("a", "b"):
         for copy in near_copy(sec, 0):
             copy.start()
-        z_start_own(sec)
-    for k in (2, 3, 1):
-        x_copy(k).start()
     for copy in own:
         copy.start()
+    z_event("a", 1)
+    if place.line:
+        inside(z_event, "a", 2)
+        z_event("b", 1)
+        inside(z_event, "b", 2)
+        v_event(2, 3)
     xy_event("a", 0)
-    z_event("a", 1)
     xy_event("b", 0)
-    z_event("a", 2)
     xy_event("a", 1)
-    z_event("b", 1)
     for k in range(1, slots):
         x_copy(k).wait_recv()
     own[0].wait()
-    for k in range(1, slots):
-        v_copy(k).start()
 
     for p in range(slots):
         x = x_out[p].astype(F32)
@@ -416,10 +445,6 @@
         h_one[position(p, place.rank), :] = (normed * gains_ref[0:1, :]).astype(BF16)
         for j in range(1, ranks):
             share("h1", h_one, p, j).start()
-    xy_event("a", 2)
-    z_event("b", 2)
-    xy_event("b", 1)
-    z_event("a", 3)
     own[1].wait()
     own[3].wait()
     done_event("a", 0)
@@ -429,27 +454,32 @@
     result("x").start()
     result("h1").start()
 
-    def g_event():
-        for k in range(1, slots):
-            g_copy(k).start()
-
-    events = {
-        (0, 1): [lambda: xy_event("a", 3)],
-        (0, 3): [lambda: z_event("b", 3), g_event],
-        (1, 0): [lambda: done_event("a", 1)],
-        (1, 3): [lambda: xy_event("b", 2)],
-        (2, 0): [lambda: done_event("a", 2)],
-        (3, 0): [lambda: done_event("a", 3)],
-    }
-    if per > 1:
-        xy_event("a", 3)
-        z_event("b", 3)
+    if place.line:
+        events = {
+            (0, 1): [lambda: inside(z_event, "a", 3), lambda: outside(z_event, "a", 2)],
+            (0, 3): [lambda: xy_event("b", 1)],
+            (1, 0): [lambda: done_event("a", 1), lambda: v_wait(place.source(1))],
+            (1, 2): [lambda: xy_event("a", 2)],
+            (1, 3): [lambda: inside(z_event, "b", 3), lambda: outside(z_event, "b", 2)],
+            (2, 0): [lambda: done_event("a", 2), lambda: v_wait(place.source(2))],
+            (2, 1): [lambda: outside(z_event, "a", 3), lambda: inside(xy_event, "a", 3)],
+            (2, 3): [lambda: xy_event("b", 2)],
+            (3, 0): [lambda: outside(xy_event, "a", 3), lambda: done_event("a", 3), g_event,
+                     lambda: v_wait(place.source(3))],
+            (3, 3): [lambda: outside(z_event, "b", 3)],
+        }
+    else:
+        events = {}
+        z_start_own("b")
+        v_event(2, 3)
         g_event()
-        xy_event("b", 2)
+        for step in range(2, slots):
+            z_event("a", step)
+            xy_event("a", step)
         for step in range(1, slots):
-            done_event("a", step)
+            z_event("b", step)
+            xy_event("b", step)
             v_wait(place.source(step))
-        events = {}
 
     def one_pair_of_heads(j, carry):
         def pump(point):
@@ -462,9 +492,6 @@
 
         pump(0)
         if per == 1:
-            @pl.when(j > 0)
-            def _():
-                v_wait(place.source(j))
             w_in = w_a[j, : 3 * head_cols, :]
             first = vf_all[place.source(j)]
         else:
@@ -490,14 +517,15 @@
         v_turned = v_out[j].T
         for step in range(length // BLOCK):
             begin, keys = step * BLOCK, (step + 1) * BLOCK
+            low = first_key(begin, length)
             queries = two_heads(q_out[j, begin:keys, :])
-            scores = dot_nt(k_out[j, :keys, :], queries)
-            scores = jnp.where(seen(first_ref, begin, keys), scores, -1e30)
+            scores = dot_nt(k_out[j, low:keys, :], queries)
+            scores = jnp.where(seen(first_ref, begin, low, keys - low), scores, -1e30)
             top = jnp.max(scores, axis=0, keepdims=True)
             exps = jnp.exp(scores - top)
             total = jnp.sum(exps, axis=0, keepdims=True)
             chances = (exps * (1.0 / total)).astype(BF16)
-            attended = dot_nn(v_turned[:, :keys], chances)
+            attended = dot_nn(v_turned[:, low:keys], chances)
             att_out[begin:keys, lanes(j, LANES)] = one_pair(attended, BLOCK).astype(BF16)
             log_total = top + jnp.log(total)
             lse_out[j, 0:1, begin:keys] = log_total[:, :BLOCK]
@@ -535,6 +563,40 @@
         for j in range(1, ranks):
             share("h2", h_two, p, j).start()
     result("mid").start()
+    for p in range(slots):
+        for j in range(1, ranks):
+            share("h2", h_two, p, j).wait_recv()
+    result("h2").start()
+
+    units = (w_b.shape[1]) // 3
+    strip = length // 2
+
+    def feed(k):
+        def strips(n, carry):
+            at = pl.ds(pl.multiple_of(n * strip, strip), strip)
+            gate = dot_nt(h_two[at, :], w_b[k, :units, :])
+            up = dot_nt(h_two[at, :], w_b[k, units : 2 * units, :])
+            hid = (gate * (1.0 / (1.0 + jnp.exp(-gate))) * up).astype(BF16)
+            out = dot_nn(hid, w_b[k, 2 * units :, :])
+            if k == 0:
+                ffn[at, :] = out
+            else:
+                ffn[at, :] += out
+            return carry
+
+        lax.fori_loop(0, length // strip, strips, 0)
+
+    own[2].wait()
+    for step in range(slots - 1):
+        done_event("b", step)
+        result(("b", step)).start()
+        if early:
+            feed(step)
+        if step == 1 and place.line:
+            xy_event("b", 3)
+    if not early:
+        ffn[0:8, :] = jnp.zeros((8, width), F32)
+    result("ffn").start()
     own[4].wait()
     for k in range(1, slots):
         g_copy(k).wait_recv()
@@ -545,14 +607,11 @@
             share("e", e_all, p, j).start()
     for p in range(slots):
         for j in range(1, ranks):
-            share("h2", h_two, p, j).wait_recv()
             share("e", e_all, p, j).wait_recv()
             share("e", e_all, p, j).wait_send()
-    result("h2").start()
     result("e").start()
-    xy_event("b", 3)
-    for step in range(slots):
-        done_event("b", step)
+    done_event("b", slots - 1)
+    result(("b", slots - 1)).start()
     for name in results:
         result(name).wait()
     for p in range(slots):
@@ -576,12 +635,11 @@
                     @pl.when(inner == 1)
                     def _(sec=sec, step=step):
                         z_relay(sec, step).wait_send()
-    own[2].wait()
 
 
 def forward_part(
     n_seq, n_head, head_cols, layer_input, values_first, weight_rows, out_grad, gains,
-    cos_wide, sin_wide, first_pos, live,
+    cos_wide, sin_wide, first_pos, live, early,
 ):
     slots, rows, width = layer_input.shape
     all_rows, part = weight_rows.shape
@@ -595,9 +653,9 @@
     shape = jax.ShapeDtypeStruct
     heads = shape((pairs, length, LANES), BF16)
     return pl.pallas_call(
-        functools.partial(forward_kernel, n_seq, n_head, head_cols),
+        functools.partial(forward_kernel, n_seq, n_head, head_cols, early),
         in_specs=[any_space] * 4 + [vmem] * 5,
-        out_specs=[any_space] * 6 + [vmem] + [any_space] * 6,
+        out_specs=[any_space] * 6 + [vmem] + [any_space] * 7,
         out_shape=[
             shape(layer_input.shape, BF16),
             shape((length, width), BF16),
@@ -610,6 +668,7 @@
             shape((length, width), BF16),
             shape(layer_input.shape, BF16),
             shape((length, width), BF16),
+            shape((length if early else 8, width), F32),
         ],
         scratch_shapes=[
             pltpu.VMEM(layer_input.shape, BF16),
@@ -626,11 +685,13 @@
             pltpu.VMEM(values_first.shape, BF16),
             pltpu.VMEM((ranks - 1, slots, rows, width), BF16),
             pltpu.VMEM((ranks - 1, slots, rows, width), BF16),
+            pltpu.VMEM((slots, all_rows - rows_a, width), BF16),
+            pltpu.VMEM((length if early else 8, width), F32),
             pltpu.SemaphoreType.DMA((2, count)),
             pltpu.SemaphoreType.DMA((2, slots)),
             pltpu.SemaphoreType.DMA((slots,)),
             pltpu.SemaphoreType.DMA((5,)),
-            pltpu.SemaphoreType.DMA((11,)),
+            pltpu.SemaphoreType.DMA((12 + slots,)),
         ],
         compiler_params=pltpu.CompilerParams(
             collective_id=0, has_side_effects=True, vmem_limit_bytes=60 << 20
@@ -644,6 +705,7 @@
 def backward_kernel(
     n_seq, n_head, head_cols,
     wa_ref, wb_ref, h_one_ref, h_two_ref, x_ref, mid_ref, g_ref, q_ref, k_ref, v_ref, att_ref, e_ref,
+    ffn_ref,
     lse_ref, gains_ref, cos_ref, sin_ref, first_ref, live_ref,
     block_out, input_out, first_out, gains_out, sum_a, sum_b, full_a, full_b,
     w_a, w_b, normed_all, e_all, x_own, middle, g_own, q_all, k_all, v_all, att_all,
@@ -711,11 +773,23 @@
             for n, (cut, to) in enumerate(plan)
         ]
 
+    upper = slot // 2
+    inner = (slot + upper) % 2
+    toward = 1 - 2 * upper
+
     def far_copy(sec, k):
         i, grads = sections[sec][:2]
         far = sections[sec][4]
-        return remote(None, grads.at[k, :, mine], far.at[slot], place.device(slot=place.source(k)),
-                      far_sems.at[0, i, k], far_sems.at[1, i, slot])
+        to = slot + toward * (1 - 2 * inner * (1 - k // 2))
+        landing = inner * (4 - 3 * (k // 3)) + (1 - inner) * ((k // 2) * k)
+        return remote(None, grads.at[k, :, mine], far.at[landing], place.device(slot=to),
+                      far_sems.at[0, i, k], far_sems.at[1, i, landing])
+
+    def far_wait(sec, landing):
+        i, grads = sections[sec][:2]
+        far = sections[sec][4]
+        remote(None, grads.at[0, :, mine], far.at[landing], elsewhere,
+               far_sems.at[0, i, 0], far_sems.at[1, i, landing]).wait_recv()
 
     def add_rows(sec, k, begin, where, addend):
         grads, strip = sections[sec][1], sections[sec][7]
@@ -756,6 +830,15 @@
             copy.wait_recv()
             add_rows(sec, k, n * half, mine, then.at[k, n])
         if sends:
+            @pl.when(inner == 0)
+            def _():
+                far_copy(sec, k).start()
+
+    def fourth(sec, k):
+        @pl.when(inner == 1)
+        def _():
+            far_wait(sec, k)
+            add_rows(sec, k, 0, mine, sections[sec][4].at[k])
             far_copy(sec, k).start()
 
     def gather_copies(sec):
@@ -778,18 +861,19 @@
         )
 
     def finish(sec):
-        i, grads = sections[sec][:2]
+        grads = sections[sec][1]
         far, total, _, strip = sections[sec][4:]
-        for j in range(1, slots):
-            source = place.at_slot(j)
-            remote(None, grads.at[0, :, mine], far.at[source], elsewhere,
-                   far_sems.at[0, i, 0], far_sems.at[1, i, source]).wait_recv()
+
+        @pl.when(inner == 1)
+        def _():
+            far_wait(sec, 0)
+            add_rows(sec, 0, 0, mine, far.at[0])
+
+        far_wait(sec, 4)
 
         def one(r, carry):
             at = pl.ds(pl.multiple_of(r * strip, 16), strip)
-            value = grads[0, at, mine].astype(F32)
-            for j in range(1, slots):
-                value = value + far[place.at_slot(j), at, :].astype(F32)
+            value = grads[0, at, mine].astype(F32) + far[4, at, :].astype(F32)
             total[at, :] = value.astype(BF16)
             return carry
 
@@ -806,6 +890,7 @@
 
     loads = {
         "h2": (h_two_ref, normed_all), "e": (e_ref, e_all), "h1": (h_one_ref, normed_all),
+        "ffn": (ffn_ref, acc_one),
         "a": (wa_ref, w_a), "x": (x_ref, x_own), "mid": (mid_ref, middle),
         "g": (g_ref, g_own), "q": (q_ref, q_all), "k": (k_ref, k_all), "v": (v_ref, v_all),
         "att": (att_ref, att_all),
@@ -821,17 +906,52 @@
     load_b(slots - 1).start()
     load("h2").start()
     load("e").start()
+    load("ffn").start()
+    load("x").start()
+    load("mid").start()
     for k in reversed(range(slots - 1)):
         load_b(k).start()
     for name in loads:
-        if name not in ("h1", "h2", "e"):
+        if name not in ("h1", "h2", "e", "ffn", "x", "mid"):
             load(name).start()
     place.greet(True)
     load("h2").wait()
     load("e").wait()
+    load("ffn").wait()
 
     strip = length // 2
     key_sum, value_sum = acc_two.at[:, :LANES], acc_two.at[:, LANES : 2 * LANES]
+
+    def away_copy(n, p):
+        return remote(("away", n, p), away.at[n, p], back.at[n, p], place.device(rank=other))
+
+    def swap(name, src, dst):
+        return [
+            remote((name, j), src.at[place.at_slot(j)], dst.at[slot],
+                   place.device(slot=place.at_slot(j)))
+            for j in (2, 3, 1)
+        ]
+
+    def keep(n, src, dst):
+        return pltpu.make_async_copy(src, dst.at[slot], own_sems.at[n])
+
+    def send_away(n, acc):
+        for p in range(slots):
+            away[n, p] = acc[position(p, other), :].astype(BF16)
+            away_copy(n, p).start()
+
+    live = live_ref[...]
+
+    def block_delta():
+        load("x").wait()
+        load("mid").wait()
+        for p in range(slots):
+            away_copy(0, p).wait_recv()
+            out = acc_one[position(p, place.rank), :] + back[0, p].astype(F32)
+            delta_own[p] = ((middle[p] - x_own[p].astype(F32) + out) * live).astype(BF16)
+        for copy in swap("block", delta_own, block_out):
+            copy.start()
+        keep(0, delta_own.at[slot], block_out).start()
 
     def units(i, carry):
         k = slots - 1 - i
@@ -851,17 +971,15 @@
             du = (d_hidden * activated).astype(BF16)
             d_gate[at, :] = dg
             d_project[at, :ffn_cols] = du
-            out = dot_nn(hid, w_b[k, 2 * ffn_cols :, :])
             d_in = dot_nn(dg, w_b[k, :ffn_cols, :]) + dot_nn(du, w_b[k, ffn_cols : 2 * ffn_cols, :])
 
             @pl.when(i == 0)
             def _():
-                acc_one[at, :] = out
+                acc_one[at, :] += dot_nn(hid, w_b[k, 2 * ffn_cols :, :])
                 acc_two[at, :] = d_in
 
             @pl.when(i > 0)
             def _():
-                acc_one[at, :] += out
                 acc_two[at, :] += d_in
 
             return carry
@@ -872,6 +990,14 @@
         w_b[k, ffn_cols : 2 * ffn_cols, :] = dot_tn(d_project[:, :ffn_cols], normed_all[...]).astype(BF16)
         launch("b", k)
 
+        @pl.when(i == 0)
+        def _():
+            send_away(0, acc_one)
+
+        @pl.when(i == 1)
+        def _():
+            block_delta()
+
         @pl.when(i > 0)
         def _():
             second("b", k + 1)
@@ -885,20 +1011,12 @@
     lax.fori_loop(0, slots, units, 0)
     load("h1").start()
 
-    def away_copy(n, p):
-        return remote(("away", n, p), away.at[n, p], back.at[n, p], place.device(rank=other))
-
     def share(p):
         where = e_all.at[position(p, place.rank), :]
         return remote(("share", p), where, where, place.device(rank=other))
 
-    for n, acc in ((1, acc_two), (0, acc_one)):
-        for p in range(slots):
-            away[n, p] = acc[position(p, other), :].astype(BF16)
-            away_copy(n, p).start()
-    for name in ("x", "mid", "g"):
-        load(name).wait()
-    live = live_ref[...]
+    send_away(1, acc_two)
+    load("g").wait()
     gain_sum[...] = jnp.zeros_like(gain_sum)
     for p in range(slots):
         value = middle[p]
@@ -908,26 +1026,10 @@
         d_normed = acc_two[position(p, place.rank), :] + back[1, p].astype(F32)
         gain_sum[1:2, :] += jnp.sum(normed * d_normed, axis=0, keepdims=True)
         delta = norm_back(d_normed * gains_ref[1:2, :], normed, inverse)
-        away_copy(0, p).wait_recv()
-        out = acc_one[position(p, place.rank), :] + back[0, p].astype(F32)
-        delta_own[p] = ((value - x_own[p].astype(F32) + out) * live).astype(BF16)
         middle[p] = delta
         e_all[position(p, place.rank), :] = (g_own[p].astype(F32) * live + delta).astype(BF16)
         share(p).start()
 
-    def swap(name, src, dst):
-        return [
-            remote((name, j), src.at[place.at_slot(j)], dst.at[slot],
-                   place.device(slot=place.at_slot(j)))
-            for j in (2, 3, 1)
-        ]
-
-    def keep(n, src, dst):
-        return pltpu.make_async_copy(src, dst.at[slot], own_sems.at[n])
-
-    for copy in swap("block", delta_own, block_out):
-        copy.start()
-    keep(0, delta_own.at[slot], block_out).start()
     for name in ("a", "h1", "q", "k", "v", "att"):
         load(name).wait()
     for p in range(slots):
@@ -952,19 +1054,20 @@
         k_turned = k_all[k].T
         for step in range(length // BLOCK):
             begin, keys = step * BLOCK, (step + 1) * BLOCK
+            low = first_key(begin, length)
             queries = two_heads(q_all[k, begin:keys, :])
             d_out = two_heads(d_att[begin:keys, :])
-            scores = dot_nt(k_all[k, :keys, :], queries)
+            scores = dot_nt(k_all[k, low:keys, :], queries)
             log_total = jnp.concatenate(
                 [lse_ref[k, 0:1, begin:keys], lse_ref[k, 1:2, begin:keys]], axis=1
             )
-            chances = jnp.where(seen(first_ref, begin, keys), jnp.exp(scores - log_total), 0.0)
-            d_chances = dot_nt(v_all[k, :keys, :], d_out)
+            chances = jnp.where(seen(first_ref, begin, low, keys - low), jnp.exp(scores - log_total), 0.0)
+            d_chances = dot_nt(v_all[k, low:keys, :], d_out)
             rest = jnp.concatenate([inner[0][:, begin:keys], inner[1][:, begin:keys]], axis=1)
             d_scores = (chances * (d_chances - rest)).astype(BF16)
-            key_sum[:keys, :] += dot_nn(d_scores, queries)
-            value_sum[:keys, :] += dot_nn(chances.astype(BF16), d_out)
-            d_query = one_pair(dot_nn(k_turned[:, :keys], d_scores), BLOCK) * 0.125
+            key_sum[low:keys, :] += dot_nn(d_scores, queries)
+            value_sum[low:keys, :] += dot_nn(chances.astype(BF16), d_out)
+            d_query = one_pair(dot_nn(k_turned[:, low:keys], d_scores), BLOCK) * 0.125
             d_project[begin:keys, :LANES] = (
                 d_query * cos_ref[begin:keys, :] - swap_halves(d_query) * sin_ref[begin:keys, :]
             ).astype(BF16)
@@ -1003,23 +1106,22 @@
         @pl.when(i == 0)
         def _():
             second("b", 0)
+            fourth("b", 3)
             third("b", 1, True)
 
         @pl.when(i == 1)
         def _():
+            fourth("b", 2)
             third("b", 0, False)
-            second("a", 3)
 
         @pl.when(i == 2)
         def _():
-            second("a", 2)
-            third("a", 3, True)
+            second("a", 3)
+            fourth("b", 1)
 
         @pl.when(i == 3)
         def _():
             finish("b")
-            second("a", 1)
-            third("a", 2, True)
 
         return carry
 
@@ -1041,8 +1143,8 @@
         gain_sum[0:1, :] += jnp.sum(normed * d_normed, axis=0, keepdims=True)
         delta = norm_back(d_normed * gains_ref[0:1, :], normed, inverse)
         delta_own[p] = ((middle[p] + delta) * live).astype(BF16)
-    for copy in swap("input", delta_own, input_out):
-        copy.start()
+    input_copies = swap("input", delta_own, input_out)
+    input_copies[0].start()
     keep(1, delta_own.at[slot], input_out).start()
 
     def gain_copies(level):
@@ -1081,12 +1183,21 @@
             copy.start()
 
     gain_step(0)
+    second("a", 2)
+    third("a", 3, True)
+    input_copies[1].start()
     relay("b")
+    second("a", 1)
+    third("a", 2, True)
+    fourth("a", 3)
+    input_copies[2].start()
+    gain_step(1)
     second("a", 0)
-    gain_step(1)
     third("a", 1, True)
+    fourth("a", 2)
     gain_step(2)
     third("a", 0, False)
+    fourth("a", 1)
     gain_step(3)
     finish("a")
     relay("a")
@@ -1126,7 +1237,7 @@
 def backward_part(n_seq, n_head, head_cols, saved, gains, tables, live):
     (
         x_own, h_one, q_rot, k_rot, v_mix, attended, log_total, weights_a, weights_b, middle, h_two,
-        grad_own, e_all,
+        grad_own, e_all, ffn,
     ) = saved
     cos_wide, sin_wide, first_pos = tables
     slots, rows, width = x_own.shape
@@ -1142,7 +1253,7 @@
     sem = pltpu.SemaphoreType.DMA
     return pl.pallas_call(
         functools.partial(backward_kernel, n_seq, n_head, head_cols),
-        in_specs=[any_space] * 12 + [vmem] * 6,
+        in_specs=[any_space] * 13 + [vmem] * 6,
         out_specs=[any_space] * 3 + [vmem] * 3 + [any_space] * 2,
         out_shape=[
             shape(x_own.shape, BF16),
@@ -1170,8 +1281,8 @@
             pltpu.VMEM((slots, 4, rows_b // 2, part), BF16),
             pltpu.VMEM((slots, 2, rows_a // 2, part), BF16),
             pltpu.VMEM((slots, 2, rows_b // 2, part), BF16),
-            pltpu.VMEM((slots, rows_a, part), BF16),
-            pltpu.VMEM((slots, rows_b, part), BF16),
+            pltpu.VMEM((slots + 1, rows_a, part), BF16),
+            pltpu.VMEM((slots + 1, rows_b, part), BF16),
             pltpu.VMEM((8, width), F32),
             pltpu.VMEM((n_seq, 8, width), F32),
             pltpu.VMEM((slots, 8, width), F32),
@@ -1179,9 +1290,9 @@
             sem((2, count)),
             sem((2, 2, slots, 4)),
             sem((2, 2, slots, 2)),
-            sem((2, 2, slots)),
+            sem((2, 2, slots + 1)),
             sem((2, slots)),
-            sem((slots + 11,)),
+            sem((slots + 12,)),
             sem((5,)),
         ],
         compiler_params=pltpu.CompilerParams(
@@ -1189,7 +1300,7 @@
         ),
     )(
         weights_a, weights_b, h_one, h_two, x_own, middle, grad_own, q_rot, k_rot, v_mix, attended,
-        e_all, log_total, gains, cos_wide, sin_wide, first_pos[None, :], live,
+        e_all, ffn, log_total, gains, cos_wide, sin_wide, first_pos[None, :], live,
     )
 
 
@@ -1522,7 +1633,7 @@
 def backward_plain(n_seq, n_head, head_cols, ffn_cols, links, saved, gains, tables, is_live):
     (
         x_bf16, h_one, q_rot, k_rot, v_mix, attended, log_total, weights_a, weights_b, middle,
-        h_two, grad_own, d_ffn,
+        h_two, grad_own, d_ffn, _,
     ) = saved
     cos_wide, sin_wide, first_pos = tables
     slots, rows, width = x_bf16.shape
@@ -1651,12 +1762,13 @@
     segment_ids = lax.dynamic_index_in_dim(segments, links.slot, 0, keepdims=False)
     first_pos, cos_wide, sin_wide = position_tables(segment_ids, head_dim)
     live = jnp.full((1, width), is_live, F32)
+    fused = n_seq == 4 and slots == 4 and links.ranks == 2 and per == 1
     saved = forward_part(
         n_seq, n_head, head_cols, layer_input, values_first, weight_rows, out_grad, norm_gains,
-        cos_wide, sin_wide, first_pos, live,
+        cos_wide, sin_wide, first_pos, live, fused,
     )
     tables = (cos_wide, sin_wide, first_pos)
-    if n_seq == 4 and slots == 4 and links.ranks == 2 and per == 1:
+    if fused:
         block_got, input_got, first_got, gains, sum_a, sum_b, full_a, full_b = backward_part(
             n_seq, n_head, head_cols, saved, norm_gains, tables, live
         )

time: 392 us -> 364 us (0.929)
  Pallas kernels: 360 us -> 328 us
    pallas_call x1, Pallas kernels: 201 us -> 174 us  [backward_part(): pl.pallas_call(functools.partial(backward_kernel, n_seq, n_head, head_col...]
    pallas_call x1, Pallas kernels: 139 us -> 134 us  [forward_part(): pl.pallas_call(functools.partial(forward_kernel, n_seq, n_head, head_cols...]
where the time goes in v5:
time: 364 us; the launch traced here: 360 us
  Pallas kernels  328 us (90%)
  other arithmetic  24.3 us (7%)
  local copies, waits for them, and re-layouts  5.63 us (2%)
    pallas_call x1, Pallas kernels, backward_part(): pl.pallas_call(functools.partial(backward_kernel, n_seq, n_head, head_col...  174 us
    pallas_call x1, Pallas kernels, forward_part(): pl.pallas_call(functools.partial(forward_kernel, n_seq, n_head, head_cols...  134 us
    pallas_call x1, Pallas kernels, shampoo(): pl.pallas_call(shampoo_kernel, grid=(members,), in_specs=[wide, wide] + [...  20.8 us

profile of v5, /device:TPU:0, one launch (start us, length us, event | category | flops | bytes accessed | tf_op | source)
XLA Modules:
  0.0 360.0 jit_solution(16737832820431730979)
XLA Ops:
  1.4 0.9 compare_reduce_fusion
  4.1 0.9 convert_element_type.63
  5.1 1.0 convert_element_type.65
  6.1 1.0 convert_bitcast_fusion.1
  7.3 0.9 pad_maximum_fusion.wt_ref
  8.2 1.9 fusion
  10.1 1.8 pad_maximum_fusion.1
  12.0 134.0 %shard_map.287 = (bf16[4,128,1024]{2,1,0:T(8,128)(2,1)}, bf16[1024,1024]{1,0:T(8,128)(2,1)}, bf16[4,1024,128]{2,1,0:T(8,128)(2,1)}, bf16[4,1024,128]{2,1,0:T(8,1...) custom-call(bf16[4,128,1024]{2,1,0:T(8,128)(2,1)} %x_ref.1, ...), custom_call_target="tpu_custom_call" | custom-call | tf_op jit(solution)/shard_map/pallas_call | solution.py:655
  146.0 173.5 %shard_map.288 = (bf16[4,128,1024]{2,1,0:T(8,128)(2,1)}, bf16[4,128,1024]{2,1,0:T(8,128)(2,1)}, bf16[4,1024,128]{2,1,0:T(8,128)(2,1)}, f32[8,1024]{1,0:T(8,128)}...) custom-call(bf16[4,512,1024]{2,1,0:T(8,128)(2,1)} %get-tuple-element, ...), custom_call_target="tpu_custom_call" | custom-call | tf_op jit(solution)/shard_map/pallas_call | solution.py:1254
  319.6 1.0 multiply_reduce_fusion
  320.6 1.4 multiply_subtract_fusion.2
  322.0 1.5 slice_convert_fusion.1
  323.5 0.9 slice.46
  324.4 0.9 copy.41
  325.3 1.7 slice_convert_fusion
  327.0 1.0 slice.47
  328.0 0.9 convert_bitcast_fusion
  328.9 1.7 convert_add_fusion.1
  331.0 1.7 convert_add_fusion
  332.7 1.5 convert_element_type.71
  334.2 0.8 copy-done.1
  335.4 20.8 %shard_map.289 = (f32[6,2,256,1024]{3,2,1,0:T(8,128)}, f32[1,2,256,1024]{3,2,1,0:T(8,128)}, f32[4,2,64,64]{3,2,1,0:T(8,128)}, f32[3,2,176,176]{3,2,1,0:T(8,128)}...) custom-call(f32[7,2,256,1024]{3,2,1,0:T(8,128)} %stat_ref.1, f32[7,2,256,1024]{3,2,1,0:T(8,128)} %root_ref.1, ...), custom_call_target="tpu_custom_call" | custom-call | tf_op jit(solution)/shard_map/pallas_call | solution.py:1560
  357.2 0.8 bitcast_subtract_fusion
  358.8 1.0 sub.29
  (51 shorter events, 4.7 us)
Async XLA Ops:
  0.7 6.6 %copy-start.9 = (f32[2,256,352]{1,2,0:T(8,128)S(1)}, f32[2,256,352]{1,2,0:T(8,128)}, u32[]{:S(2)}) copy-start(f32[2,256,352]{1,2,0:T(8,128)} %param.19) | copy-start | bytes 2162692
  319.5 9.4 %copy-start.7 = (bf16[4,128,1024]{2,1,0:T(8,128)(2,1)S(1)}, bf16[4,128,1024]{2,1,0:T(8,128)(2,1)}, u32[]{:S(2)}) copy-start(bf16[4,128,1024]{2,1,0:T(8,128)(2,1)} %x_ref.1) | copy-start | bytes 3145732
  319.5 9.4 %copy-start.15 = (bf16[4,128,1024]{2,1,0:T(8,128)(2,1)S(1)}, bf16[4,128,1024]{2,1,0:T(8,128)(2,1)}, u32[]{:S(2)}) copy-start(bf16[4,128,1024]{2,1,0:T(8,128)(2,1)} %get-tuple-element.59) | copy-start | bytes 3145732
  320.6 10.0 %copy-start.17 = (f32[2,1024]{1,0:T(2,128)}, f32[2,1024]{1,0:T(2,128)S(1)}, u32[]{:S(2)}) copy-start(f32[2,1024]{1,0:T(2,128)S(1)} %get-tuple-element.74) | copy-start | bytes 24580
  328.9 1.7 copy-start.8
  328.9 2.1 copy-start.14
  331.0 1.7 copy-start.13
  331.0 3.2 copy-start.4
  331.0 3.2 copy-start.5
  331.0 3.2 copy-start.6
  332.7 1.5 copy-start
  332.7 2.3 copy-start.1
  332.7 2.6 copy-start.2
  332.7 2.6 copy-start.3
  335.4 20.8 %copy-start.16 = (f32[128,256]{1,0:T(8,128)S(1)}, f32[128,256]{1,0:T(8,128)}, u32[]{:S(2)}) copy-start(f32[128,256]{1,0:T(8,128)} %param.20) | copy-start | bytes 393220
  356.1 1.0 copy-start.11
  356.1 1.8 copy-start.12
  356.8 2.0 copy-start.10
